TPU v7x, 128 devices: a whole 4x4x4 slice. The times are simulated.
128 devices in a mesh: dp: 8 (over x_lo, z), tp: 16 (over x_hi, y, core).
Axes of the slice: x: 4 (x_hi: 2, x_lo: 2; x = x_hi * 2 + x_lo), y: 4, z: 4, core: 2. Of those that a mesh axis runs over, the one named last changes fastest.
Arguments:
- queries: bfloat16 [1024, 8192], P('dp', 'tp'), may hold values from -160 to 160
- keys_cache: bfloat16 [256, 16, 384, 128], P('dp', 'tp'), may hold values from -7 to 7, as said below
- values_cache: bfloat16 [256, 16, 384, 128], P('dp', 'tp'), may hold values from -6 to 6, as said below
- prefix_len: int32 [256], P('dp'), may hold values from 2 to 380, as said below
- accepted: int32 [256], P('dp'), may hold values from 1 to 4
- residual_in: bfloat16 [1024, 8192], P('dp', 'tp'), may hold values from -0.59765625 to 0.59765625
- low_hidden: bfloat16 [1024, 8192], P('dp', 'tp'), may hold values from -6 to 6
- mid_hidden: bfloat16 [1024, 8192], P('dp', 'tp'), may hold values from -6 to 6
- out_weight: bfloat16 [8192, 8192], P('tp'), may hold values from -0.0625 to 0.0625
- merge_weight: bfloat16 [3, 8192, 8192], P(None, 'dp', 'tp'), may hold values from -0.0390625 to 0.0390625
Outputs:
- top_hidden: bfloat16 [1024, 8192], P('dp', 'tp')
- merge_grad: float32 [3, 8192, 8192], P(None, 'dp', 'tp')
Inputs may be any that keep to these rules, and one draw needn't show every extreme that they name: Slots j and i of keys_cache hold the same key head k, and are equal, when j * 8 // 16 = i * 8 // 16 = k. Slots j and i of values_cache hold the same value head k, and are equal, when j * 8 // 16 = i * 8 // 16 = k. `prefix_len`: some row has the largest length.
All inputs are finite; a program needn't handle non-finite values.
Results may differ from a plain program's by a relative error of at most 0.014.
Values may be sent and summed in bfloat16 or wider, within the bound.
No kernel may reach another device: no remote copies, remote signals or barrier semaphores. Data moves between devices by JAX's collectives and lax.ppermute only.
A program may use at most 128 MiB of HBM per device.

v0:
```python
import jax
import jax.numpy as jnp
from jax import lax
from jax.sharding import PartitionSpec as P

STEPS = 4


def attend(queries, keys, values, lens):
    rows = keys.shape[0]
    head_size = keys.shape[-1]
    grouped = queries.reshape(rows, STEPS, -1, head_size)
    scores = jnp.einsum(
        "rshd,rpd->rhsp", grouped, keys, preferred_element_type=jnp.float32
    ) * head_size ** (-0.5)
    limit = lens[:, None] + jnp.arange(STEPS, dtype=jnp.int32)[None, :] + 1
    visible = jnp.arange(keys.shape[1], dtype=jnp.int32)[None, None, :] < limit[:, :, None]
    scores = jnp.where(visible[:, None], scores, -1e30)
    largest = jnp.max(scores, axis=-1, keepdims=True)
    expo = jnp.exp(scores - largest)
    weights = (expo / jnp.sum(expo, axis=-1, keepdims=True)).astype(jnp.bfloat16)
    context = jnp.einsum("rhsp,rpd->rshd", weights, values, preferred_element_type=jnp.float32)
    return context.astype(jnp.bfloat16).reshape(rows * STEPS, -1)


def shifted(features):
    grouped = features.reshape(-1, STEPS, features.shape[-1])
    moved = jnp.concatenate([grouped[:, 1:], jnp.zeros_like(grouped[:, :1])], axis=1)
    return moved.reshape(features.shape)


def contract(source, errors):
    return lax.dot_general(
        source, errors, (((0,), (0,)), ((), ())), preferred_element_type=jnp.float32
    )


def local(
    queries,
    keys_cache,
    values_cache,
    prefix_len,
    accepted,
    residual_in,
    low_hidden,
    mid_hidden,
    out_weight,
    merge_weight,
):
    context = attend(queries, keys_cache[:, 0], values_cache[:, 0], prefix_len)
    projected = jnp.dot(context, out_weight, preferred_element_type=jnp.float32)
    summed = lax.psum_scatter(projected, "tp", scatter_dimension=1, tiled=True)
    top_hidden = (residual_in.astype(jnp.float32) + summed).astype(jnp.bfloat16)
    low_whole, mid_whole, top_whole = (
        lax.all_gather(low_hidden, "tp", axis=1, tiled=True),
        lax.all_gather(mid_hidden, "tp", axis=1, tiled=True),
        lax.all_gather(top_hidden, "tp", axis=1, tiled=True),
    )
    low_moved, mid_moved, top_moved = (
        lax.all_to_all(low_whole, "dp", split_axis=1, concat_axis=0, tiled=True),
        lax.all_to_all(mid_whole, "dp", split_axis=1, concat_axis=0, tiled=True),
        lax.all_to_all(top_whole, "dp", split_axis=1, concat_axis=0, tiled=True),
    )
    merged_part = jnp.dot(low_moved, merge_weight[0], preferred_element_type=jnp.float32)
    merged_part = merged_part + jnp.dot(
        mid_moved, merge_weight[1], preferred_element_type=jnp.float32
    )
    merged_part = merged_part + jnp.dot(
        top_moved, merge_weight[2], preferred_element_type=jnp.float32
    )
    scale = low_moved.shape[0] ** (-0.5)
    keep_local = (
        (jnp.arange(STEPS, dtype=jnp.int32)[None, :] + 1 < accepted[:, None])
        .astype(jnp.float32)
        .reshape(-1)
    )
    merged = lax.psum(merged_part, "dp")
    top_all, keep_all = (
        lax.all_gather(top_hidden, "dp", axis=0, tiled=True),
        lax.all_gather(keep_local.astype(jnp.bfloat16), "dp", axis=0, tiled=True),
    )
    errors = (
        keep_all.astype(jnp.float32)[:, None]
        * (merged - shifted(top_all).astype(jnp.float32))
        * scale
    ).astype(jnp.bfloat16)
    merge_grad = jnp.stack(
        [contract(low_moved, errors), contract(mid_moved, errors), contract(top_moved, errors)],
        axis=0,
    )
    return (top_hidden, merge_grad)


def solution(mesh):
    in_specs = (
        P("dp", "tp"),
        P("dp", "tp", None, None),
        P("dp", "tp", None, None),
        P("dp"),
        P("dp"),
        P("dp", "tp"),
        P("dp", "tp"),
        P("dp", "tp"),
        P("tp", None),
        P(None, "dp", "tp"),
    )
    out_specs = (P("dp", "tp"), P(None, "dp", "tp"))
    return jax.shard_map(local, mesh=mesh, in_specs=in_specs, out_specs=out_specs, check_vma=False)
```

profile of v0, /device:TPU:0, one launch (start us, length us, event | category | flops | bytes accessed | tf_op | source)
XLA Modules:
  0.0 417.6 jit_solution(6566466031145826714)
XLA Ops:
  9.2 2.2 fusion.34
  12.7 2.6 fusion.19
  15.4 6.7 %fusion.31 = f32[128,8192]{1,0:T(8,128)} fusion(bf16[512,8192]{1,0:T(8,128)(2,1)} %param.18, bf16[16,8,4,128]{3,2,1,0:T(4,128)(2,1)S(1)} %bitcast.92), kind=kOutput, calls=%fused_computation.32 | convolution fusion | flops 1073741824 | bytes 12713984 | tf_op jit(solution)/shard_map/dot_general | solution.py:51
  24.6 80.5 %reduce-scatter.2.cloned.1.call-done = f32[128,512]{1,0:T(8,128)} async-done(((f32[128,8192]{1,0:T(8,128)}), f32[128,512]{1,0:T(8,128)}) %reduce-scatter.2.cloned.1.call-update) | async-done | bytes 262160 | tf_op jit(solution)/shard_map/reduce_scatter | solution.py:52
  106.8 47.4 %all-gather.8.cloned.1.call-done = bf16[128,8192]{0,1:T(8,128)(2,1)} async-done(((bf16[128,512]{0,1:T(8,128)(2,1)}), bf16[128,8192]{0,1:T(8,128)(2,1)}) %all-gather.8.cloned.1.call-update) | async-done | bytes 2097168 | tf_op jit(solution)/shard_map/all_gather | solution.py:56
  154.2 4.4 %all-to-all-start.1 = ((bf16[128,8,1024]{0,2,1:T(8,128)(2,1)}), bf16[128,8,1024]{0,2,1:T(8,128)(2,1)S(1)}, u32[]{:S(2)}, u32[]{:S(2)}) async-start(bf16[128,8,1024]{0,2,1:T(8,128)(2,1)} %bitcast.90), calls=%async_computation.2 | async-start | bytes 4194304 | tf_op jit(solution)/shard_map/all_to_all | solution.py:61
  158.7 46.1 %all-gather.6.cloned.1.call-done = bf16[128,8192]{0,1:T(8,128)(2,1)} async-done(((bf16[128,512]{0,1:T(8,128)(2,1)}), bf16[128,8192]{0,1:T(8,128)(2,1)}) %all-gather.6.cloned.1.call-update) | async-done | bytes 2097168 | tf_op jit(solution)/shard_map/all_gather | solution.py:55
  206.1 4.4 %all-to-all-start = ((bf16[128,8,1024]{0,2,1:T(8,128)(2,1)}), bf16[128,8,1024]{0,2,1:T(8,128)(2,1)}, u32[]{:S(2)}, u32[]{:S(2)}) async-start(bf16[128,8,1024]{0,2,1:T(8,128)(2,1)} %bitcast.89), calls=%async_computation.1 | async-start | bytes 4194304 | tf_op jit(solution)/shard_map/all_to_all | solution.py:60
  210.6 44.5 %all-gather.10.cloned.1.call-done = bf16[128,8192]{1,0:T(8,128)(2,1)} async-done(((bf16[128,512]{1,0:T(8,128)(2,1)}), bf16[128,8192]{1,0:T(8,128)(2,1)}) %all-gather.10.cloned.1.call-update) | async-done | bytes 2097168 | tf_op jit(solution)/shard_map/all_gather | solution.py:57
  255.1 3.1 copy.50
  258.2 4.4 %all-to-all-start.2 = ((bf16[128,8,1024]{2,0,1:T(8,128)(2,1)}), bf16[128,8,1024]{2,0,1:T(8,128)(2,1)S(1)}, u32[]{:S(2)}, u32[]{:S(2)}) async-start(bf16[128,8,1024]{2,0,1:T(8,128)(2,1)} %bitcast.88), calls=%async_computation.3 | async-start | bytes 4194304 | tf_op jit(solution)/shard_map/all_to_all | solution.py:62
  263.3 3.9 copy.34
  267.2 3.9 copy.32
  271.1 4.6 %fusion.23 = f32[1024,512]{1,0:T(8,128)} fusion(bf16[1024,1024]{1,0:T(8,128)(2,1)} %bitcast.83, bf16[3,1024,512]{2,1,0:T(8,128)(2,1)} %param.19), kind=kOutput, calls=%fused_computation.20 | convolution fusion | flops 1073741824 | bytes 5242880 | tf_op jit(solution)/shard_map/dot_general | solution.py:65
  275.7 3.8 fusion.25
  279.6 13.3 %all-to-all-done.2 = bf16[128,8,1024]{2,0,1:T(8,128)(2,1)S(1)} async-done(((bf16[128,8,1024]{2,0,1:T(8,128)(2,1)}), bf16[128,8,1024]{2,0,1:T(8,128)(2,1)S(1)}, u32[]{:S(2)}, u32[]{:S(2)}) %all-to-all-start.2) | async-done | bytes 2097184 | tf_op jit(solution)/shard_map/all_to_all | solution.py:62
  292.9 5.1 %add_add_fusion = f32[1024,512]{1,0:T(8,128)} fusion(f32[1024,512]{1,0:T(8,128)} %fusion.25, f32[1024,512]{1,0:T(8,128)} %fusion.23, bf16[1024,1024]{1,0:T(8,128)(2,1)S(1)} %bitcast.81, bf16[3,1024,512]{2,1,0:T(8,128)(2,1)} %param.19), kind=kOutput, calls=%fused_computation.8 | convolution fusion | flops 1074790400 | bytes 9437184 | tf_op jit(solution)/shard_map/dot_general | solution.py:68
  298.9 17.9 %all-gather = bf16[8,1,128]{2,1,0:T(2,128)(2,1)S(1)} all-gather(bf16[1,1,128]{2,1,0:T(2,128)(2,1)S(1)} %reshape.69), channel_id=1, replica_groups=mesh['dp'=8,'tp'=16] {'dp'}, dimensions={0}, use_global_device_ids=true | all-gather | bytes 2304 | tf_op jit(solution)/shard_map/all_gather | solution.py:80
  316.8 2.1 reshape.67
  322.6 3.0 reshape.68
  325.6 68.2 %all-reduce.3.cloned.1.call-done = f32[1024,512]{1,0:T(8,128)} async-done(((f32[1024,512]{1,0:T(8,128)}), f32[1024,512]{1,0:T(8,128)}) %all-reduce.3.cloned.1.call-update) | async-done | bytes 2097168 | tf_op jit(solution)/shard_map/psum | solution.py:77
  393.8 2.6 multiply_convert_fusion
  400.8 3.2 pad_maximum_fusion
  404.0 6.7 %copy.37 = f32[3,1024,512]{2,1,0:T(8,128)} copy(f32[3,1024,512]{1,2,0:T(8,128)} %pad_maximum_fusion) | data formatting | bytes 12582912
  (52 shorter events, 18.4 us)
Async XLA Ops:
  7.2 2.0 copy-start
  7.2 98.0 %reduce-scatter.2.cloned.1.call-start = ((), (), s32[]{:S(2)}) async-start(), calls=%async_computation.4 | async-start | bytes 4456448 | tf_op jit(solution)/shard_map/reduce_scatter | solution.py:52
  22.1 0.9 copy-start.6
  22.1 1.7 copy-start.7
  22.1 83.1 %copy-start.8 = (bf16[128,512]{1,0:T(8,128)(2,1)S(1)}, bf16[128,512]{1,0:T(8,128)(2,1)}, u32[]{:S(2)}) copy-start(bf16[128,512]{1,0:T(8,128)(2,1)} %param.15) | copy-start | bytes 393220
  22.1 132.2 %all-gather.8.cloned.1.call-start = ((), (), s32[]{:S(2)}) async-start(), calls=%async_computation.6 | async-start | bytes 2228224 | tf_op jit(solution)/shard_map/all_gather | solution.py:56
  23.7 181.1 %all-gather.6.cloned.1.call-start = ((), (), s32[]{:S(2)}) async-start(), calls=%async_computation.5 | async-start | bytes 2228224 | tf_op jit(solution)/shard_map/all_gather | solution.py:55
  24.6 230.5 %all-gather.10.cloned.1.call-start = ((), (), s32[]{:S(2)}) async-start(), calls=%async_computation.7 | async-start | bytes 2228224 | tf_op jit(solution)/shard_map/all_gather | solution.py:57
  154.2 50.6 %all-to-all-start.1 = ((bf16[128,8,1024]{0,2,1:T(8,128)(2,1)}), bf16[128,8,1024]{0,2,1:T(8,128)(2,1)S(1)}, u32[]{:S(2)}, u32[]{:S(2)}) async-start(bf16[128,8,1024]{0,2,1:T(8,128)(2,1)} %bitcast.90), calls=%async_computation.2 | async-start | bytes 4194304 | tf_op jit(solution)/shard_map/all_to_all | solution.py:61
  204.8 1.3 copy-start.5
  206.1 52.1 %all-to-all-start = ((bf16[128,8,1024]{0,2,1:T(8,128)(2,1)}), bf16[128,8,1024]{0,2,1:T(8,128)(2,1)}, u32[]{:S(2)}, u32[]{:S(2)}) async-start(bf16[128,8,1024]{0,2,1:T(8,128)(2,1)} %bitcast.89), calls=%async_computation.1 | async-start | bytes 4194304 | tf_op jit(solution)/shard_map/all_to_all | solution.py:60
  258.2 34.7 %all-to-all-start.2 = ((bf16[128,8,1024]{2,0,1:T(8,128)(2,1)}), bf16[128,8,1024]{2,0,1:T(8,128)(2,1)S(1)}, u32[]{:S(2)}, u32[]{:S(2)}) async-start(bf16[128,8,1024]{2,0,1:T(8,128)(2,1)} %bitcast.88), calls=%async_computation.3 | async-start | bytes 4194304 | tf_op jit(solution)/shard_map/all_to_all | solution.py:62
  262.6 54.1 %all-gather.12.cloned.1.call-start = ((), (), s32[]{:S(2)}) async-start(), calls=%async_computation.9 | async-start | bytes 1179648 | tf_op jit(solution)/shard_map/all_gather | solution.py:79
  263.2 130.5 %all-reduce.3.cloned.1.call-start = ((), (), s32[]{:S(2)}) async-start(), calls=%async_computation.8 | async-start | bytes 4194304 | tf_op jit(solution)/shard_map/psum | solution.py:77
  271.1 4.6 %copy-start.3 = (bf16[8,128,1024]{2,1,0:T(8,128)(2,1)S(1)}, bf16[8,128,1024]{2,1,0:T(8,128)(2,1)}, u32[]{:S(2)}) copy-start(bf16[8,128,1024]{2,1,0:T(8,128)(2,1)} %copy.32) | copy-start | bytes 6291460
  298.0 0.7 copy-start.9
  396.3 1.6 copy-start.4
  397.9 1.6 copy-start.2
  404.0 6.7 %copy-start.1 = (bf16[32,1,384,128]{3,2,1,0:T(8,128)(2,1)S(1)}, bf16[32,1,384,128]{3,2,1,0:T(8,128)(2,1)}, u32[]{:S(2)}) copy-start(bf16[32,1,384,128]{3,2,1,0:T(8,128)(2,1)} %param.11) | copy-start | bytes 9437188
Sparse Core Ops, SparseCore 0:
  22.2 82.8 reduce-scatter.1
  107.9 46.2 all-gather.7
  157.0 47.7 all-gather.5
  207.8 47.2 all-gather.9
  265.5 44.4 all-gather.11
  313.0 80.6 all-reduce.2
where the time goes:
time: 418 us
  waiting for transfers between devices  301 us (72%)
  local copies, waits for them, and re-layouts  30.8 us (7%)
  matrix products  28.9 us (7%)
  blocking collectives  17.9 us (4%)
  between operations  14.2 us (3%)
  starting transfers between devices  13.5 us (3%)
  other arithmetic  11.6 us (3%)
    reduce_scatter x1, waiting for transfers between devices, local(): summed = lax.psum_scatter(projected, 'tp', scatter_dimension=1, tiled=True)  80.5 us
    psum x1, waiting for transfers between devices, local(): merged = lax.psum(merged_part, 'dp')  68.2 us
    all_gather x1, waiting for transfers between devices, local(): lax.all_gather(mid_hidden, 'tp', axis=1, tiled=True)  47.4 us
    all_gather x1, waiting for transfers between devices, local(): lax.all_gather(low_hidden, 'tp', axis=1, tiled=True)  46.1 us
    all_gather x1, waiting for transfers between devices, local(): lax.all_gather(top_hidden, 'tp', axis=1, tiled=True)  44.5 us
    all_gather x1, blocking collectives, local(): lax.all_gather(keep_local.astype(jnp.bfloat16), 'dp', axis=0, tiled=True)  17.9 us
    all_to_all x1, waiting for transfers between devices, local(): lax.all_to_all(top_whole, 'dp', split_axis=1, concat_axis=0, tiled=True)  13.3 us
    unnamed x24, local copies, waits for them, and re-layouts  11.7 us
  transfers between devices with their start and end apart: 9, of which 6 were waited for; matrix products, arithmetic and copies ran while one was open for 9% of the time, Pallas kernels for 0%

commit v1 on v0

v1 whole, which is shorter than its diff:
```python
import jax
import jax.numpy as jnp
from jax import lax
from jax.sharding import PartitionSpec as P

STEPS = 4
CHIPS = 8


def dev(xl, z, xh, y, c):
    return (xl * 4 + z) * 16 + xh * 8 + y * 2 + c


def coords():
    return [
        (xl, z, xh, y, c)
        for xl in range(2)
        for z in range(4)
        for xh in range(2)
        for y in range(4)
        for c in range(2)
    ]


TO_READER = [(dev(*p), dev(p[2], p[3], p[0], (p[3] - p[1]) % 4, p[4])) for p in coords()]
READERS = [
    [dev(xl, z, xh, (z - k) % 4, c) for xh in range(2) for k in range(4)]
    for xl in range(2)
    for z in range(4)
    for c in range(2)
]
READERS_BOTH = [
    [dev(xl, z, xh, (z - k) % 4, c) for c in range(2) for xh in range(2) for k in range(4)]
    for xl in range(2)
    for z in range(4)
]
SAME_CORE = [[2 * t + c for t in range(CHIPS)] for c in range(2)]
OTHER_CORE = [(j, j ^ 1) for j in range(16)]
BOTH = ("dp", "tp")


def attend(queries, keys, values, lens):
    rows = keys.shape[0]
    head_size = keys.shape[-1]
    grouped = queries.reshape(rows, STEPS, -1, head_size)
    scores = jnp.einsum(
        "rshd,rpd->rhsp", grouped, keys, preferred_element_type=jnp.float32
    ) * head_size ** (-0.5)
    limit = lens[:, None] + jnp.arange(STEPS, dtype=jnp.int32)[None, :] + 1
    visible = jnp.arange(keys.shape[1], dtype=jnp.int32)[None, None, :] < limit[:, :, None]
    scores = jnp.where(visible[:, None], scores, -1e30)
    largest = jnp.max(scores, axis=-1, keepdims=True)
    expo = jnp.exp(scores - largest)
    weights = (expo / jnp.sum(expo, axis=-1, keepdims=True)).astype(jnp.bfloat16)
    context = jnp.einsum("rhsp,rpd->rshd", weights, values, preferred_element_type=jnp.float32)
    return context.astype(jnp.bfloat16).reshape(rows * STEPS, -1)


def dot(a, b):
    return jnp.dot(a, b, preferred_element_type=jnp.float32)


def contract(source, errors):
    return lax.dot_general(
        source, errors, (((0,), (0,)), ((), ())), preferred_element_type=jnp.float32
    )


def spread(block, axis, groups=None):
    copies = jnp.broadcast_to(block[None], (CHIPS, *block.shape))
    return lax.all_to_all(copies, axis, 0, 0, tiled=True, axis_index_groups=groups)


def local(
    queries,
    keys_cache,
    values_cache,
    prefix_len,
    accepted,
    residual_in,
    low_hidden,
    mid_hidden,
    out_weight,
    merge_weight,
):
    tokens, width = residual_in.shape
    core = lax.axis_index("tp") % 2

    both = lax.ppermute(jnp.concatenate([low_hidden, mid_hidden], axis=1), BOTH, TO_READER)
    both = lax.all_gather(both, BOTH, axis=0, tiled=True, axis_index_groups=READERS_BOTH)
    both = both.reshape(2, CHIPS * tokens, 2 * width)
    weight = merge_weight.reshape(3, 2, width, width)
    merged_both = dot(both[0], weight[:2, 0].reshape(2 * width, width)) + dot(
        both[1], weight[:2, 1].reshape(2 * width, width)
    )
    weight_own = lax.dynamic_index_in_dim(weight[2], core, 0, keepdims=False)
    weight_other = lax.dynamic_index_in_dim(weight[2], 1 - core, 0, keepdims=False)

    context = attend(queries, keys_cache[:, 0], values_cache[:, 0], prefix_len)
    projected = dot(context, out_weight).astype(jnp.bfloat16)
    projected = projected.reshape(tokens, CHIPS, 2, width).transpose(2, 1, 0, 3)
    kept = lax.dynamic_index_in_dim(projected, core, 0, keepdims=False)
    given = lax.dynamic_index_in_dim(projected, 1 - core, 0, keepdims=False)
    taken = lax.ppermute(given, "tp", OTHER_CORE)
    pair = (kept.astype(jnp.float32) + taken.astype(jnp.float32)).astype(jnp.bfloat16)
    parts = lax.all_to_all(pair, "tp", 0, 0, tiled=True, axis_index_groups=SAME_CORE)
    summed = jnp.sum(parts.astype(jnp.float32), axis=0)
    top_hidden = (residual_in.astype(jnp.float32) + summed).astype(jnp.bfloat16)

    top_own = spread(lax.ppermute(top_hidden, BOTH, TO_READER), BOTH, READERS)
    top_other = lax.ppermute(top_own, "tp", OTHER_CORE)
    top_own = top_own.reshape(CHIPS * tokens, width)
    top_other = top_other.reshape(CHIPS * tokens, width)

    merged_part = merged_both + dot(top_own, weight_own) + dot(top_other, weight_other)
    merged_part = merged_part.astype(jnp.bfloat16).reshape(CHIPS, tokens, width)
    merged_parts = lax.all_to_all(merged_part, "dp", 0, 0, tiled=True)
    merged = jnp.sum(merged_parts.astype(jnp.float32), axis=0)

    step = lax.broadcasted_iota(jnp.int32, (tokens, 1), 0) % STEPS
    keep = (step + 1 < jnp.repeat(accepted, STEPS)[:, None]).astype(jnp.float32)
    following = jnp.concatenate([top_hidden[1:], jnp.zeros_like(top_hidden[:1])], axis=0)
    following = jnp.where(step < STEPS - 1, following, jnp.zeros_like(following))
    scale = (CHIPS * tokens) ** (-0.5)
    errors = (keep * (merged - following.astype(jnp.float32)) * scale).astype(jnp.bfloat16)
    errors = spread(errors, "dp").reshape(CHIPS * tokens, width)

    grad_both = [contract(both[half], errors).reshape(2, width, width) for half in range(2)]
    grad_own, grad_other = contract(top_own, errors), contract(top_other, errors)
    grad_top = jnp.where(
        core == 0, jnp.stack([grad_own, grad_other]), jnp.stack([grad_other, grad_own])
    )
    grad = jnp.concatenate([jnp.stack(grad_both, axis=1), grad_top[None]], axis=0)
    return (top_hidden, grad.reshape(3, 2 * width, width))


def solution(mesh):
    in_specs = (
        P("dp", "tp"),
        P("dp", "tp", None, None),
        P("dp", "tp", None, None),
        P("dp"),
        P("dp"),
        P("dp", "tp"),
        P("dp", "tp"),
        P("dp", "tp"),
        P("tp", None),
        P(None, "dp", "tp"),
    )
    out_specs = (P("dp", "tp"), P(None, "dp", "tp"))
    return jax.shard_map(local, mesh=mesh, in_specs=in_specs, out_specs=out_specs, check_vma=False)
```

time: 418 us -> 193 us (0.46)
  waiting for transfers between devices: 301 us -> 22.5 us
  blocking collectives: 17.9 us -> 78.7 us
    all_gather x4 -> x1, waiting for transfers between devices: 138 us -> 0.02 us  [local(): lax.all_gather(both, BOTH, axis=0, tiled=True, axis_index_groups=READERS_...]
    reduce_scatter x1 -> x0, waiting for transfers between devices: 80.5 us -> none  [local(): summed = lax.psum_scatter(projected, 'tp', scatter_dimension=1, tiled=True)]
    all_to_all x0 -> x2, blocking collectives: none -> 78.7 us  [the longest x1 41.9 us: local(): lax.all_to_all(pair, 'tp', 0, 0, tiled=True, axis_index_groups=SAME_CORE)]
    psum x1 -> x0, waiting for transfers between devices: 68.2 us -> none  [local(): merged = lax.psum(merged_part, 'dp')]
    all_gather x1 -> x0, blocking collectives: 17.9 us -> none  [local(): lax.all_gather(keep_local.astype(jnp.bfloat16), 'dp', axis=0, tiled=True)]
    dot_general x0 -> x3, local copies, waits for them, and re-layouts: none -> 10.5 us  [contract(): lax.dot_general(source, errors, (((0,), (0,)), ((), ())), preferred_eleme...]
    unnamed x24 -> x23, local copies, waits for them, and re-layouts: 11.7 us -> 2.02 us
    all_to_all x3 -> x1, local copies, waits for them, and re-layouts: 11 us -> 1.48 us  [spread(): lax.all_to_all(copies, axis, 0, 0, tiled=True, axis_index_groups=groups)]
  transfers between devices with their start and end apart: 9 -> 7, of which waited for: 6 -> 3; matrix products, arithmetic and copies ran while one was open for 9% -> 22% of each run, Pallas kernels for 0% -> 0%
where the time goes in v1:
time: 193 us; the launch traced here: 192 us
  blocking collectives  78.7 us (41%)
  local copies, waits for them, and re-layouts  29.1 us (15%)
  matrix products  26.8 us (14%)
  waiting for transfers between devices  22.5 us (12%)
  between operations  14.4 us (7%)
  starting transfers between devices  11.2 us (6%)
  other arithmetic  9.26 us (5%)
    all_to_all x1, blocking collectives, local(): lax.all_to_all(pair, 'tp', 0, 0, tiled=True, axis_index_groups=SAME_CORE)  41.9 us
    all_to_all x1, blocking collectives, spread(): lax.all_to_all(copies, axis, 0, 0, tiled=True, axis_index_groups=groups)  36.8 us
    all_to_all x1, waiting for transfers between devices, local(): merged_parts = lax.all_to_all(merged_part, 'dp', 0, 0, tiled=True)  15.2 us
    dot_general x5, matrix products, dot(): return jnp.dot(a, b, preferred_element_type=jnp.float32)  14 us
    dot_general x3, local copies, waits for them, and re-layouts, contract(): lax.dot_general(source, errors, (((0,), (0,)), ((), ())), preferred_eleme...  10.5 us
    dot_general x4, matrix products, contract(): lax.dot_general(source, errors, (((0,), (0,)), ((), ())), preferred_eleme...  8.07 us
    all_to_all x1, starting transfers between devices, local(): merged_parts = lax.all_to_all(merged_part, 'dp', 0, 0, tiled=True)  5.91 us
    dynamic_slice x1, local copies, waits for them, and re-layouts, local(): kept = lax.dynamic_index_in_dim(projected, core, 0, keepdims=False)  4.85 us
  transfers between devices with their start and end apart: 7, of which 3 were waited for; matrix products, arithmetic and copies ran while one was open for 22% of the time, Pallas kernels for 0%

profile of v1, /device:TPU:0, one launch (start us, length us, event | category | flops | bytes accessed | tf_op | source)
XLA Modules:
  0.0 191.9 jit_solution(10730599527717363802)
XLA Ops:
  11.6 2.2 %fusion.38 = (f32[32,4,4]{1,2,0:T(4,128)S(1)}, f32[32,4,4,384]{3,1,2,0:T(4,128)}) fusion(bf16[32,4,4,128]{3,2,1,0:T(4,128)(2,1)S(1)} %reshape.137, bf16[32,1,384,128]{3,2,1,0:T(8,128)(2,1)S(1)} %copy-done, pred[32,4,384]{2,1,0:T(4,128)(4,1)S(1)} %iota_compare_fusion), kind=kOutput, calls=%fused_computation.54 | convolution fusion | flops 51118464 | bytes 4114432 | tf_op jit(solution)/shard_map/sub | solution.py:53
  15.2 2.6 %fusion.24 = bf16[32,4,4,128]{3,1,2,0:T(4,128)(2,1)S(1)} fusion(bf16[32,1,384,128]{3,2,1,0:T(8,128)(2,1)} %param.12, bf16[32,4,4,384]{3,1,2,0:T(4,128)(2,1)S(1)} %divide_convert_fusion), kind=kOutput, calls=%fused_computation.30 | convolution fusion | flops 50397184 | bytes 3670016 | tf_op jit(solution)/shard_map/rhsp,rpd->rshd/dot_general | solution.py:55
  17.8 6.0 %convolution_convert_fusion = bf16[128,8192]{1,0:T(8,128)(2,1)} fusion(bf16[512,8192]{1,0:T(8,128)(2,1)} %param.18, bf16[16,8,4,128]{3,2,1,0:T(4,128)(2,1)S(1)} %bitcast.112), kind=kOutput, calls=%fused_computation.1 | convolution fusion | flops 1074790400 | bytes 10616832 | tf_op jit(solution)/shard_map/dot_general | solution.py:60
  23.8 3.3 %reshape.139 = bf16[128,8,2,512]{3,2,1,0:T(2,128)(2,1)S(1)} reshape(bf16[128,8192]{1,0:T(8,128)(2,1)} %convolution_convert_fusion) | data formatting | bytes 4194304 | tf_op jit(solution)/shard_map/reshape | solution.py:101
  27.1 4.9 %constant_dynamic-slice_fusion.1 = (bf16[128,8,1,512]{3,2,1,0:T(2,128)(2,1)S(1)}, bf16[128,8,1,512]{3,2,1,0:T(2,128)(2,1)S(1)}) fusion(bf16[128,8,2,512]{3,2,1,0:T(2,128)(2,1)S(1)} %reshape.139, s32[]{:T(128)S(6)} %select_n.62, s32[]{:T(128)S(6)} %select_n.63), kind=kLoop, calls=%fused_computation.51 | loop fusion | bytes 4194312 | tf_op jit(solution)/shard_map/jit(dynamic_index_in_dim)/dynamic_slice | solution.py:102
  33.2 2.6 %collective-permute-done = bf16[8,128,512]{2,1,0:T(8,128)(2,1)S(1)} collective-permute-done((bf16[8,128,512]{2,1,0:T(8,128)(2,1)S(1)}, bf16[8,128,512]{2,1,0:T(8,128)(2,1)S(1)}, u32[]{:S(2)}, u32[]{:S(2)}) %collective-permute-start) | collective-permute-done | bytes 1048608 | tf_op jit(solution)/shard_map/ppermute | solution.py:104
  37.2 41.9 %all_to_all.20 = bf16[8,128,512]{2,1,0:T(8,128)(2,1)S(1)} all-to-all(bf16[8,128,512]{2,1,0:T(8,128)(2,1)S(1)} %fusion.5), channel_id=1, replica_groups={{0,2,4,6,8,10,12,14},{1,3,5,7,9,11,13,15},{16,18,20,22,24,26,28,30},{17..., dimensions={0} | all-to-all | bytes 2097152 | tf_op jit(solution)/shard_map/all_to_all | solution.py:106
  80.4 36.8 %all_to_all.21 = bf16[8,128,512]{1,2,0:T(8,128)(2,1)} all-to-all(bf16[8,128,512]{1,2,0:T(8,128)(2,1)S(1)} %broadcast_in_dim.31), channel_id=1, replica_groups={{0,6,4,2,8,14,12,10},{1,7,5,3,9,15,13,11},{18,16,22,20,26,24,30,28},{19..., dimensions={0} | all-to-all | bytes 2097152 | tf_op jit(solution)/shard_map/all_to_all | solution.py:71
  119.7 1.5 copy.23
  121.2 1.7 fusion.28
  123.0 1.5 copy.24
  124.5 3.2 %fusion.6 = f32[1024,512]{1,0:T(8,128)S(1)} fusion(bf16[1024,512]{1,0:T(8,128)(2,1)} %bitcast.111, bf16[2048,1024]{1,0:T(8,128)(2,1)} %all-gather.2.cloned.1.call-done), kind=kOutput, calls=%fused_computation.15 | convolution fusion | flops 1073741824 | bytes 5242880 | tf_op jit(solution)/shard_map/dot_general | solution.py:60
  129.2 1.8 add_convert_fusion
  130.9 5.9 %all-to-all-start.2 = ((bf16[8,128,512]{2,1,0:T(8,128)(2,1)}), bf16[8,128,512]{2,1,0:T(8,128)(2,1)S(1)}, u32[]{:S(2)}, u32[]{:S(2)}) async-start(bf16[8,128,512]{2,1,0:T(8,128)(2,1)} %bitcast.22), calls=%async_computation.2 | async-start | bytes 2097152 | tf_op jit(solution)/shard_map/all_to_all | solution.py:117
  137.1 15.2 %all-to-all-done.2 = bf16[8,128,512]{2,1,0:T(8,128)(2,1)S(1)} async-done(((bf16[8,128,512]{2,1,0:T(8,128)(2,1)}), bf16[8,128,512]{2,1,0:T(8,128)(2,1)S(1)}, u32[]{:S(2)}, u32[]{:S(2)}) %all-to-all-start.2) | async-done | bytes 1048608 | tf_op jit(solution)/shard_map/all_to_all | solution.py:117
  153.7 3.6 %all-to-all-start.3 = ((bf16[8,128,512]{2,1,0:T(8,128)(2,1)}), bf16[8,128,512]{2,1,0:T(8,128)(2,1)S(1)}, u32[]{:S(2)}, u32[]{:S(2)}) async-start(bf16[8,128,512]{2,1,0:T(8,128)(2,1)} %broadcast_in_dim.53), calls=%async_computation.3 | async-start | bytes 2097152 | tf_op jit(solution)/shard_map/all_to_all | solution.py:71
  157.3 4.0 %slice_bitcast_fusion.1 = (bf16[1024,1024]{0,1:T(8,128)(2,1)S(1)}, bf16[1024,1024]{0,1:T(8,128)(2,1)}) fusion(bf16[2048,1024]{1,0:T(8,128)(2,1)} %all-gather.2.cloned.1.call-done), kind=kLoop, calls=%fused_computation.19 | loop fusion | bytes 8388608 | tf_op jit(solution)/shard_map/dot_general | solution.py:64
  161.3 4.0 %copy.25 = bf16[1024,1024]{1,0:T(8,128)(2,1)} copy(bf16[1024,1024]{0,1:T(8,128)(2,1)} %get-tuple-element.3) | data formatting | bytes 4194304 | tf_op jit(solution)/shard_map/dot_general | solution.py:64
  165.3 2.5 %copy.21 = bf16[1024,1024]{1,0:T(8,128)(2,1)} copy(bf16[1024,1024]{0,1:T(8,128)(2,1)S(1)} %get-tuple-element.2) | data formatting | bytes 4194304 | tf_op jit(solution)/shard_map/dot_general | solution.py:64
  167.8 4.5 %all-to-all-done.3 = bf16[8,128,512]{2,1,0:T(8,128)(2,1)S(1)} async-done(((bf16[8,128,512]{2,1,0:T(8,128)(2,1)}), bf16[8,128,512]{2,1,0:T(8,128)(2,1)S(1)}, u32[]{:S(2)}, u32[]{:S(2)}) %all-to-all-start.3) | async-done | bytes 1048608 | tf_op jit(solution)/shard_map/all_to_all | solution.py:71
  172.3 3.0 %convolution_bitcast_fusion = f32[2,1,512,512]{3,2,0,1:T(8,128)S(1)} fusion(bf16[2,512,1024]{2,1,0:T(8,128)(2,1)} %bitcast.105, bf16[1024,512,1]{1,0,2:T(8,128)(2,1)S(1)} %bitcast.108), kind=kOutput, calls=%fused_computation.20 | convolution fusion | flops 1073741824 | bytes 5242880 | tf_op jit(solution)/shard_map/dot_general | solution.py:64
  177.5 1.9 %convolution_bitcast_fusion.3 = f32[1,1,512,512]{3,2,1,0:T(8,128)S(1)} fusion(bf16[8,128,512]{1,2,0:T(8,128)(2,1)} %all_to_all.21, bf16[8,128,512]{2,1,0:T(8,128)(2,1)S(1)} %all-to-all-done.3), kind=kOutput, calls=%fused_computation.24 | convolution fusion | flops 536870912 | bytes 3145728 | tf_op jit(solution)/shard_map/dot_general | solution.py:64
  179.4 1.9 %convolution_bitcast_fusion.2 = f32[1,1,512,512]{3,2,1,0:T(8,128)S(1)} fusion(bf16[8,128,512]{1,2,0:T(8,128)(2,1)} %collective-permute-done.3, bf16[8,128,512]{2,1,0:T(8,128)(2,1)S(1)} %all-to-all-done.3), kind=kOutput, calls=%fused_computation.23 | convolution fusion | flops 536870912 | bytes 3145728 | tf_op jit(solution)/shard_map/dot_general | solution.py:64
  181.6 3.4 %pad_maximum_fusion = f32[3,1024,512]{2,1,0:T(8,128)} fusion(f32[1,1024,512]{2,1,0:T(8,128)S(1)} %bitcast.99, f32[2,1024,512]{2,1,0:T(8,128)S(1)} %bitcast.98), kind=kLoop, calls=%fused_computation.2 | loop fusion | flops 1572864 | bytes 12582912 | tf_op jit(solution)/shard_map/concatenate | solution.py:133
  (58 shorter events, 17.5 us)
Async XLA Ops:
  7.2 4.5 %copy-start = (bf16[32,1,384,128]{3,2,1,0:T(8,128)(2,1)S(1)}, bf16[32,1,384,128]{3,2,1,0:T(8,128)(2,1)}, u32[]{:S(2)}) copy-start(bf16[32,1,384,128]{3,2,1,0:T(8,128)(2,1)} %param.11) | copy-start | bytes 9437188
  7.2 117.3 %all-gather.2.cloned.1.call-start = ((), (), s32[]{:S(2)}) async-start(), calls=%async_computation.4 | async-start | bytes 4456448 | tf_op jit(solution)/shard_map/all_gather | solution.py:90
  8.4 0.7 collective-permute-start.1
  9.1 0.7 copy-start.8
  33.1 2.7 %collective-permute-start = (bf16[8,128,512]{2,1,0:T(8,128)(2,1)S(1)}, bf16[8,128,512]{2,1,0:T(8,128)(2,1)S(1)}, u32[]{:S(2)}, u32[]{:S(2)}) collective-permute-start(bf16[8,128,512]{2,1,0:T(8,128)(2,1)S(1)} %bitcast.107), channel_id=1, source_target_pairs={{0,1},{1,0},{2,3},{3,2},{4,5},{5,4},{6,7},{7,6},{8,9},{9,8},{10,11... | collective-permute-start | bytes 3145736 | tf_op jit(solution)/shard_map/ppermute | solution.py:104
  37.2 42.1 %copy-start.9 = (bf16[128,512]{1,0:T(8,128)(2,1)S(1)}, bf16[128,512]{1,0:T(8,128)(2,1)}, u32[]{:S(2)}) copy-start(bf16[128,512]{1,0:T(8,128)(2,1)} %param.15) | copy-start | bytes 393220
  79.2 38.0 %copy-start.4 = (bf16[3,1024,512]{2,1,0:T(8,128)(2,1)S(1)}, bf16[3,1024,512]{2,1,0:T(8,128)(2,1)}, u32[]{:S(2)}) copy-start(bf16[3,1024,512]{2,1,0:T(8,128)(2,1)} %param.19) | copy-start | bytes 9437188
  79.3 57.8 %copy-start.7 = (bf16[128,512]{1,0:T(8,128)(2,1)}, bf16[128,512]{1,0:T(8,128)(2,1)S(1)}, u32[]{:S(2)}) copy-start(bf16[128,512]{1,0:T(8,128)(2,1)S(1)} %add_convert_fusion.1) | copy-start | bytes 393220
  79.3 0.8 collective-permute-start.2
  117.2 5.8 %collective-permute-start.3 = (bf16[8,128,512]{1,2,0:T(8,128)(2,1)}, bf16[8,128,512]{1,2,0:T(8,128)(2,1)}, u32[]{:S(2)}, u32[]{:S(2)}) collective-permute-start(bf16[8,128,512]{1,2,0:T(8,128)(2,1)} %all_to_all.21), channel_id=1, source_target_pairs={{0,1},{1,0},{2,3},{3,2},{4,5},{5,4},{6,7},{7,6},{8,9},{9,8},{10,11... | collective-permute-start | bytes 3145736 | tf_op jit(solution)/shard_map/ppermute | solution.py:111
  124.5 3.3 %copy-start.3 = (bf16[2048,1024]{1,0:T(8,128)(2,1)S(1)}, bf16[2048,1024]{1,0:T(8,128)(2,1)}, u32[]{:S(2)}) copy-start(bf16[2048,1024]{1,0:T(8,128)(2,1)} %all-gather.2.cloned.1.call-done) | copy-start | bytes 12582916
  124.5 3.4 %copy-start.6 = (bf16[2,1,512,512]{3,2,1,0:T(8,128)(2,1)S(1)}, bf16[2,1,512,512]{3,2,1,0:T(8,128)(2,1)}, u32[]{:S(2)}) copy-start(bf16[2,1,512,512]{3,2,1,0:T(8,128)(2,1)} %get-tuple-element.5) | copy-start | bytes 3145732
  127.9 1.3 copy-start.2
  130.9 5.9 %copy-start.10 = (s32[32]{0:T(128)S(1)}, s32[32]{0:T(128)}, u32[]{:S(2)}) copy-start(s32[32]{0:T(128)} %param.14) | copy-start | bytes 388
  130.9 21.4 %all-to-all-start.2 = ((bf16[8,128,512]{2,1,0:T(8,128)(2,1)}), bf16[8,128,512]{2,1,0:T(8,128)(2,1)S(1)}, u32[]{:S(2)}, u32[]{:S(2)}) async-start(bf16[8,128,512]{2,1,0:T(8,128)(2,1)} %bitcast.22), calls=%async_computation.2 | async-start | bytes 2097152 | tf_op jit(solution)/shard_map/all_to_all | solution.py:117
  153.7 18.6 %all-to-all-start.3 = ((bf16[8,128,512]{2,1,0:T(8,128)(2,1)}), bf16[8,128,512]{2,1,0:T(8,128)(2,1)S(1)}, u32[]{:S(2)}, u32[]{:S(2)}) async-start(bf16[8,128,512]{2,1,0:T(8,128)(2,1)} %broadcast_in_dim.53), calls=%async_computation.3 | async-start | bytes 2097152 | tf_op jit(solution)/shard_map/all_to_all | solution.py:71
  172.3 3.0 %copy-start.5 = (bf16[1024,1024]{1,0:T(8,128)(2,1)S(1)}, bf16[1024,1024]{1,0:T(8,128)(2,1)}, u32[]{:S(2)}) copy-start(bf16[1024,1024]{1,0:T(8,128)(2,1)} %copy.21) | copy-start | bytes 6291460
  181.6 3.5 %copy-start.1 = (bf16[32,1,384,128]{3,2,1,0:T(8,128)(2,1)S(1)}, bf16[32,1,384,128]{3,2,1,0:T(8,128)(2,1)}, u32[]{:S(2)}) copy-start(bf16[32,1,384,128]{3,2,1,0:T(8,128)(2,1)} %param.11) | copy-start | bytes 9437188
Sparse Core Ops, SparseCore 0:
  9.9 106.3 all-gather.1

commit v2 on v1

v2 whole, which is shorter than its diff:
```python
import functools

import jax
import jax.numpy as jnp
from jax import lax
from jax.experimental import pallas as pl
from jax.experimental.pallas import tpu as pltpu
from jax.sharding import PartitionSpec as P

STEPS = 4
CHIPS = 8
VMEM = 62 * 2**20


def dev(xl, z, xh, y, c):
    return (xl * 4 + z) * 16 + xh * 8 + y * 2 + c


def coords():
    return [
        (xl, z, xh, y, c)
        for xl in range(2)
        for z in range(4)
        for xh in range(2)
        for y in range(4)
        for c in range(2)
    ]


TO_READER = [(dev(*p), dev(p[2], p[3], p[0], (p[3] - p[1]) % 4, p[4])) for p in coords()]
TO_ACROSS = [(dev(*p), dev(p[2], p[3], 1 - p[0], (p[3] - p[1]) % 4, p[4])) for p in coords()]
READERS = [
    [dev(xl, z, xh, (z - k) % 4, c) for xh in range(2) for k in range(4)]
    for xl in range(2)
    for z in range(4)
    for c in range(2)
]
SAME_CORE = [[2 * t + c for t in range(CHIPS)] for c in range(2)]
OTHER_CORE = [(j, j ^ 1) for j in range(16)]
BOTH = ("dp", "tp")
SCALARS = pl.BlockSpec(memory_space=pltpu.SMEM)
HERE = pl.BlockSpec(memory_space=pltpu.VMEM)
THERE = pl.BlockSpec(memory_space=pl.ANY)
FREE = pl.CostEstimate(flops=0, bytes_accessed=0, transcendentals=0)


def from_y(far):
    return [(j, (j & 8) | (j - 2 * far) % 8) for j in range(16)]


def dot(a, b):
    return jnp.dot(a, b, preferred_element_type=jnp.float32)


def spread(block, axis, groups=None):
    copies = jnp.broadcast_to(block[None], (CHIPS, *block.shape))
    return lax.all_to_all(copies, axis, 0, 0, tiled=True, axis_index_groups=groups)


def fetch(pairs, sems):
    copies = [
        pltpu.make_async_copy(source, target, sems.at[i])
        for i, (source, target) in enumerate(pairs)
    ]
    for copy in copies:
        copy.start()
    return copies


def attend_kernel(lens, queries, keys, values, out, held, scores, weights, gathered, sems):
    rows, width = held.shape[1], keys.shape[2]
    heads = queries.shape[1] // width
    size = heads * STEPS
    copies = fetch(
        [
            (source.at[pl.ds(i * rows // 2, rows // 2)], held.at[j, pl.ds(i * rows // 2, rows // 2)])
            for i in range(2)
            for j, source in enumerate((keys, values))
        ],
        sems,
    )
    shape = (size, keys.shape[1])
    position = lax.broadcasted_iota(jnp.int32, shape, 1)
    step = lax.broadcasted_iota(jnp.int32, shape, 0) % STEPS
    scale = width ** (-0.5)
    for h in range(heads):
        asked = queries[:, h * width : (h + 1) * width].astype(jnp.float32)
        for r in range(rows):
            gathered[r, h * STEPS : (h + 1) * STEPS, :] = asked[r * STEPS : (r + 1) * STEPS]
    for i in range(2):
        copies[2 * i].wait()
        for r in range(i * rows // 2, (i + 1) * rows // 2):
            score = lax.dot_general(
                gathered[r].astype(queries.dtype), held[0, r], (((1,), (1,)), ((), ())), preferred_element_type=jnp.float32
            )
            visible = position < lens[r] + step + 1
            scores[r * size : (r + 1) * size, :] = jnp.where(visible, score * scale, -1e30)
        part = slice(i * rows * size // 2, (i + 1) * rows * size // 2)
        score = scores[part, :]
        expo = jnp.exp(score - jnp.max(score, axis=-1, keepdims=True))
        inverse = 1.0 / jnp.sum(expo, axis=-1, keepdims=True)
        weights[part, :] = (expo * inverse).astype(weights.dtype)
        copies[2 * i + 1].wait()
        for r in range(i * rows // 2, (i + 1) * rows // 2):
            gathered[r] = dot(weights[r * size : (r + 1) * size, :], held[1, r])
    for h in range(heads):
        context = [gathered[r, h * STEPS : (h + 1) * STEPS, :] for r in range(rows)]
        out[:, h * width : (h + 1) * width] = jnp.concatenate(context, axis=0).astype(out.dtype)


def attend(queries, keys, values, lens):
    rows, positions, width = keys.shape
    tokens, depth = queries.shape
    size = STEPS * depth // width
    return pl.pallas_call(
        attend_kernel,
        in_specs=[SCALARS, HERE, THERE, THERE],
        out_specs=HERE,
        out_shape=jax.ShapeDtypeStruct(queries.shape, queries.dtype),
        scratch_shapes=[
            pltpu.VMEM((2, rows, positions, width), jnp.bfloat16),
            pltpu.VMEM((rows * size, positions), jnp.float32),
            pltpu.VMEM((rows * size, positions), jnp.bfloat16),
            pltpu.VMEM((rows, size, width), jnp.float32),
            pltpu.SemaphoreType.DMA((4,)),
        ],
        compiler_params=pltpu.CompilerParams(vmem_limit_bytes=VMEM),
        cost_estimate=FREE,
        name="attend",
    )(lens, queries, keys, values)


def pack_kernel(cuts, *refs):
    *sources, out, held, in_sems, out_sem = refs
    for copy in fetch([(s, held.at[cut]) for s, cut in zip(sources, cuts)], in_sems):
        copy.wait()
    for copy in fetch([(held, out)], out_sem):
        copy.wait()


def pack(arrays, axis):
    shape = list(arrays[0].shape)
    size = shape[axis]
    cuts = [(slice(None),) * axis + (slice(i * size, (i + 1) * size),) for i in range(len(arrays))]
    shape[axis] *= len(arrays)
    return pl.pallas_call(
        functools.partial(pack_kernel, cuts),
        in_specs=[THERE] * len(arrays),
        out_specs=THERE,
        out_shape=jax.ShapeDtypeStruct(shape, arrays[0].dtype),
        scratch_shapes=[
            pltpu.VMEM(shape, arrays[0].dtype),
            pltpu.SemaphoreType.DMA((len(arrays),)),
            pltpu.SemaphoreType.DMA((1,)),
        ],
        compiler_params=pltpu.CompilerParams(vmem_limit_bytes=VMEM),
        cost_estimate=FREE,
        name="pack",
    )(*arrays)


def project_kernel(half, context, weight, out, held, sems):
    width = out.shape[-1]
    copies = fetch(
        [
            (weight.at[:, pl.ds((2 * t + half[0]) * width, width)], held.at[t])
            for t in range(CHIPS)
        ],
        sems,
    )
    for t in range(CHIPS):
        copies[t].wait()
        out[t] = dot(context[...], held[t]).astype(out.dtype)


def project(context, weight, half):
    tokens, depth = context.shape
    width = weight.shape[1] // (2 * CHIPS)
    return pl.pallas_call(
        project_kernel,
        in_specs=[SCALARS, HERE, THERE],
        out_specs=HERE,
        out_shape=jax.ShapeDtypeStruct((CHIPS, tokens, width), jnp.bfloat16),
        scratch_shapes=[
            pltpu.VMEM((CHIPS, depth, width), jnp.bfloat16),
            pltpu.SemaphoreType.DMA((CHIPS,)),
        ],
        compiler_params=pltpu.CompilerParams(vmem_limit_bytes=VMEM),
        cost_estimate=FREE,
        name="project",
    )(half, context, weight)


def base_kernel(core, *refs):
    count = len(refs) - 5
    sources, (weight, out, held, held_weight, sems) = refs[:count], refs[count:]
    copies = fetch(
        [(weight.at[k], held_weight.at[k]) for k in range(2)]
        + [(source, held.at[i]) for i, source in enumerate(sources)],
        sems,
    )
    half = core[0]
    width = out.shape[-1]
    rows = sources[0].shape[0]
    copies[0].wait()
    copies[1].wait()
    for i in range(count // 2):
        copies[2 + 2 * i].wait()
        copies[3 + 2 * i].wait()
        total = dot(held[2 * i, :, :width], held_weight[0, half])
        total += dot(held[2 * i, :, width:], held_weight[1, half])
        total += dot(held[2 * i + 1, :, :width], held_weight[0, 1 - half])
        total += dot(held[2 * i + 1, :, width:], held_weight[1, 1 - half])
        out[i * rows : (i + 1) * rows, :] = total.astype(out.dtype)


def base(pieces, weight, core):
    rows, depth = pieces[0].shape
    tokens, width = len(pieces) // 2 * rows, depth // 2
    return pl.pallas_call(
        base_kernel,
        in_specs=[SCALARS] + [THERE] * (len(pieces) + 1),
        out_specs=HERE,
        out_shape=jax.ShapeDtypeStruct((tokens, width), jnp.bfloat16),
        scratch_shapes=[
            pltpu.VMEM((len(pieces), rows, depth), jnp.bfloat16),
            pltpu.VMEM((2, *weight.shape[1:]), jnp.bfloat16),
            pltpu.SemaphoreType.DMA((len(pieces) + 2,)),
        ],
        compiler_params=pltpu.CompilerParams(vmem_limit_bytes=VMEM),
        cost_estimate=FREE,
        name="base",
    )(core, *pieces, weight)


def add_kernel(own, core, places, total, source, weight, out, held, near, held_weight, sems):
    blocks, rows, width = source.shape
    half = core[0] if own else 1 - core[0]
    pairs = [(weight.at[2, half], held_weight)]
    for p in range(0, blocks, 2):
        pairs.append((source.at[p : p + 2], near.at[p : p + 2]))
        pairs += [(total.at[places[i] if own else i], held.at[i]) for i in (p, p + 1)]
    copies = fetch(pairs, sems)
    copies[0].wait()
    for p in range(0, blocks, 2):
        for copy in copies[1 + p // 2 * 3 : 4 + p // 2 * 3]:
            copy.wait()
        added = dot(near[p : p + 2].reshape(2 * rows, width), held_weight[...])
        added = added.reshape(2, rows, width) + held[p : p + 2].astype(jnp.float32)
        out[p : p + 2] = added.astype(out.dtype)


def add_top(own, total, source, weight, core, places):
    blocks, rows, width = total.shape
    return pl.pallas_call(
        functools.partial(add_kernel, own),
        in_specs=[SCALARS] * 2 + [THERE] * 3,
        out_specs=HERE,
        out_shape=jax.ShapeDtypeStruct(total.shape, total.dtype),
        scratch_shapes=[
            pltpu.VMEM(total.shape, total.dtype),
            pltpu.VMEM(source.shape, source.dtype),
            pltpu.VMEM(weight.shape[2:], weight.dtype),
            pltpu.SemaphoreType.DMA((1 + blocks // 2 * 3,)),
        ],
        compiler_params=pltpu.CompilerParams(vmem_limit_bytes=VMEM),
        cost_estimate=FREE,
        name="add_top",
    )(core, places, total, source, weight)


def grad_kernel(core, places, errors, *refs):
    count = len(refs) - 10
    pieces, (top_own, top_other, out, near, ordered, held, tops, made, sems, out_sems) = (
        refs[:count],
        refs[count:],
    )
    blocks, rows, width = errors.shape
    tokens = blocks * rows
    pairs = [(errors, near)]
    pairs += [(pieces[i], held.at[0, i // 2]) for i in range(0, count, 2)]
    first = fetch(pairs, sems)
    rest = [(pieces[i], held.at[1, i // 2]) for i in range(1, count, 2)]
    rest += [(top_own, tops.at[0]), (top_other, tops.at[1])]

    def product(source, target):
        return lax.dot_general(
            source, target, (((0,), (0,)), ((), ())), preferred_element_type=jnp.float32
        )

    first[0].wait()
    for p in range(blocks):
        ordered[p * rows : (p + 1) * rows, :] = near[places[p]]
    for copy in first[1:]:
        copy.wait()
    rest = fetch(rest, sems.at[pl.ds(len(pairs), len(rest))])
    sent = []
    for i in range(6):
        if i == 2:
            for copy in rest[: count // 2]:
                copy.wait()
        if i >= 4:
            rest[count // 2 + i - 4].wait()
        half = 1 - core[0] if i in (2, 3, 5) else core[0]
        for part in range(2):
            step, cut = 2 * i + part, width // 2
            slot = step % made.shape[0]
            if step >= made.shape[0]:
                sent[step - made.shape[0]].wait()
            columns = slice(part * cut, (part + 1) * cut)
            if i < 4:
                columns = slice(i % 2 * width + part * cut, i % 2 * width + (part + 1) * cut)
                source = held[i // 2, :, :, columns].reshape(tokens, cut)
                made[slot] = product(source, ordered[...])
            else:
                made[slot] = product(tops[i - 4, :, columns], near[...].reshape(tokens, width))
            target = out.at[i % 2 if i < 4 else 2, pl.ds(half * width + part * cut, cut)]
            copy = pltpu.make_async_copy(made.at[slot], target, out_sems.at[step])
            copy.start()
            sent.append(copy)
    for copy in sent[-made.shape[0] :]:
        copy.wait()


def grad(errors, pieces, top_own, top_other, core, places):
    blocks, rows, width = errors.shape
    tokens = blocks * rows
    count = len(pieces)
    return pl.pallas_call(
        grad_kernel,
        in_specs=[SCALARS] * 2 + [THERE] * (count + 3),
        out_specs=THERE,
        out_shape=jax.ShapeDtypeStruct((3, 2 * width, width), jnp.float32),
        scratch_shapes=[
            pltpu.VMEM(errors.shape, jnp.bfloat16),
            pltpu.VMEM((tokens, width), jnp.bfloat16),
            pltpu.VMEM((2, count // 2, *pieces[0].shape), jnp.bfloat16),
            pltpu.VMEM((2, tokens, width), jnp.bfloat16),
            pltpu.VMEM((4, width // 2, width), jnp.float32),
            pltpu.SemaphoreType.DMA((count + 3,)),
            pltpu.SemaphoreType.DMA((12,)),
        ],
        compiler_params=pltpu.CompilerParams(vmem_limit_bytes=VMEM),
        cost_estimate=FREE,
        name="grad",
    )(core, places, errors, *pieces, top_own, top_other)


def local(
    queries,
    keys_cache,
    values_cache,
    prefix_len,
    accepted,
    residual_in,
    low_hidden,
    mid_hidden,
    out_weight,
    merge_weight,
):
    tokens, width = residual_in.shape
    me_dp, me_tp = lax.axis_index("dp"), lax.axis_index("tp")
    xl, z = me_dp // 4, me_dp % 4
    xh, y, core = me_tp // 8, me_tp // 2 % 4, me_tp % 2
    me = core.reshape(1)
    index = jnp.arange(CHIPS)
    lies = ((z - y - index) % 4 * 2 + (xh ^ (index // 4))).astype(jnp.int32)
    held = ((xh ^ (index % 2)) * 4 + (z - y - index // 2) % 4).astype(jnp.int32)
    weight = merge_weight.reshape(3, 2, width, width)

    both = pack([low_hidden, mid_hidden], 1)
    both = [lax.ppermute(both, BOTH, way) for way in (TO_READER, TO_ACROSS)]
    context = attend(queries, keys_cache[:, 0], values_cache[:, 0], prefix_len)
    taken = project(context, out_weight, 1 - me)
    taken, *both = lax.optimization_barrier((taken, *both))
    both = pack(both, 0)
    both = [both] + [lax.ppermute(both, "tp", from_y(far)) for far in (1, 2, 3)]
    taken = lax.ppermute(taken, "tp", OTHER_CORE)
    kept = project(context, out_weight, me)
    pair = (kept.astype(jnp.float32) + taken.astype(jnp.float32)).astype(jnp.bfloat16)
    pair, *both = lax.optimization_barrier((pair, *both))
    parts = lax.all_to_all(pair, "tp", 0, 0, tiled=True, axis_index_groups=SAME_CORE)
    summed = jnp.sum(parts.astype(jnp.float32), axis=0)
    top_hidden = (residual_in.astype(jnp.float32) + summed).astype(jnp.bfloat16)

    pieces = []
    for piece in both:
        pieces += [piece, lax.ppermute(piece, "tp", OTHER_CORE)]
    total = base(pieces, weight, me).reshape(CHIPS, tokens, width)
    top_hidden, total = lax.optimization_barrier((top_hidden, total))

    top_own = spread(lax.ppermute(top_hidden, BOTH, TO_READER), BOTH, READERS)
    top_other = lax.ppermute(top_own, "tp", OTHER_CORE)
    total = add_top(True, total, top_own, weight, me, lies)
    total = add_top(False, total, top_other, weight, me, lies)
    merged_parts = lax.all_to_all(total, "dp", 0, 0, tiled=True)
    merged = jnp.sum(merged_parts.astype(jnp.float32), axis=0)

    step = lax.broadcasted_iota(jnp.int32, (tokens, 1), 0) % STEPS
    keep = (step + 1 < jnp.repeat(accepted, STEPS)[:, None]).astype(jnp.float32)
    following = jnp.concatenate([top_hidden[1:], jnp.zeros_like(top_hidden[:1])], axis=0)
    following = jnp.where(step < STEPS - 1, following, jnp.zeros_like(following))
    scale = (CHIPS * tokens) ** (-0.5)
    errors = (keep * (merged - following.astype(jnp.float32)) * scale).astype(jnp.bfloat16)
    errors = spread(errors, "dp")

    tops = [part.reshape(CHIPS * tokens, width) for part in (top_own, top_other)]
    merge_grad = grad(errors, pieces, *tops, me, held)
    return (top_hidden, merge_grad)


def solution(mesh):
    in_specs = (
        P("dp", "tp"),
        P("dp", "tp", None, None),
        P("dp", "tp", None, None),
        P("dp"),
        P("dp"),
        P("dp", "tp"),
        P("dp", "tp"),
        P("dp", "tp"),
        P("tp", None),
        P(None, "dp", "tp"),
    )
    out_specs = (P("dp", "tp"), P(None, "dp", "tp"))
    return jax.shard_map(local, mesh=mesh, in_specs=in_specs, out_specs=out_specs, check_vma=False)
```

time: 193 us -> 167 us (0.87)
  blocking collectives: 78.7 us -> 31.8 us
  Pallas kernels: 0 us -> 42 us
  matrix products: 26.8 us -> 0 us
  waiting for transfers between devices: 22.5 us -> 48.6 us
  local copies, waits for them, and re-layouts: 29.1 us -> 6.03 us
  starting transfers between devices: 11.2 us -> 32 us
  between operations: 14.4 us -> 1.07 us
  other arithmetic: 9.26 us -> 4.48 us
    pallas_call x0 -> x9, Pallas kernels: none -> 42 us  [the longest x2 9.73 us: project(): pl.pallas_call(project_kernel, in_specs=[SCALARS, HERE, THERE], out_specs...]
    all_to_all x1 -> x0, blocking collectives: 41.9 us -> none  [local(): lax.all_to_all(pair, 'tp', 0, 0, tiled=True, axis_index_groups=SAME_CORE)]
    dot_general x10 -> x0, matrix products: 24.6 us -> none  [the longest x5 14 us: dot(): return jnp.dot(a, b, preferred_element_type=jnp.float32)]
    ppermute x2 -> x10, starting transfers between devices: 0.76 us -> 16.9 us  [the longest x3 10.9 us: local(): both = [both] + [lax.ppermute(both, 'tp', from_y(far)) for far in (1, 2, 3)]]
    ppermute x2 -> x10, waiting for transfers between devices: 2.65 us -> 16.3 us  [the longest x3 13 us: local(): both = [both] + [lax.ppermute(both, 'tp', from_y(far)) for far in (1, 2, 3)]]
    dot_general x3 -> x0, local copies, waits for them, and re-layouts: 10.5 us -> none  [contract(): lax.dot_general(source, errors, (((0,), (0,)), ((), ())), preferred_eleme...]
    all_to_all x1, waiting for transfers between devices: 4.54 us -> 14.3 us  [spread(): lax.all_to_all(copies, axis, 0, 0, tiled=True, axis_index_groups=groups)]
    all_to_all x1, blocking collectives: 36.8 us -> 31.8 us  [spread(): lax.all_to_all(copies, axis, 0, 0, tiled=True, axis_index_groups=groups)]
  transfers between devices with their start and end apart: 7 -> 15, of which waited for: 3 -> 8; matrix products, arithmetic and copies ran while one was open for 22% -> 3% of each run, Pallas kernels for 0% -> 16%
where the time goes in v2:
time: 167 us; the launch traced here: 166 us
  waiting for transfers between devices  48.6 us (29%)
  Pallas kernels  42 us (25%)
  starting transfers between devices  32 us (19%)
  blocking collectives  31.8 us (19%)
  local copies, waits for them, and re-layouts  6.03 us (4%)
  other arithmetic  4.48 us (3%)
    all_to_all x1, blocking collectives, spread(): lax.all_to_all(copies, axis, 0, 0, tiled=True, axis_index_groups=groups)  31.8 us
    all_to_all x1, waiting for transfers between devices, local(): merged_parts = lax.all_to_all(total, 'dp', 0, 0, tiled=True)  15 us
    all_to_all x1, waiting for transfers between devices, spread(): lax.all_to_all(copies, axis, 0, 0, tiled=True, axis_index_groups=groups)  14.3 us
    ppermute x3, waiting for transfers between devices, local(): both = [both] + [lax.ppermute(both, 'tp', from_y(far)) for far in (1, 2, 3)]  13 us
    ppermute x3, starting transfers between devices, local(): both = [both] + [lax.ppermute(both, 'tp', from_y(far)) for far in (1, 2, 3)]  10.9 us
    pallas_call x2, Pallas kernels, project(): pl.pallas_call(project_kernel, in_specs=[SCALARS, HERE, THERE], out_specs...  9.73 us
    pallas_call x1, Pallas kernels, grad(): pl.pallas_call(grad_kernel, in_specs=[SCALARS] * 2 + [THERE] * (count + 3...  9.08 us
    pallas_call x2, Pallas kernels, add_top(): pl.pallas_call(functools.partial(add_kernel, own), in_specs=[SCALARS] * 2...  8.32 us
  transfers between devices with their start and end apart: 15, of which 8 were waited for; matrix products, arithmetic and copies ran while one was open for 3% of the time, Pallas kernels for 16%

profile of v2, /device:TPU:0, one launch (start us, length us, event | category | flops | bytes accessed | tf_op | source)
XLA Modules:
  0.0 165.9 jit_solution(13385676102153147472)
XLA Ops:
  0.6 1.7 %pack.2 = bf16[128,1024]{1,0:T(8,128)(2,1)} custom-call(bf16[128,512]{1,0:T(8,128)(2,1)} %refs_0_.1, bf16[128,512]{1,0:T(8,128)(2,1)} %refs_1_.1), custom_call_target="tpu_custom_call" | custom-call | tf_op jit(solution)/shard_map/pack/pallas_call | solution.py:146
  2.3 3.2 %collective-permute-start.1 = (bf16[128,1024]{1,0:T(8,128)(2,1)}, bf16[128,1024]{1,0:T(8,128)(2,1)S(1)}, u32[]{:S(2)}, u32[]{:S(2)}) collective-permute-start(bf16[128,1024]{1,0:T(8,128)(2,1)} %pack.2), channel_id=1, source_target_pairs={{0,8},{1,9},{2,26},{3,27},{4,44},{5,45},{6,62},{7,63},{8,72},{9,73... | collective-permute-start | bytes 786440 | tf_op jit(solution)/shard_map/ppermute | solution.py:372
  5.5 1.6 collective-permute-start
  7.1 5.5 %attend.1.context = bf16[128,512]{1,0:T(8,128)(2,1)} custom-call(s32[32]{0:T(128)} %lens.1, bf16[128,512]{1,0:T(8,128)(2,1)} %queries.1, bf16[32,384,128]{2,1,0:T(8,128)(2,1)} %bitcast.12, bf16[32,384,128]{2,1,0:T(8,128)(2,1)} %bitcast.13), custom_call_target="tpu_custom_call" | custom-call | tf_op jit(solution)/shard_map/attend/pallas_call | solution.py:115
  12.6 4.9 %project.3 = bf16[8,128,512]{2,1,0:T(8,128)(2,1)} custom-call(s32[1]{0:T(128)S(6)} %sub.34.half, bf16[128,512]{1,0:T(8,128)(2,1)} %attend.1.context, bf16[512,8192]{1,0:T(8,128)(2,1)} %weight.3), custom_call_target="tpu_custom_call" | custom-call | tf_op jit(solution)/shard_map/project/pallas_call | solution.py:179
  18.3 1.9 %pack.3.refs_0_ = bf16[256,1024]{1,0:T(8,128)(2,1)} custom-call(bf16[128,1024]{1,0:T(8,128)(2,1)} %copy-done.12, bf16[128,1024]{1,0:T(8,128)(2,1)} %copy-done.11), custom_call_target="tpu_custom_call" | custom-call | tf_op jit(solution)/shard_map/pack/pallas_call | solution.py:146
  20.2 3.8 %collective-permute-start.5 = (bf16[256,1024]{1,0:T(8,128)(2,1)}, bf16[256,1024]{1,0:T(8,128)(2,1)S(1)}, u32[]{:S(2)}, u32[]{:S(2)}) collective-permute-start(bf16[256,1024]{1,0:T(8,128)(2,1)} %pack.3.refs_0_), channel_id=1, source_target_pairs={{0,2},{1,3},{2,4},{3,5},{4,6},{5,7},{6,0},{7,1},{8,10},{9,11},{10,... | collective-permute-start | bytes 1572872 | tf_op jit(solution)/shard_map/ppermute | solution.py:377
  23.9 4.8 %collective-permute-start.4 = (bf16[256,1024]{1,0:T(8,128)(2,1)}, bf16[256,1024]{1,0:T(8,128)(2,1)S(1)}, u32[]{:S(2)}, u32[]{:S(2)}) collective-permute-start(bf16[256,1024]{1,0:T(8,128)(2,1)} %pack.3.refs_0_), channel_id=1, source_target_pairs={{0,4},{1,5},{2,6},{3,7},{4,0},{5,1},{6,2},{7,3},{8,12},{9,13},{10,... | collective-permute-start | bytes 1572872 | tf_op jit(solution)/shard_map/ppermute | solution.py:377
  28.7 2.4 %collective-permute-start.3 = (bf16[256,1024]{1,0:T(8,128)(2,1)}, bf16[256,1024]{1,0:T(8,128)(2,1)S(1)}, u32[]{:S(2)}, u32[]{:S(2)}) collective-permute-start(bf16[256,1024]{1,0:T(8,128)(2,1)} %pack.3.refs_0_), channel_id=1, source_target_pairs={{0,6},{1,7},{2,0},{3,1},{4,2},{5,3},{6,4},{7,5},{8,14},{9,15},{10,... | collective-permute-start | bytes 1572872 | tf_op jit(solution)/shard_map/ppermute | solution.py:377
  31.1 4.9 %project.2 = bf16[8,128,512]{2,1,0:T(8,128)(2,1)} custom-call(s32[1]{0:T(128)} %bitcast.half.core, bf16[128,512]{1,0:T(8,128)(2,1)} %attend.1.context, bf16[512,8192]{1,0:T(8,128)(2,1)} %weight.3), custom_call_target="tpu_custom_call" | custom-call | tf_op jit(solution)/shard_map/project/pallas_call | solution.py:179
  36.0 2.9 %add_convert_fusion = bf16[8,128,512]{2,1,0:T(8,128)(2,1)} fusion(bf16[8,128,512]{2,1,0:T(8,128)(2,1)} %collective-permute-done.2, bf16[8,128,512]{2,1,0:T(8,128)(2,1)} %project.2), kind=kLoop, calls=%fused_computation.2 | loop fusion | flops 2097152 | bytes 3145728 | tf_op jit(solution)/shard_map/convert_element_type | solution.py:380
  39.4 12.4 %collective-permute-done.4.refs_4_ = bf16[256,1024]{1,0:T(8,128)(2,1)S(1)} collective-permute-done((bf16[256,1024]{1,0:T(8,128)(2,1)}, bf16[256,1024]{1,0:T(8,128)(2,1)S(1)}, u32[]{:S(2)}, u32[]{:S(2)}) %collective-permute-start.4) | collective-permute-done | bytes 524320 | tf_op jit(solution)/shard_map/ppermute | solution.py:377
  52.8 7.2 %all-to-all-start = ((bf16[8,128,512]{2,1,0:T(8,128)(2,1)}), bf16[8,128,512]{2,1,0:T(8,128)(2,1)S(1)}, u32[]{:S(2)}, u32[]{:S(2)}) async-start(bf16[8,128,512]{2,1,0:T(8,128)(2,1)} %add_convert_fusion), calls=%async_computation | async-start | bytes 2097152 | tf_op jit(solution)/shard_map/all_to_all | solution.py:382
  62.0 1.7 %collective-permute-done.7.refs_3_ = bf16[256,1024]{1,0:T(8,128)(2,1)S(1)} collective-permute-done((bf16[256,1024]{1,0:T(8,128)(2,1)}, bf16[256,1024]{1,0:T(8,128)(2,1)S(1)}, u32[]{:S(2)}, u32[]{:S(2)}) %collective-permute-start.7) | collective-permute-done | bytes 524320 | tf_op jit(solution)/shard_map/ppermute | solution.py:388
  66.1 5.8 %base.1 = bf16[1024,512]{1,0:T(8,128)(2,1)} custom-call(s32[1]{0:T(128)} %bitcast.half.core, bf16[256,1024]{1,0:T(8,128)(2,1)} %pack.3.refs_0_, bf16[256,1024]{1,0:T(8,128)(2,1)} %copy-done.6, bf16[256,1024]{1,0:T(8,128)(2,1)} %copy-done.5, bf16[256,1024]{1,0:T(8,128)(2,1)} %copy-done.7, bf16[256,1024]{1,0:T(8,128)(2,1)} %copy-done.4, ...), custom_call_target="tpu_custom_call" | custom-call | tf_op jit(solution)/shard_map/base/pallas_call | solution.py:220
  71.9 3.0 %all-to-all-done = bf16[8,128,512]{2,1,0:T(8,128)(2,1)S(1)} async-done(((bf16[8,128,512]{2,1,0:T(8,128)(2,1)}), bf16[8,128,512]{2,1,0:T(8,128)(2,1)S(1)}, u32[]{:S(2)}, u32[]{:S(2)}) %all-to-all-start) | async-done | bytes 1048608 | tf_op jit(solution)/shard_map/all_to_all | solution.py:382
  75.8 31.8 %all_to_all.20.source = bf16[8,128,512]{2,1,0:T(8,128)(2,1)S(1)} all-to-all(bf16[8,128,512]{2,1,0:T(8,128)(2,1)S(1)} %broadcast_in_dim.28), channel_id=1, replica_groups={{0,6,4,2,8,14,12,10},{1,7,5,3,9,15,13,11},{18,16,22,20,26,24,30,28},{19..., dimensions={0} | all-to-all | bytes 2097152 | tf_op jit(solution)/shard_map/all_to_all | solution.py:57
  108.6 4.2 %add_top.2.total = bf16[8,128,512]{2,1,0:T(8,128)(2,1)} custom-call(s32[1]{0:T(128)} %bitcast.half.core, s32[8]{0:T(128)} %fusion.2.places, bf16[8,128,512]{2,1,0:T(8,128)(2,1)} %bitcast.11, bf16[8,128,512]{2,1,0:T(8,128)(2,1)} %copy-done, bf16[3,2,512,512]{3,2,1,0:T(8,128)(2,1)} %bitcast.8), custom_call_target="tpu_custom_call" | custom-call | tf_op jit(solution)/shard_map/add_top/pallas_call | solution.py:255
  112.8 4.2 %add_top.3 = bf16[8,128,512]{2,1,0:T(8,128)(2,1)} custom-call(s32[1]{0:T(128)} %bitcast.half.core, s32[8]{0:T(128)} %fusion.2.places, bf16[8,128,512]{2,1,0:T(8,128)(2,1)} %add_top.2.total, bf16[8,128,512]{2,1,0:T(8,128)(2,1)} %collective-permute-done.11.source, bf16[3,2,512,512]{3,2,1,0:T(8,128)(2,1)} %bitcast.9), custom_call_target="tpu_custom_call" | custom-call | tf_op jit(solution)/shard_map/add_top/pallas_call | solution.py:255
  117.0 3.6 %all-to-all-start.2 = ((bf16[8,128,512]{2,1,0:T(8,128)(2,1)}), bf16[8,128,512]{2,1,0:T(8,128)(2,1)S(1)}, u32[]{:S(2)}, u32[]{:S(2)}) async-start(bf16[8,128,512]{2,1,0:T(8,128)(2,1)} %add_top.3), calls=%async_computation.2 | async-start | bytes 2097152 | tf_op jit(solution)/shard_map/all_to_all | solution.py:396
  120.8 15.0 %all-to-all-done.2 = bf16[8,128,512]{2,1,0:T(8,128)(2,1)S(1)} async-done(((bf16[8,128,512]{2,1,0:T(8,128)(2,1)}), bf16[8,128,512]{2,1,0:T(8,128)(2,1)S(1)}, u32[]{:S(2)}, u32[]{:S(2)}) %all-to-all-start.2) | async-done | bytes 1048608 | tf_op jit(solution)/shard_map/all_to_all | solution.py:396
  137.1 3.7 %all-to-all-start.3 = ((bf16[8,128,512]{2,1,0:T(8,128)(2,1)}), bf16[8,128,512]{2,1,0:T(8,128)(2,1)S(1)}, u32[]{:S(2)}, u32[]{:S(2)}) async-start(bf16[8,128,512]{2,1,0:T(8,128)(2,1)} %broadcast_in_dim.31), calls=%async_computation.3 | async-start | bytes 2097152 | tf_op jit(solution)/shard_map/all_to_all | solution.py:57
  141.4 14.3 %all-to-all-done.3.errors = bf16[8,128,512]{2,1,0:T(8,128)(2,1)S(1)} async-done(((bf16[8,128,512]{2,1,0:T(8,128)(2,1)}), bf16[8,128,512]{2,1,0:T(8,128)(2,1)S(1)}, u32[]{:S(2)}, u32[]{:S(2)}) %all-to-all-start.3) | async-done | bytes 1048608 | tf_op jit(solution)/shard_map/all_to_all | solution.py:57
  156.7 9.1 %grad.1 = f32[3,1024,512]{2,1,0:T(8,128)} custom-call(s32[1]{0:T(128)} %bitcast.half.core, s32[8]{0:T(128)} %fusion.places, bf16[8,128,512]{2,1,0:T(8,128)(2,1)} %copy-done.2, bf16[256,1024]{1,0:T(8,128)(2,1)} %pack.3.refs_0_, bf16[256,1024]{1,0:T(8,128)(2,1)} %copy-done.6, bf16[256,1024]{1,0:T(8,128)(2,1)} %copy-done.5, bf16[256,1024]{1,0:T(8,128)(2,1)} %copy-done.7, ...), custom_call_target="tpu_custom_call" | custom-call | tf_op jit(solution)/shard_map/grad/pallas_call | solution.py:329
  (59 shorter events, 11.7 us)
Async XLA Ops:
  2.3 15.1 %collective-permute-start.1 = (bf16[128,1024]{1,0:T(8,128)(2,1)}, bf16[128,1024]{1,0:T(8,128)(2,1)S(1)}, u32[]{:S(2)}, u32[]{:S(2)}) collective-permute-start(bf16[128,1024]{1,0:T(8,128)(2,1)} %pack.2), channel_id=1, source_target_pairs={{0,8},{1,9},{2,26},{3,27},{4,44},{5,45},{6,62},{7,63},{8,72},{9,73... | collective-permute-start | bytes 786440 | tf_op jit(solution)/shard_map/ppermute | solution.py:372
  5.5 12.0 %collective-permute-start = (bf16[128,1024]{1,0:T(8,128)(2,1)}, bf16[128,1024]{1,0:T(8,128)(2,1)S(1)}, u32[]{:S(2)}, u32[]{:S(2)}) collective-permute-start(bf16[128,1024]{1,0:T(8,128)(2,1)} %pack.2), channel_id=1, source_target_pairs={{0,0},{1,1},{2,18},{3,19},{4,36},{5,37},{6,54},{7,55},{8,64},{9,65... | collective-permute-start | bytes 786440 | tf_op jit(solution)/shard_map/ppermute | solution.py:372
  17.5 18.4 %collective-permute-start.2 = (bf16[8,128,512]{2,1,0:T(8,128)(2,1)}, bf16[8,128,512]{2,1,0:T(8,128)(2,1)}, u32[]{:S(2)}, u32[]{:S(2)}) collective-permute-start(bf16[8,128,512]{2,1,0:T(8,128)(2,1)} %project.3), channel_id=1, source_target_pairs={{0,1},{1,0},{2,3},{3,2},{4,5},{5,4},{6,7},{7,6},{8,9},{9,8},{10,11... | collective-permute-start | bytes 3145736 | tf_op jit(solution)/shard_map/ppermute | solution.py:378
  20.2 19.2 %collective-permute-start.5 = (bf16[256,1024]{1,0:T(8,128)(2,1)}, bf16[256,1024]{1,0:T(8,128)(2,1)S(1)}, u32[]{:S(2)}, u32[]{:S(2)}) collective-permute-start(bf16[256,1024]{1,0:T(8,128)(2,1)} %pack.3.refs_0_), channel_id=1, source_target_pairs={{0,2},{1,3},{2,4},{3,5},{4,6},{5,7},{6,0},{7,1},{8,10},{9,11},{10,... | collective-permute-start | bytes 1572872 | tf_op jit(solution)/shard_map/ppermute | solution.py:377
  23.9 27.9 %collective-permute-start.4 = (bf16[256,1024]{1,0:T(8,128)(2,1)}, bf16[256,1024]{1,0:T(8,128)(2,1)S(1)}, u32[]{:S(2)}, u32[]{:S(2)}) collective-permute-start(bf16[256,1024]{1,0:T(8,128)(2,1)} %pack.3.refs_0_), channel_id=1, source_target_pairs={{0,4},{1,5},{2,6},{3,7},{4,0},{5,1},{6,2},{7,3},{8,12},{9,13},{10,... | collective-permute-start | bytes 1572872 | tf_op jit(solution)/shard_map/ppermute | solution.py:377
  28.7 23.1 %collective-permute-start.3 = (bf16[256,1024]{1,0:T(8,128)(2,1)}, bf16[256,1024]{1,0:T(8,128)(2,1)S(1)}, u32[]{:S(2)}, u32[]{:S(2)}) collective-permute-start(bf16[256,1024]{1,0:T(8,128)(2,1)} %pack.3.refs_0_), channel_id=1, source_target_pairs={{0,6},{1,7},{2,0},{3,1},{4,2},{5,3},{6,4},{7,5},{8,14},{9,15},{10,... | collective-permute-start | bytes 1572872 | tf_op jit(solution)/shard_map/ppermute | solution.py:377
  35.9 24.1 %copy-start.1 = (bf16[256,1024]{1,0:T(8,128)(2,1)S(1)}, bf16[256,1024]{1,0:T(8,128)(2,1)}, u32[]{:S(2)}) copy-start(bf16[256,1024]{1,0:T(8,128)(2,1)} %pack.3.refs_0_) | copy-start | bytes 1572868
  39.4 26.7 %copy-start.3 = (bf16[256,1024]{1,0:T(8,128)(2,1)}, bf16[256,1024]{1,0:T(8,128)(2,1)S(1)}, u32[]{:S(2)}) copy-start(bf16[256,1024]{1,0:T(8,128)(2,1)S(1)} %collective-permute-done.5.refs_6_) | copy-start | bytes 1572868
  51.8 1.0 copy-start.5
  52.8 22.0 %all-to-all-start = ((bf16[8,128,512]{2,1,0:T(8,128)(2,1)}), bf16[8,128,512]{2,1,0:T(8,128)(2,1)S(1)}, u32[]{:S(2)}, u32[]{:S(2)}) async-start(bf16[8,128,512]{2,1,0:T(8,128)(2,1)} %add_convert_fusion), calls=%async_computation | async-start | bytes 2097152 | tf_op jit(solution)/shard_map/all_to_all | solution.py:382
  60.0 2.0 %collective-permute-start.6 = (bf16[256,1024]{1,0:T(8,128)(2,1)S(1)}, bf16[256,1024]{1,0:T(8,128)(2,1)S(1)}, u32[]{:S(2)}, u32[]{:S(2)}) collective-permute-start(bf16[256,1024]{1,0:T(8,128)(2,1)S(1)} %copy-done.1), channel_id=1, source_target_pairs={{0,1},{1,0},{2,3},{3,2},{4,5},{5,4},{6,7},{7,6},{8,9},{9,8},{10,11... | collective-permute-start | bytes 1572872 | tf_op jit(solution)/shard_map/ppermute | solution.py:388
  60.1 3.6 %collective-permute-start.7 = (bf16[256,1024]{1,0:T(8,128)(2,1)}, bf16[256,1024]{1,0:T(8,128)(2,1)S(1)}, u32[]{:S(2)}, u32[]{:S(2)}) collective-permute-start(bf16[256,1024]{1,0:T(8,128)(2,1)} %copy-done.5), channel_id=1, source_target_pairs={{0,1},{1,0},{2,3},{3,2},{4,5},{5,4},{6,7},{7,6},{8,9},{9,8},{10,11... | collective-permute-start | bytes 1572872 | tf_op jit(solution)/shard_map/ppermute | solution.py:388
  60.6 3.9 %collective-permute-start.8 = (bf16[256,1024]{1,0:T(8,128)(2,1)}, bf16[256,1024]{1,0:T(8,128)(2,1)S(1)}, u32[]{:S(2)}, u32[]{:S(2)}) collective-permute-start(bf16[256,1024]{1,0:T(8,128)(2,1)} %copy-done.4), channel_id=1, source_target_pairs={{0,1},{1,0},{2,3},{3,2},{4,5},{5,4},{6,7},{7,6},{8,9},{9,8},{10,11... | collective-permute-start | bytes 1572872 | tf_op jit(solution)/shard_map/ppermute | solution.py:388
  60.7 3.8 %collective-permute-start.9 = (bf16[256,1024]{1,0:T(8,128)(2,1)S(1)}, bf16[256,1024]{1,0:T(8,128)(2,1)S(1)}, u32[]{:S(2)}, u32[]{:S(2)}) collective-permute-start(bf16[256,1024]{1,0:T(8,128)(2,1)S(1)} %collective-permute-done.5.refs_6_), channel_id=1, source_target_pairs={{0,1},{1,0},{2,3},{3,2},{4,5},{5,4},{6,7},{7,6},{8,9},{9,8},{10,11... | collective-permute-start | bytes 1572872 | tf_op jit(solution)/shard_map/ppermute | solution.py:388
  62.0 2.5 %copy-start.6 = (bf16[256,1024]{1,0:T(8,128)(2,1)}, bf16[256,1024]{1,0:T(8,128)(2,1)S(1)}, u32[]{:S(2)}) copy-start(bf16[256,1024]{1,0:T(8,128)(2,1)S(1)} %collective-permute-done.6.refs_1_) | copy-start | bytes 1572868
  66.1 8.9 %copy-start.13 = (bf16[128,512]{1,0:T(8,128)(2,1)S(1)}, bf16[128,512]{1,0:T(8,128)(2,1)}, u32[]{:S(2)}) copy-start(bf16[128,512]{1,0:T(8,128)(2,1)} %param.15) | copy-start | bytes 393220
  75.0 45.7 %copy-start.10 = (bf16[128,512]{1,0:T(8,128)(2,1)}, bf16[128,512]{1,0:T(8,128)(2,1)S(1)}, u32[]{:S(2)}) copy-start(bf16[128,512]{1,0:T(8,128)(2,1)S(1)} %add_convert_fusion.1) | copy-start | bytes 393220
  75.0 0.7 collective-permute-start.10
  107.6 1.0 copy-start
  107.6 5.2 %collective-permute-start.11 = (bf16[8,128,512]{2,1,0:T(8,128)(2,1)S(1)}, bf16[8,128,512]{2,1,0:T(8,128)(2,1)}, u32[]{:S(2)}, u32[]{:S(2)}) collective-permute-start(bf16[8,128,512]{2,1,0:T(8,128)(2,1)S(1)} %all_to_all.20.source), channel_id=1, source_target_pairs={{0,1},{1,0},{2,3},{3,2},{4,5},{5,4},{6,7},{7,6},{8,9},{9,8},{10,11... | collective-permute-start | bytes 3145736 | tf_op jit(solution)/shard_map/ppermute | solution.py:393
  112.8 7.8 %copy-start.14 = (s32[32]{0:T(128)S(1)}, s32[32]{0:T(128)}, u32[]{:S(2)}) copy-start(s32[32]{0:T(128)} %param.14) | copy-start | bytes 388
  117.0 18.8 %all-to-all-start.2 = ((bf16[8,128,512]{2,1,0:T(8,128)(2,1)}), bf16[8,128,512]{2,1,0:T(8,128)(2,1)S(1)}, u32[]{:S(2)}, u32[]{:S(2)}) async-start(bf16[8,128,512]{2,1,0:T(8,128)(2,1)} %add_top.3), calls=%async_computation.2 | async-start | bytes 2097152 | tf_op jit(solution)/shard_map/all_to_all | solution.py:396
  137.1 18.6 %all-to-all-start.3 = ((bf16[8,128,512]{2,1,0:T(8,128)(2,1)}), bf16[8,128,512]{2,1,0:T(8,128)(2,1)S(1)}, u32[]{:S(2)}, u32[]{:S(2)}) async-start(bf16[8,128,512]{2,1,0:T(8,128)(2,1)} %broadcast_in_dim.31), calls=%async_computation.3 | async-start | bytes 2097152 | tf_op jit(solution)/shard_map/all_to_all | solution.py:57
  155.7 1.0 copy-start.2
  (6 other events, 4.7 us)

commit v3 on v2

--- a/solution.py
+++ b/solution.py
@@ -233,61 +233,66 @@
     )(core, *pieces, weight)
 
 
-def add_kernel(own, core, places, total, source, weight, out, held, near, held_weight, sems):
+def add_kernel(own, core, places, *refs):
+    *totals, source, weight, out, held, near, held_weight, sems = refs
     blocks, rows, width = source.shape
     half = core[0] if own else 1 - core[0]
     pairs = [(weight.at[2, half], held_weight)]
+    if own:
+        order = (0, 1, 2, 3, 6, 7, 4, 5)
+        lies = [(total, i) for total in totals for i in range(total.shape[0] // rows)]
+        pairs += [
+            (total.at[pl.ds(i * rows, rows)], held.at[places[b]])
+            for (total, i), b in zip(lies, order)
+        ]
+        pairs += [(source, near)]
+    else:
+        for p in range(0, blocks, 2):
+            pairs.append((source.at[p : p + 2], near.at[p : p + 2]))
+            pairs.append((totals[0].at[p : p + 2], held.at[p : p + 2]))
+    copies = fetch(pairs, sems.at[pl.ds(0, len(pairs))])
+    copies[0].wait()
+    if own:
+        for copy in copies[1:]:
+            copy.wait()
     for p in range(0, blocks, 2):
-        pairs.append((source.at[p : p + 2], near.at[p : p + 2]))
-        pairs += [(total.at[places[i] if own else i], held.at[i]) for i in (p, p + 1)]
-    copies = fetch(pairs, sems)
-    copies[0].wait()
-    for p in range(0, blocks, 2):
-        for copy in copies[1 + p // 2 * 3 : 4 + p // 2 * 3]:
-            copy.wait()
+        if not own:
+            copies[1 + p].wait()
+            copies[2 + p].wait()
         added = dot(near[p : p + 2].reshape(2 * rows, width), held_weight[...])
         added = added.reshape(2, rows, width) + held[p : p + 2].astype(jnp.float32)
         out[p : p + 2] = added.astype(out.dtype)
 
 
-def add_top(own, total, source, weight, core, places):
-    blocks, rows, width = total.shape
+def add_top(own, totals, source, weight, core, places):
     return pl.pallas_call(
         functools.partial(add_kernel, own),
-        in_specs=[SCALARS] * 2 + [THERE] * 3,
+        in_specs=[SCALARS] * 2 + [THERE] * (2 + len(totals)),
         out_specs=HERE,
-        out_shape=jax.ShapeDtypeStruct(total.shape, total.dtype),
-        scratch_shapes=[
-            pltpu.VMEM(total.shape, total.dtype),
+        out_shape=jax.ShapeDtypeStruct(source.shape, source.dtype),
+        scratch_shapes=[
+            pltpu.VMEM(source.shape, source.dtype),
             pltpu.VMEM(source.shape, source.dtype),
             pltpu.VMEM(weight.shape[2:], weight.dtype),
-            pltpu.SemaphoreType.DMA((1 + blocks // 2 * 3,)),
+            pltpu.SemaphoreType.DMA((10,)),
         ],
         compiler_params=pltpu.CompilerParams(vmem_limit_bytes=VMEM),
         cost_estimate=FREE,
         name="add_top",
-    )(core, places, total, source, weight)
+    )(core, places, *totals, source, weight)
 
 
 def grad_kernel(core, places, errors, *refs):
     count = len(refs) - 10
-    pieces, (top_own, top_other, out, near, ordered, held, tops, made, sems, out_sems) = (
-        refs[:count],
-        refs[count:],
-    )
+    boths, refs = refs[:count], refs[count:]
+    top_own, top_other, out, near, ordered, held, tops, made, sems, out_sems = refs
     blocks, rows, width = errors.shape
     tokens = blocks * rows
     pairs = [(errors, near)]
-    pairs += [(pieces[i], held.at[0, i // 2]) for i in range(0, count, 2)]
-    first = fetch(pairs, sems)
-    rest = [(pieces[i], held.at[1, i // 2]) for i in range(1, count, 2)]
+    pairs += [(boths[i], held.at[0, i // 2]) for i in range(0, count, 2)]
+    first = fetch(pairs, sems.at[pl.ds(0, len(pairs))])
+    rest = [(boths[i], held.at[1, i // 2]) for i in range(1, count, 2)]
     rest += [(top_own, tops.at[0]), (top_other, tops.at[1])]
-
-    def product(source, target):
-        return lax.dot_general(
-            source, target, (((0,), (0,)), ((), ())), preferred_element_type=jnp.float32
-        )
-
     first[0].wait()
     for p in range(blocks):
         ordered[p * rows : (p + 1) * rows, :] = near[places[p]]
@@ -307,13 +312,16 @@
             slot = step % made.shape[0]
             if step >= made.shape[0]:
                 sent[step - made.shape[0]].wait()
-            columns = slice(part * cut, (part + 1) * cut)
             if i < 4:
-                columns = slice(i % 2 * width + part * cut, i % 2 * width + (part + 1) * cut)
-                source = held[i // 2, :, :, columns].reshape(tokens, cut)
-                made[slot] = product(source, ordered[...])
+                begin = i % 2 * width + part * cut
+                source = held[i // 2, :, :, begin : begin + cut].reshape(tokens, cut)
+                against = ordered[...]
             else:
-                made[slot] = product(tops[i - 4, :, columns], near[...].reshape(tokens, width))
+                source = tops[i - 4, :, part * cut : (part + 1) * cut]
+                against = near[...].reshape(tokens, width)
+            made[slot] = lax.dot_general(
+                source, against, (((0,), (0,)), ((), ())), preferred_element_type=jnp.float32
+            )
             target = out.at[i % 2 if i < 4 else 2, pl.ds(half * width + part * cut, cut)]
             copy = pltpu.make_async_copy(made.at[slot], target, out_sems.at[step])
             copy.start()
@@ -322,10 +330,10 @@
         copy.wait()
 
 
-def grad(errors, pieces, top_own, top_other, core, places):
+def grad(errors, boths, tops, core, places):
     blocks, rows, width = errors.shape
     tokens = blocks * rows
-    count = len(pieces)
+    count = len(boths)
     return pl.pallas_call(
         grad_kernel,
         in_specs=[SCALARS] * 2 + [THERE] * (count + 3),
@@ -334,7 +342,7 @@
         scratch_shapes=[
             pltpu.VMEM(errors.shape, jnp.bfloat16),
             pltpu.VMEM((tokens, width), jnp.bfloat16),
-            pltpu.VMEM((2, count // 2, *pieces[0].shape), jnp.bfloat16),
+            pltpu.VMEM((2, count // 2, *boths[0].shape), jnp.bfloat16),
             pltpu.VMEM((2, tokens, width), jnp.bfloat16),
             pltpu.VMEM((4, width // 2, width), jnp.float32),
             pltpu.SemaphoreType.DMA((count + 3,)),
@@ -343,7 +351,7 @@
         compiler_params=pltpu.CompilerParams(vmem_limit_bytes=VMEM),
         cost_estimate=FREE,
         name="grad",
-    )(core, places, errors, *pieces, top_own, top_other)
+    )(core, places, errors, *boths, *tops)
 
 
 def local(
@@ -364,7 +372,6 @@
     xh, y, core = me_tp // 8, me_tp // 2 % 4, me_tp % 2
     me = core.reshape(1)
     index = jnp.arange(CHIPS)
-    lies = ((z - y - index) % 4 * 2 + (xh ^ (index // 4))).astype(jnp.int32)
     held = ((xh ^ (index % 2)) * 4 + (z - y - index // 2) % 4).astype(jnp.int32)
     weight = merge_weight.reshape(3, 2, width, width)
 
@@ -378,21 +385,26 @@
     taken = lax.ppermute(taken, "tp", OTHER_CORE)
     kept = project(context, out_weight, me)
     pair = (kept.astype(jnp.float32) + taken.astype(jnp.float32)).astype(jnp.bfloat16)
-    pair, *both = lax.optimization_barrier((pair, *both))
+    pair, both[1], both[3] = lax.optimization_barrier((pair, both[1], both[3]))
     parts = lax.all_to_all(pair, "tp", 0, 0, tiled=True, axis_index_groups=SAME_CORE)
     summed = jnp.sum(parts.astype(jnp.float32), axis=0)
     top_hidden = (residual_in.astype(jnp.float32) + summed).astype(jnp.bfloat16)
 
-    pieces = []
-    for piece in both:
-        pieces += [piece, lax.ppermute(piece, "tp", OTHER_CORE)]
-    total = base(pieces, weight, me).reshape(CHIPS, tokens, width)
-    top_hidden, total = lax.optimization_barrier((top_hidden, total))
-
-    top_own = spread(lax.ppermute(top_hidden, BOTH, TO_READER), BOTH, READERS)
+    def twins(pieces):
+        return [half for piece in pieces for half in (piece, lax.ppermute(piece, "tp", OTHER_CORE))]
+
+    first = twins([both[0], both[1], both[3]])
+    total = base(first, weight, me)
+    top_hidden, total, held = lax.optimization_barrier((top_hidden, total, held))
+
+    top_moved = lax.ppermute(top_hidden, BOTH, TO_READER)
+    second = twins([both[2]])
+    rest = base(second, weight, me)
+    top_own = spread(top_moved, BOTH, READERS)
+    top_own, rest = lax.optimization_barrier((top_own, rest))
     top_other = lax.ppermute(top_own, "tp", OTHER_CORE)
-    total = add_top(True, total, top_own, weight, me, lies)
-    total = add_top(False, total, top_other, weight, me, lies)
+    total = add_top(True, (total, rest), top_own, weight, me, held)
+    total = add_top(False, (total,), top_other, weight, me, held)
     merged_parts = lax.all_to_all(total, "dp", 0, 0, tiled=True)
     merged = jnp.sum(merged_parts.astype(jnp.float32), axis=0)
 
@@ -404,8 +416,9 @@
     errors = (keep * (merged - following.astype(jnp.float32)) * scale).astype(jnp.bfloat16)
     errors = spread(errors, "dp")
 
+    boths = first[:4] + second + first[4:]
     tops = [part.reshape(CHIPS * tokens, width) for part in (top_own, top_other)]
-    merge_grad = grad(errors, pieces, *tops, me, held)
+    merge_grad = grad(errors, boths, tops, me, held)
     return (top_hidden, merge_grad)
 
 

time: 167 us -> 156 us (0.934)
  starting transfers between devices: 32 us -> 46.5 us
  waiting for transfers between devices: 48.6 us -> 34.3 us
  blocking collectives: 31.8 us -> 19.5 us
  Pallas kernels: 42 us -> 44.3 us
    all_to_all x1, blocking collectives: 31.8 us -> 19.5 us  [spread(): lax.all_to_all(copies, axis, 0, 0, tiled=True, axis_index_groups=groups)]
    all_to_all x1, starting transfers between devices: 3.74 us -> 15.4 us  [spread(): lax.all_to_all(copies, axis, 0, 0, tiled=True, axis_index_groups=groups)]
    ppermute x3, waiting for transfers between devices: 13 us -> 5.12 us  [local(): both = [both] + [lax.ppermute(both, 'tp', from_y(far)) for far in (1, 2, 3)]]
    all_to_all x1, waiting for transfers between devices: 14.3 us -> 8.14 us  [spread(): lax.all_to_all(copies, axis, 0, 0, tiled=True, axis_index_groups=groups)]
    all_to_all x1, starting transfers between devices: 3.57 us -> 8.18 us  [local(): merged_parts = lax.all_to_all(total, 'dp', 0, 0, tiled=True)]
    pallas_call x1 -> x2, Pallas kernels: 5.78 us -> 8.21 us  [base(): pl.pallas_call(base_kernel, in_specs=[SCALARS] + [THERE] * (len(pieces) +...]
    unnamed x30 -> x24, local copies, waits for them, and re-layouts: 4.68 us -> 4.89 us
  transfers between devices with their start and end apart: 15 -> 15, of which waited for: 8 -> 6; matrix products, arithmetic and copies ran while one was open for 3% -> 3% of each run, Pallas kernels for 16% -> 19%
where the time goes in v3:
time: 156 us
  starting transfers between devices  46.5 us (30%)
  Pallas kernels  44.3 us (28%)
  waiting for transfers between devices  34.3 us (22%)
  blocking collectives  19.5 us (12%)
  local copies, waits for them, and re-layouts  6.24 us (4%)
  other arithmetic  3.91 us (3%)
    all_to_all x1, blocking collectives, spread(): lax.all_to_all(copies, axis, 0, 0, tiled=True, axis_index_groups=groups)  19.5 us
    all_to_all x1, starting transfers between devices, spread(): lax.all_to_all(copies, axis, 0, 0, tiled=True, axis_index_groups=groups)  15.4 us
    all_to_all x1, waiting for transfers between devices, local(): merged_parts = lax.all_to_all(total, 'dp', 0, 0, tiled=True)  14.2 us
    ppermute x3, starting transfers between devices, local(): both = [both] + [lax.ppermute(both, 'tp', from_y(far)) for far in (1, 2, 3)]  10.6 us
    pallas_call x2, Pallas kernels, project(): pl.pallas_call(project_kernel, in_specs=[SCALARS, HERE, THERE], out_specs...  9.74 us
    pallas_call x1, Pallas kernels, grad(): pl.pallas_call(grad_kernel, in_specs=[SCALARS] * 2 + [THERE] * (count + 3...  9.08 us
    pallas_call x2, Pallas kernels, add_top(): pl.pallas_call(functools.partial(add_kernel, own), in_specs=[SCALARS] * 2...  8.28 us
    pallas_call x2, Pallas kernels, base(): pl.pallas_call(base_kernel, in_specs=[SCALARS] + [THERE] * (len(pieces) +...  8.21 us
  transfers between devices with their start and end apart: 15, of which 6 were waited for; matrix products, arithmetic and copies ran while one was open for 3% of the time, Pallas kernels for 19%

profile of v3, /device:TPU:0, one launch (start us, length us, event | category | flops | bytes accessed | tf_op | source)
XLA Modules:
  0.0 155.8 jit_solution(15845390182391985063)
XLA Ops:
  0.6 1.7 %pack.2 = bf16[128,1024]{1,0:T(8,128)(2,1)} custom-call(bf16[128,512]{1,0:T(8,128)(2,1)} %refs_0_.1, bf16[128,512]{1,0:T(8,128)(2,1)} %refs_1_.1), custom_call_target="tpu_custom_call" | custom-call | tf_op jit(solution)/shard_map/pack/pallas_call | solution.py:146
  2.3 3.2 %collective-permute-start.1 = (bf16[128,1024]{1,0:T(8,128)(2,1)}, bf16[128,1024]{1,0:T(8,128)(2,1)S(1)}, u32[]{:S(2)}, u32[]{:S(2)}) collective-permute-start(bf16[128,1024]{1,0:T(8,128)(2,1)} %pack.2), channel_id=1, source_target_pairs={{0,8},{1,9},{2,26},{3,27},{4,44},{5,45},{6,62},{7,63},{8,72},{9,73... | collective-permute-start | bytes 786440 | tf_op jit(solution)/shard_map/ppermute | solution.py:379
  7.1 5.5 %attend.1.context = bf16[128,512]{1,0:T(8,128)(2,1)} custom-call(s32[32]{0:T(128)} %lens.1, bf16[128,512]{1,0:T(8,128)(2,1)} %queries.1, bf16[32,384,128]{2,1,0:T(8,128)(2,1)} %bitcast.11, bf16[32,384,128]{2,1,0:T(8,128)(2,1)} %bitcast.12), custom_call_target="tpu_custom_call" | custom-call | tf_op jit(solution)/shard_map/attend/pallas_call | solution.py:115
  12.6 4.9 %project.3 = bf16[8,128,512]{2,1,0:T(8,128)(2,1)} custom-call(s32[1]{0:T(128)S(6)} %sub.26.half, bf16[128,512]{1,0:T(8,128)(2,1)} %attend.1.context, bf16[512,8192]{1,0:T(8,128)(2,1)} %weight.3), custom_call_target="tpu_custom_call" | custom-call | tf_op jit(solution)/shard_map/project/pallas_call | solution.py:179
  18.3 1.8 %pack.3.refs_0_ = bf16[256,1024]{1,0:T(8,128)(2,1)} custom-call(bf16[128,1024]{1,0:T(8,128)(2,1)} %copy-done.9, bf16[128,1024]{1,0:T(8,128)(2,1)} %copy-done.8), custom_call_target="tpu_custom_call" | custom-call | tf_op jit(solution)/shard_map/pack/pallas_call | solution.py:146
  20.1 3.8 %collective-permute-start.4 = (bf16[256,1024]{1,0:T(8,128)(2,1)}, bf16[256,1024]{1,0:T(8,128)(2,1)S(1)}, u32[]{:S(2)}, u32[]{:S(2)}) collective-permute-start(bf16[256,1024]{1,0:T(8,128)(2,1)} %pack.3.refs_0_), channel_id=1, source_target_pairs={{0,2},{1,3},{2,4},{3,5},{4,6},{5,7},{6,0},{7,1},{8,10},{9,11},{10,... | collective-permute-start | bytes 1572872 | tf_op jit(solution)/shard_map/ppermute | solution.py:384
  23.9 3.4 %collective-permute-start.3 = (bf16[256,1024]{1,0:T(8,128)(2,1)}, bf16[256,1024]{1,0:T(8,128)(2,1)S(1)}, u32[]{:S(2)}, u32[]{:S(2)}) collective-permute-start(bf16[256,1024]{1,0:T(8,128)(2,1)} %pack.3.refs_0_), channel_id=1, source_target_pairs={{0,6},{1,7},{2,0},{3,1},{4,2},{5,3},{6,4},{7,5},{8,14},{9,15},{10,... | collective-permute-start | bytes 1572872 | tf_op jit(solution)/shard_map/ppermute | solution.py:384
  27.3 4.9 %project.2 = bf16[8,128,512]{2,1,0:T(8,128)(2,1)} custom-call(s32[1]{0:T(128)} %bitcast.half.core, bf16[128,512]{1,0:T(8,128)(2,1)} %attend.1.context, bf16[512,8192]{1,0:T(8,128)(2,1)} %weight.3), custom_call_target="tpu_custom_call" | custom-call | tf_op jit(solution)/shard_map/project/pallas_call | solution.py:179
  32.2 2.9 %add_convert_fusion = bf16[8,128,512]{2,1,0:T(8,128)(2,1)} fusion(bf16[8,128,512]{2,1,0:T(8,128)(2,1)} %collective-permute-done.2, bf16[8,128,512]{2,1,0:T(8,128)(2,1)} %project.2), kind=kLoop, calls=%fused_computation.2 | loop fusion | flops 2097152 | bytes 3145728 | tf_op jit(solution)/shard_map/convert_element_type | solution.py:387
  35.1 4.3 %collective-permute-done.4.refs_4_.refs_6_ = bf16[256,1024]{1,0:T(8,128)(2,1)S(1)} collective-permute-done((bf16[256,1024]{1,0:T(8,128)(2,1)}, bf16[256,1024]{1,0:T(8,128)(2,1)S(1)}, u32[]{:S(2)}, u32[]{:S(2)}) %collective-permute-start.4) | collective-permute-done | bytes 524320 | tf_op jit(solution)/shard_map/ppermute | solution.py:384
  41.0 6.0 %all-to-all-start = ((bf16[8,128,512]{2,1,0:T(8,128)(2,1)}), bf16[8,128,512]{2,1,0:T(8,128)(2,1)S(1)}, u32[]{:S(2)}, u32[]{:S(2)}) async-start(bf16[8,128,512]{2,1,0:T(8,128)(2,1)} %add_convert_fusion), calls=%async_computation | async-start | bytes 2097152 | tf_op jit(solution)/shard_map/all_to_all | solution.py:389
  48.3 3.4 %collective-permute-start.9 = (bf16[256,1024]{1,0:T(8,128)(2,1)S(1)}, bf16[256,1024]{1,0:T(8,128)(2,1)}, u32[]{:S(2)}, u32[]{:S(2)}) collective-permute-start(bf16[256,1024]{1,0:T(8,128)(2,1)S(1)} %copy-done.1), channel_id=1, source_target_pairs={{0,4},{1,5},{2,6},{3,7},{4,0},{5,1},{6,2},{7,3},{8,12},{9,13},{10,... | collective-permute-start | bytes 1572872 | tf_op jit(solution)/shard_map/ppermute | solution.py:384
  53.4 4.9 %base.2.refs_0_ = bf16[768,512]{1,0:T(8,128)(2,1)} custom-call(s32[1]{0:T(128)} %bitcast.half.core, bf16[256,1024]{1,0:T(8,128)(2,1)} %pack.3.refs_0_, bf16[256,1024]{1,0:T(8,128)(2,1)} %copy-done.4, bf16[256,1024]{1,0:T(8,128)(2,1)} %copy-done.3, bf16[256,1024]{1,0:T(8,128)(2,1)} %copy-done.5, bf16[256,1024]{1,0:T(8,128)(2,1)} %copy-done.2, ...), custom_call_target="tpu_custom_call" | custom-call | tf_op jit(solution)/shard_map/base/pallas_call | solution.py:220
  58.3 4.6 %all-to-all-done = bf16[8,128,512]{2,1,0:T(8,128)(2,1)S(1)} async-done(((bf16[8,128,512]{2,1,0:T(8,128)(2,1)}), bf16[8,128,512]{2,1,0:T(8,128)(2,1)S(1)}, u32[]{:S(2)}, u32[]{:S(2)}) %all-to-all-start) | async-done | bytes 1048608 | tf_op jit(solution)/shard_map/all_to_all | solution.py:389
  64.9 15.4 %all-to-all-start.1 = ((bf16[8,128,512]{2,1,0:T(8,128)(2,1)}), bf16[8,128,512]{2,1,0:T(8,128)(2,1)S(1)}, u32[]{:S(2)}, u32[]{:S(2)}) async-start(bf16[8,128,512]{2,1,0:T(8,128)(2,1)} %broadcast_in_dim.28), calls=%async_computation.1 | async-start | bytes 2097152 | tf_op jit(solution)/shard_map/all_to_all | solution.py:57
  80.4 2.1 %collective-permute-done.10.refs_1_.refs_5_ = bf16[256,1024]{1,0:T(8,128)(2,1)S(1)} collective-permute-done((bf16[256,1024]{1,0:T(8,128)(2,1)}, bf16[256,1024]{1,0:T(8,128)(2,1)S(1)}, u32[]{:S(2)}, u32[]{:S(2)}) %collective-permute-start.10) | collective-permute-done | bytes 524320 | tf_op jit(solution)/shard_map/ppermute | solution.py:394
  83.3 3.3 %base.3.refs_1_ = bf16[256,512]{1,0:T(8,128)(2,1)} custom-call(s32[1]{0:T(128)} %bitcast.half.core, bf16[256,1024]{1,0:T(8,128)(2,1)} %collective-permute-done.9.refs_0_.refs_4_, bf16[256,1024]{1,0:T(8,128)(2,1)} %copy-done.6, bf16[3,2,512,512]{3,2,1,0:T(8,128)(2,1)} %bitcast.7), custom_call_target="tpu_custom_call" | custom-call | tf_op jit(solution)/shard_map/base/pallas_call | solution.py:220
  86.6 8.1 %all-to-all-done.1.refs_2_ = bf16[8,128,512]{2,1,0:T(8,128)(2,1)S(1)} async-done(((bf16[8,128,512]{2,1,0:T(8,128)(2,1)}), bf16[8,128,512]{2,1,0:T(8,128)(2,1)S(1)}, u32[]{:S(2)}, u32[]{:S(2)}) %all-to-all-start.1) | async-done | bytes 1048608 | tf_op jit(solution)/shard_map/all_to_all | solution.py:57
  95.7 4.1 %add_top.2.refs_0_ = bf16[8,128,512]{2,1,0:T(8,128)(2,1)} custom-call(s32[1]{0:T(128)} %bitcast.half.core, s32[8]{0:T(128)} %fusion.places, bf16[768,512]{1,0:T(8,128)(2,1)} %base.2.refs_0_, bf16[256,512]{1,0:T(8,128)(2,1)} %base.3.refs_1_, bf16[8,128,512]{2,1,0:T(8,128)(2,1)} %copy-done, bf16[3,2,512,512]{3,2,1,0:T(8,128)(2,1)} %bitcast.8), custom_call_target="tpu_custom_call" | custom-call | tf_op jit(solution)/shard_map/add_top/pallas_call | solution.py:268
  99.9 4.1 %add_top.3 = bf16[8,128,512]{2,1,0:T(8,128)(2,1)} custom-call(s32[1]{0:T(128)} %bitcast.half.core, s32[8]{0:T(128)} %fusion.places, bf16[8,128,512]{2,1,0:T(8,128)(2,1)} %add_top.2.refs_0_, bf16[8,128,512]{2,1,0:T(8,128)(2,1)} %collective-permute-done.11.refs_1_, bf16[3,2,512,512]{3,2,1,0:T(8,128)(2,1)} %bitcast.9), custom_call_target="tpu_custom_call" | custom-call | tf_op jit(solution)/shard_map/add_top/pallas_call | solution.py:268
  104.0 8.2 %all-to-all-start.2 = ((bf16[8,128,512]{2,1,0:T(8,128)(2,1)}), bf16[8,128,512]{2,1,0:T(8,128)(2,1)S(1)}, u32[]{:S(2)}, u32[]{:S(2)}) async-start(bf16[8,128,512]{2,1,0:T(8,128)(2,1)} %add_top.3), calls=%async_computation.2 | async-start | bytes 2097152 | tf_op jit(solution)/shard_map/all_to_all | solution.py:408
  112.5 14.2 %all-to-all-done.2 = bf16[8,128,512]{2,1,0:T(8,128)(2,1)S(1)} async-done(((bf16[8,128,512]{2,1,0:T(8,128)(2,1)}), bf16[8,128,512]{2,1,0:T(8,128)(2,1)S(1)}, u32[]{:S(2)}, u32[]{:S(2)}) %all-to-all-start.2) | async-done | bytes 1048608 | tf_op jit(solution)/shard_map/all_to_all | solution.py:408
  127.0 19.5 %all_to_all.20.errors = bf16[8,128,512]{2,1,0:T(8,128)(2,1)} all-to-all(bf16[8,128,512]{2,1,0:T(8,128)(2,1)S(1)} %broadcast_in_dim.31), channel_id=1, replica_groups=mesh['dp'=8,'tp'=16] {'dp'}, dimensions={0} | all-to-all | bytes 2097152 | tf_op jit(solution)/shard_map/all_to_all | solution.py:57
  146.5 9.1 %grad.1 = f32[3,1024,512]{2,1,0:T(8,128)} custom-call(s32[1]{0:T(128)} %bitcast.half.core, s32[8]{0:T(128)} %fusion.places, bf16[8,128,512]{2,1,0:T(8,128)(2,1)} %all_to_all.20.errors, bf16[256,1024]{1,0:T(8,128)(2,1)} %pack.3.refs_0_, bf16[256,1024]{1,0:T(8,128)(2,1)} %copy-done.4, bf16[256,1024]{1,0:T(8,128)(2,1)} %copy-done.3, ...), custom_call_target="tpu_custom_call" | custom-call | tf_op jit(solution)/shard_map/grad/pallas_call | solution.py:337
  (53 shorter events, 11.3 us)
Async XLA Ops:
  2.3 15.1 %collective-permute-start.1 = (bf16[128,1024]{1,0:T(8,128)(2,1)}, bf16[128,1024]{1,0:T(8,128)(2,1)S(1)}, u32[]{:S(2)}, u32[]{:S(2)}) collective-permute-start(bf16[128,1024]{1,0:T(8,128)(2,1)} %pack.2), channel_id=1, source_target_pairs={{0,8},{1,9},{2,26},{3,27},{4,44},{5,45},{6,62},{7,63},{8,72},{9,73... | collective-permute-start | bytes 786440 | tf_op jit(solution)/shard_map/ppermute | solution.py:379
  5.5 12.0 %collective-permute-start = (bf16[128,1024]{1,0:T(8,128)(2,1)}, bf16[128,1024]{1,0:T(8,128)(2,1)S(1)}, u32[]{:S(2)}, u32[]{:S(2)}) collective-permute-start(bf16[128,1024]{1,0:T(8,128)(2,1)} %pack.2), channel_id=1, source_target_pairs={{0,0},{1,1},{2,18},{3,19},{4,36},{5,37},{6,54},{7,55},{8,64},{9,65... | collective-permute-start | bytes 786440 | tf_op jit(solution)/shard_map/ppermute | solution.py:379
  17.5 14.7 %collective-permute-start.2 = (bf16[8,128,512]{2,1,0:T(8,128)(2,1)}, bf16[8,128,512]{2,1,0:T(8,128)(2,1)}, u32[]{:S(2)}, u32[]{:S(2)}) collective-permute-start(bf16[8,128,512]{2,1,0:T(8,128)(2,1)} %project.3), channel_id=1, source_target_pairs={{0,1},{1,0},{2,3},{3,2},{4,5},{5,4},{6,7},{7,6},{8,9},{9,8},{10,11... | collective-permute-start | bytes 3145736 | tf_op jit(solution)/shard_map/ppermute | solution.py:385
  20.1 19.2 %collective-permute-start.4 = (bf16[256,1024]{1,0:T(8,128)(2,1)}, bf16[256,1024]{1,0:T(8,128)(2,1)S(1)}, u32[]{:S(2)}, u32[]{:S(2)}) collective-permute-start(bf16[256,1024]{1,0:T(8,128)(2,1)} %pack.3.refs_0_), channel_id=1, source_target_pairs={{0,2},{1,3},{2,4},{3,5},{4,6},{5,7},{6,0},{7,1},{8,10},{9,11},{10,... | collective-permute-start | bytes 1572872 | tf_op jit(solution)/shard_map/ppermute | solution.py:384
  23.9 16.3 %collective-permute-start.3 = (bf16[256,1024]{1,0:T(8,128)(2,1)}, bf16[256,1024]{1,0:T(8,128)(2,1)S(1)}, u32[]{:S(2)}, u32[]{:S(2)}) collective-permute-start(bf16[256,1024]{1,0:T(8,128)(2,1)} %pack.3.refs_0_), channel_id=1, source_target_pairs={{0,6},{1,7},{2,0},{3,1},{4,2},{5,3},{6,4},{7,5},{8,14},{9,15},{10,... | collective-permute-start | bytes 1572872 | tf_op jit(solution)/shard_map/ppermute | solution.py:384
  32.2 14.9 %copy-start.1 = (bf16[256,1024]{1,0:T(8,128)(2,1)S(1)}, bf16[256,1024]{1,0:T(8,128)(2,1)}, u32[]{:S(2)}) copy-start(bf16[256,1024]{1,0:T(8,128)(2,1)} %pack.3.refs_0_) | copy-start | bytes 1572868
  39.4 0.9 copy-start.2
  40.2 0.8 copy-start.3
  41.0 21.9 %all-to-all-start = ((bf16[8,128,512]{2,1,0:T(8,128)(2,1)}), bf16[8,128,512]{2,1,0:T(8,128)(2,1)S(1)}, u32[]{:S(2)}, u32[]{:S(2)}) async-start(bf16[8,128,512]{2,1,0:T(8,128)(2,1)} %add_convert_fusion), calls=%async_computation | async-start | bytes 2097152 | tf_op jit(solution)/shard_map/all_to_all | solution.py:389
  47.1 4.7 %collective-permute-start.5 = (bf16[256,1024]{1,0:T(8,128)(2,1)S(1)}, bf16[256,1024]{1,0:T(8,128)(2,1)S(1)}, u32[]{:S(2)}, u32[]{:S(2)}) collective-permute-start(bf16[256,1024]{1,0:T(8,128)(2,1)S(1)} %copy-done.1), channel_id=1, source_target_pairs={{0,1},{1,0},{2,3},{3,2},{4,5},{5,4},{6,7},{7,6},{8,9},{9,8},{10,11... | collective-permute-start | bytes 1572872 | tf_op jit(solution)/shard_map/ppermute | solution.py:394
  47.2 5.4 %collective-permute-start.6 = (bf16[256,1024]{1,0:T(8,128)(2,1)}, bf16[256,1024]{1,0:T(8,128)(2,1)S(1)}, u32[]{:S(2)}, u32[]{:S(2)}) collective-permute-start(bf16[256,1024]{1,0:T(8,128)(2,1)} %copy-done.3), channel_id=1, source_target_pairs={{0,1},{1,0},{2,3},{3,2},{4,5},{5,4},{6,7},{7,6},{8,9},{9,8},{10,11... | collective-permute-start | bytes 1572872 | tf_op jit(solution)/shard_map/ppermute | solution.py:394
  47.7 5.7 %collective-permute-start.7 = (bf16[256,1024]{1,0:T(8,128)(2,1)}, bf16[256,1024]{1,0:T(8,128)(2,1)}, u32[]{:S(2)}, u32[]{:S(2)}) collective-permute-start(bf16[256,1024]{1,0:T(8,128)(2,1)} %copy-done.2), channel_id=1, source_target_pairs={{0,1},{1,0},{2,3},{3,2},{4,5},{5,4},{6,7},{7,6},{8,9},{9,8},{10,11... | collective-permute-start | bytes 1572872 | tf_op jit(solution)/shard_map/ppermute | solution.py:394
  48.3 31.9 %collective-permute-start.9 = (bf16[256,1024]{1,0:T(8,128)(2,1)S(1)}, bf16[256,1024]{1,0:T(8,128)(2,1)}, u32[]{:S(2)}, u32[]{:S(2)}) collective-permute-start(bf16[256,1024]{1,0:T(8,128)(2,1)S(1)} %copy-done.1), channel_id=1, source_target_pairs={{0,4},{1,5},{2,6},{3,7},{4,0},{5,1},{6,2},{7,3},{8,12},{9,13},{10,... | collective-permute-start | bytes 1572872 | tf_op jit(solution)/shard_map/ppermute | solution.py:384
  52.6 0.8 copy-start.5
  53.4 9.7 %copy-start.10 = (bf16[128,512]{1,0:T(8,128)(2,1)S(1)}, bf16[128,512]{1,0:T(8,128)(2,1)}, u32[]{:S(2)}) copy-start(bf16[128,512]{1,0:T(8,128)(2,1)} %param.15) | copy-start | bytes 393220
  63.1 49.3 %copy-start.7 = (bf16[128,512]{1,0:T(8,128)(2,1)}, bf16[128,512]{1,0:T(8,128)(2,1)S(1)}, u32[]{:S(2)}) copy-start(bf16[128,512]{1,0:T(8,128)(2,1)S(1)} %add_convert_fusion.1) | copy-start | bytes 393220
  63.2 0.7 collective-permute-start.8
  64.9 29.8 %all-to-all-start.1 = ((bf16[8,128,512]{2,1,0:T(8,128)(2,1)}), bf16[8,128,512]{2,1,0:T(8,128)(2,1)S(1)}, u32[]{:S(2)}, u32[]{:S(2)}) async-start(bf16[8,128,512]{2,1,0:T(8,128)(2,1)} %broadcast_in_dim.28), calls=%async_computation.1 | async-start | bytes 2097152 | tf_op jit(solution)/shard_map/all_to_all | solution.py:57
  80.3 2.2 %collective-permute-start.10 = (bf16[256,1024]{1,0:T(8,128)(2,1)}, bf16[256,1024]{1,0:T(8,128)(2,1)S(1)}, u32[]{:S(2)}, u32[]{:S(2)}) collective-permute-start(bf16[256,1024]{1,0:T(8,128)(2,1)} %collective-permute-done.9.refs_0_.refs_4_), channel_id=1, source_target_pairs={{0,1},{1,0},{2,3},{3,2},{4,5},{5,4},{6,7},{7,6},{8,9},{9,8},{10,11... | collective-permute-start | bytes 1572872 | tf_op jit(solution)/shard_map/ppermute | solution.py:394
  82.5 0.8 copy-start.6
  94.7 1.0 copy-start
  94.7 5.2 %collective-permute-start.11 = (bf16[8,128,512]{2,1,0:T(8,128)(2,1)S(1)}, bf16[8,128,512]{2,1,0:T(8,128)(2,1)}, u32[]{:S(2)}, u32[]{:S(2)}) collective-permute-start(bf16[8,128,512]{2,1,0:T(8,128)(2,1)S(1)} %all-to-all-done.1.refs_2_), channel_id=1, source_target_pairs={{0,1},{1,0},{2,3},{3,2},{4,5},{5,4},{6,7},{7,6},{8,9},{9,8},{10,11... | collective-permute-start | bytes 3145736 | tf_op jit(solution)/shard_map/ppermute | solution.py:405
  99.9 12.4 %copy-start.11 = (s32[32]{0:T(128)S(1)}, s32[32]{0:T(128)}, u32[]{:S(2)}) copy-start(s32[32]{0:T(128)} %param.14) | copy-start | bytes 388
  104.0 22.7 %all-to-all-start.2 = ((bf16[8,128,512]{2,1,0:T(8,128)(2,1)}), bf16[8,128,512]{2,1,0:T(8,128)(2,1)S(1)}, u32[]{:S(2)}, u32[]{:S(2)}) async-start(bf16[8,128,512]{2,1,0:T(8,128)(2,1)} %add_top.3), calls=%async_computation.2 | async-start | bytes 2097152 | tf_op jit(solution)/shard_map/all_to_all | solution.py:408
  (3 other events, 2.3 us)

commit v4 on v3

--- a/solution.py
+++ b/solution.py
@@ -233,53 +233,51 @@
     )(core, *pieces, weight)
 
 
-def add_kernel(own, core, places, *refs):
-    *totals, source, weight, out, held, near, held_weight, sems = refs
-    blocks, rows, width = source.shape
-    half = core[0] if own else 1 - core[0]
-    pairs = [(weight.at[2, half], held_weight)]
-    if own:
-        order = (0, 1, 2, 3, 6, 7, 4, 5)
-        lies = [(total, i) for total in totals for i in range(total.shape[0] // rows)]
-        pairs += [
-            (total.at[pl.ds(i * rows, rows)], held.at[places[b]])
-            for (total, i), b in zip(lies, order)
-        ]
-        pairs += [(source, near)]
-    else:
-        for p in range(0, blocks, 2):
-            pairs.append((source.at[p : p + 2], near.at[p : p + 2]))
-            pairs.append((totals[0].at[p : p + 2], held.at[p : p + 2]))
-    copies = fetch(pairs, sems.at[pl.ds(0, len(pairs))])
-    copies[0].wait()
-    if own:
-        for copy in copies[1:]:
-            copy.wait()
+def join_kernel(core, places, total, rest, own, other, weight, out, held, near, held_weight, made, sems, out_sems):
+    blocks, rows, width = own.shape
+    order = (0, 1, 2, 3, 6, 7, 4, 5)
+    lies = [(part, i) for part in (total, rest) for i in range(part.shape[0] // rows)]
+    pairs = [(weight.at[2], held_weight)]
+    pairs += [
+        (part.at[pl.ds(i * rows, rows)], held.at[places[b]]) for (part, i), b in zip(lies, order)
+    ]
     for p in range(0, blocks, 2):
-        if not own:
-            copies[1 + p].wait()
-            copies[2 + p].wait()
-        added = dot(near[p : p + 2].reshape(2 * rows, width), held_weight[...])
-        added = added.reshape(2, rows, width) + held[p : p + 2].astype(jnp.float32)
-        out[p : p + 2] = added.astype(out.dtype)
-
-
-def add_top(own, totals, source, weight, core, places):
-    return pl.pallas_call(
-        functools.partial(add_kernel, own),
-        in_specs=[SCALARS] * 2 + [THERE] * (2 + len(totals)),
-        out_specs=HERE,
-        out_shape=jax.ShapeDtypeStruct(source.shape, source.dtype),
-        scratch_shapes=[
-            pltpu.VMEM(source.shape, source.dtype),
-            pltpu.VMEM(source.shape, source.dtype),
-            pltpu.VMEM(weight.shape[2:], weight.dtype),
-            pltpu.SemaphoreType.DMA((10,)),
-        ],
-        compiler_params=pltpu.CompilerParams(vmem_limit_bytes=VMEM),
-        cost_estimate=FREE,
-        name="add_top",
-    )(core, places, *totals, source, weight)
+        pairs += [(part.at[p : p + 2], near.at[i, p : p + 2]) for i, part in enumerate((own, other))]
+    copies = fetch(pairs, sems)
+    for copy in copies[: 1 + blocks]:
+        copy.wait()
+    sent = []
+    for p in range(0, blocks, 2):
+        copies[1 + blocks + p].wait()
+        copies[2 + blocks + p].wait()
+        joined = dot(near[0, p : p + 2].reshape(2 * rows, width), held_weight[core[0]])
+        joined += dot(near[1, p : p + 2].reshape(2 * rows, width), held_weight[1 - core[0]])
+        joined = joined.reshape(2, rows, width) + held[p : p + 2].astype(jnp.float32)
+        made[p : p + 2] = joined.astype(made.dtype)
+        sent += fetch([(made.at[p : p + 2], out.at[p : p + 2])], out_sems.at[pl.ds(p // 2, 1)])
+    for copy in sent:
+        copy.wait()
+
+
+def join(total, rest, own, other, weight, core, places):
+    blocks, rows, width = own.shape
+    return pl.pallas_call(
+        join_kernel,
+        in_specs=[SCALARS] * 2 + [THERE] * 5,
+        out_specs=THERE,
+        out_shape=jax.ShapeDtypeStruct(own.shape, own.dtype),
+        scratch_shapes=[
+            pltpu.VMEM(own.shape, own.dtype),
+            pltpu.VMEM((2, *own.shape), own.dtype),
+            pltpu.VMEM(weight.shape[1:], weight.dtype),
+            pltpu.VMEM(own.shape, own.dtype),
+            pltpu.SemaphoreType.DMA((1 + 2 * blocks,)),
+            pltpu.SemaphoreType.DMA((blocks // 2,)),
+        ],
+        compiler_params=pltpu.CompilerParams(vmem_limit_bytes=VMEM),
+        cost_estimate=FREE,
+        name="join",
+    )(core, places, total, rest, own, other, weight)
 
 
 def grad_kernel(core, places, errors, *refs):
@@ -294,11 +292,11 @@
     rest = [(boths[i], held.at[1, i // 2]) for i in range(1, count, 2)]
     rest += [(top_own, tops.at[0]), (top_other, tops.at[1])]
     first[0].wait()
+    rest = fetch(rest, sems.at[pl.ds(len(pairs), len(rest))])
     for p in range(blocks):
         ordered[p * rows : (p + 1) * rows, :] = near[places[p]]
     for copy in first[1:]:
         copy.wait()
-    rest = fetch(rest, sems.at[pl.ds(len(pairs), len(rest))])
     sent = []
     for i in range(6):
         if i == 2:
@@ -403,8 +401,7 @@
     top_own = spread(top_moved, BOTH, READERS)
     top_own, rest = lax.optimization_barrier((top_own, rest))
     top_other = lax.ppermute(top_own, "tp", OTHER_CORE)
-    total = add_top(True, (total, rest), top_own, weight, me, held)
-    total = add_top(False, (total,), top_other, weight, me, held)
+    total = join(total, rest, top_own, top_other, weight, me, held)
     merged_parts = lax.all_to_all(total, "dp", 0, 0, tiled=True)
     merged = jnp.sum(merged_parts.astype(jnp.float32), axis=0)
 

time: 156 us -> 155 us (level)
  Pallas kernels: 44.3 us -> 40.5 us
  waiting for transfers between devices: 34.3 us -> 37.7 us
    pallas_call x2 -> x1, Pallas kernels: 8.28 us -> 4.97 us  [join(): pl.pallas_call(join_kernel, in_specs=[SCALARS] * 2 + [THERE] * 5, out_spe...]
    ppermute x1, waiting for transfers between devices: 0.01 us -> 2.79 us  [local(): top_other = lax.ppermute(top_own, 'tp', OTHER_CORE)]
  transfers between devices with their start and end apart: 15 -> 15, of which waited for: 6 -> 7; matrix products, arithmetic and copies ran while one was open for 3% -> 3% of each run, Pallas kernels for 19% -> 16%
where the time goes in v4:
time: 155 us; the launch traced here: 154 us
  starting transfers between devices  46.5 us (30%)
  Pallas kernels  40.5 us (26%)
  waiting for transfers between devices  37.7 us (24%)
  blocking collectives  19.5 us (13%)
  local copies, waits for them, and re-layouts  5.24 us (3%)
  other arithmetic  3.91 us (3%)
    all_to_all x1, blocking collectives, spread(): lax.all_to_all(copies, axis, 0, 0, tiled=True, axis_index_groups=groups)  19.5 us
    all_to_all x1, starting transfers between devices, spread(): lax.all_to_all(copies, axis, 0, 0, tiled=True, axis_index_groups=groups)  15.4 us
    all_to_all x1, waiting for transfers between devices, local(): merged_parts = lax.all_to_all(total, 'dp', 0, 0, tiled=True)  14.9 us
    ppermute x3, starting transfers between devices, local(): both = [both] + [lax.ppermute(both, 'tp', from_y(far)) for far in (1, 2, 3)]  10.6 us
    pallas_call x2, Pallas kernels, project(): pl.pallas_call(project_kernel, in_specs=[SCALARS, HERE, THERE], out_specs...  9.74 us
    pallas_call x1, Pallas kernels, grad(): pl.pallas_call(grad_kernel, in_specs=[SCALARS] * 2 + [THERE] * (count + 3...  8.56 us
    pallas_call x2, Pallas kernels, base(): pl.pallas_call(base_kernel, in_specs=[SCALARS] + [THERE] * (len(pieces) +...  8.21 us
    all_to_all x1, starting transfers between devices, local(): merged_parts = lax.all_to_all(total, 'dp', 0, 0, tiled=True)  8.18 us
  transfers between devices with their start and end apart: 15, of which 7 were waited for; matrix products, arithmetic and copies ran while one was open for 3% of the time, Pallas kernels for 16%

profile of v4, /device:TPU:0, one launch (start us, length us, event | category | flops | bytes accessed | tf_op | source)
XLA Modules:
  0.0 154.3 jit_solution(1564811450870870758)
XLA Ops:
  0.6 1.7 %pack.2 = bf16[128,1024]{1,0:T(8,128)(2,1)} custom-call(bf16[128,512]{1,0:T(8,128)(2,1)} %refs_0_.1, bf16[128,512]{1,0:T(8,128)(2,1)} %refs_1_.1), custom_call_target="tpu_custom_call" | custom-call | tf_op jit(solution)/shard_map/pack/pallas_call | solution.py:146
  2.3 3.2 %collective-permute-start.1 = (bf16[128,1024]{1,0:T(8,128)(2,1)}, bf16[128,1024]{1,0:T(8,128)(2,1)S(1)}, u32[]{:S(2)}, u32[]{:S(2)}) collective-permute-start(bf16[128,1024]{1,0:T(8,128)(2,1)} %pack.2), channel_id=1, source_target_pairs={{0,8},{1,9},{2,26},{3,27},{4,44},{5,45},{6,62},{7,63},{8,72},{9,73... | collective-permute-start | bytes 786440 | tf_op jit(solution)/shard_map/ppermute | solution.py:377
  7.1 5.5 %attend.1.context = bf16[128,512]{1,0:T(8,128)(2,1)} custom-call(s32[32]{0:T(128)} %lens.1, bf16[128,512]{1,0:T(8,128)(2,1)} %queries.1, bf16[32,384,128]{2,1,0:T(8,128)(2,1)} %bitcast.10, bf16[32,384,128]{2,1,0:T(8,128)(2,1)} %bitcast.11), custom_call_target="tpu_custom_call" | custom-call | tf_op jit(solution)/shard_map/attend/pallas_call | solution.py:115
  12.6 4.9 %project.3 = bf16[8,128,512]{2,1,0:T(8,128)(2,1)} custom-call(s32[1]{0:T(128)S(6)} %sub.26.half, bf16[128,512]{1,0:T(8,128)(2,1)} %attend.1.context, bf16[512,8192]{1,0:T(8,128)(2,1)} %weight.3), custom_call_target="tpu_custom_call" | custom-call | tf_op jit(solution)/shard_map/project/pallas_call | solution.py:179
  18.3 1.8 %pack.3.refs_0_ = bf16[256,1024]{1,0:T(8,128)(2,1)} custom-call(bf16[128,1024]{1,0:T(8,128)(2,1)} %copy-done.9, bf16[128,1024]{1,0:T(8,128)(2,1)} %copy-done.8), custom_call_target="tpu_custom_call" | custom-call | tf_op jit(solution)/shard_map/pack/pallas_call | solution.py:146
  20.1 3.8 %collective-permute-start.4 = (bf16[256,1024]{1,0:T(8,128)(2,1)}, bf16[256,1024]{1,0:T(8,128)(2,1)S(1)}, u32[]{:S(2)}, u32[]{:S(2)}) collective-permute-start(bf16[256,1024]{1,0:T(8,128)(2,1)} %pack.3.refs_0_), channel_id=1, source_target_pairs={{0,2},{1,3},{2,4},{3,5},{4,6},{5,7},{6,0},{7,1},{8,10},{9,11},{10,... | collective-permute-start | bytes 1572872 | tf_op jit(solution)/shard_map/ppermute | solution.py:382
  23.9 3.4 %collective-permute-start.3 = (bf16[256,1024]{1,0:T(8,128)(2,1)}, bf16[256,1024]{1,0:T(8,128)(2,1)S(1)}, u32[]{:S(2)}, u32[]{:S(2)}) collective-permute-start(bf16[256,1024]{1,0:T(8,128)(2,1)} %pack.3.refs_0_), channel_id=1, source_target_pairs={{0,6},{1,7},{2,0},{3,1},{4,2},{5,3},{6,4},{7,5},{8,14},{9,15},{10,... | collective-permute-start | bytes 1572872 | tf_op jit(solution)/shard_map/ppermute | solution.py:382
  27.3 4.9 %project.2 = bf16[8,128,512]{2,1,0:T(8,128)(2,1)} custom-call(s32[1]{0:T(128)} %bitcast.half.core, bf16[128,512]{1,0:T(8,128)(2,1)} %attend.1.context, bf16[512,8192]{1,0:T(8,128)(2,1)} %weight.3), custom_call_target="tpu_custom_call" | custom-call | tf_op jit(solution)/shard_map/project/pallas_call | solution.py:179
  32.2 2.9 %add_convert_fusion = bf16[8,128,512]{2,1,0:T(8,128)(2,1)} fusion(bf16[8,128,512]{2,1,0:T(8,128)(2,1)} %collective-permute-done.2, bf16[8,128,512]{2,1,0:T(8,128)(2,1)} %project.2), kind=kLoop, calls=%fused_computation.2 | loop fusion | flops 2097152 | bytes 3145728 | tf_op jit(solution)/shard_map/convert_element_type | solution.py:385
  35.1 4.3 %collective-permute-done.4.refs_4_.refs_6_ = bf16[256,1024]{1,0:T(8,128)(2,1)S(1)} collective-permute-done((bf16[256,1024]{1,0:T(8,128)(2,1)}, bf16[256,1024]{1,0:T(8,128)(2,1)S(1)}, u32[]{:S(2)}, u32[]{:S(2)}) %collective-permute-start.4) | collective-permute-done | bytes 524320 | tf_op jit(solution)/shard_map/ppermute | solution.py:382
  41.0 6.0 %all-to-all-start = ((bf16[8,128,512]{2,1,0:T(8,128)(2,1)}), bf16[8,128,512]{2,1,0:T(8,128)(2,1)S(1)}, u32[]{:S(2)}, u32[]{:S(2)}) async-start(bf16[8,128,512]{2,1,0:T(8,128)(2,1)} %add_convert_fusion), calls=%async_computation | async-start | bytes 2097152 | tf_op jit(solution)/shard_map/all_to_all | solution.py:387
  48.3 3.4 %collective-permute-start.9 = (bf16[256,1024]{1,0:T(8,128)(2,1)S(1)}, bf16[256,1024]{1,0:T(8,128)(2,1)}, u32[]{:S(2)}, u32[]{:S(2)}) collective-permute-start(bf16[256,1024]{1,0:T(8,128)(2,1)S(1)} %copy-done.1), channel_id=1, source_target_pairs={{0,4},{1,5},{2,6},{3,7},{4,0},{5,1},{6,2},{7,3},{8,12},{9,13},{10,... | collective-permute-start | bytes 1572872 | tf_op jit(solution)/shard_map/ppermute | solution.py:382
  53.4 4.9 %base.2.total = bf16[768,512]{1,0:T(8,128)(2,1)} custom-call(s32[1]{0:T(128)} %bitcast.half.core, bf16[256,1024]{1,0:T(8,128)(2,1)} %pack.3.refs_0_, bf16[256,1024]{1,0:T(8,128)(2,1)} %copy-done.4, bf16[256,1024]{1,0:T(8,128)(2,1)} %copy-done.3, bf16[256,1024]{1,0:T(8,128)(2,1)} %copy-done.5, bf16[256,1024]{1,0:T(8,128)(2,1)} %copy-done.2, ...), custom_call_target="tpu_custom_call" | custom-call | tf_op jit(solution)/shard_map/base/pallas_call | solution.py:220
  58.3 4.6 %all-to-all-done = bf16[8,128,512]{2,1,0:T(8,128)(2,1)S(1)} async-done(((bf16[8,128,512]{2,1,0:T(8,128)(2,1)}), bf16[8,128,512]{2,1,0:T(8,128)(2,1)S(1)}, u32[]{:S(2)}, u32[]{:S(2)}) %all-to-all-start) | async-done | bytes 1048608 | tf_op jit(solution)/shard_map/all_to_all | solution.py:387
  64.9 15.4 %all-to-all-start.1 = ((bf16[8,128,512]{2,1,0:T(8,128)(2,1)}), bf16[8,128,512]{2,1,0:T(8,128)(2,1)S(1)}, u32[]{:S(2)}, u32[]{:S(2)}) async-start(bf16[8,128,512]{2,1,0:T(8,128)(2,1)} %broadcast_in_dim.28), calls=%async_computation.1 | async-start | bytes 2097152 | tf_op jit(solution)/shard_map/all_to_all | solution.py:57
  80.4 2.1 %collective-permute-done.10.refs_1_.refs_5_ = bf16[256,1024]{1,0:T(8,128)(2,1)S(1)} collective-permute-done((bf16[256,1024]{1,0:T(8,128)(2,1)}, bf16[256,1024]{1,0:T(8,128)(2,1)S(1)}, u32[]{:S(2)}, u32[]{:S(2)}) %collective-permute-start.10) | collective-permute-done | bytes 524320 | tf_op jit(solution)/shard_map/ppermute | solution.py:392
  83.3 3.3 %base.3.rest = bf16[256,512]{1,0:T(8,128)(2,1)} custom-call(s32[1]{0:T(128)} %bitcast.half.core, bf16[256,1024]{1,0:T(8,128)(2,1)} %collective-permute-done.9.refs_0_.refs_4_, bf16[256,1024]{1,0:T(8,128)(2,1)} %copy-done.6, bf16[3,2,512,512]{3,2,1,0:T(8,128)(2,1)} %bitcast.7), custom_call_target="tpu_custom_call" | custom-call | tf_op jit(solution)/shard_map/base/pallas_call | solution.py:220
  86.6 8.1 %all-to-all-done.1.own = bf16[8,128,512]{2,1,0:T(8,128)(2,1)S(1)} async-done(((bf16[8,128,512]{2,1,0:T(8,128)(2,1)}), bf16[8,128,512]{2,1,0:T(8,128)(2,1)S(1)}, u32[]{:S(2)}, u32[]{:S(2)}) %all-to-all-start.1) | async-done | bytes 1048608 | tf_op jit(solution)/shard_map/all_to_all | solution.py:57
  94.7 2.8 %collective-permute-done.11.other = bf16[8,128,512]{2,1,0:T(8,128)(2,1)} collective-permute-done((bf16[8,128,512]{2,1,0:T(8,128)(2,1)S(1)}, bf16[8,128,512]{2,1,0:T(8,128)(2,1)}, u32[]{:S(2)}, u32[]{:S(2)}) %collective-permute-start.11) | collective-permute-done | bytes 1048608 | tf_op jit(solution)/shard_map/ppermute | solution.py:403
  97.5 5.0 %join.1 = bf16[8,128,512]{2,1,0:T(8,128)(2,1)} custom-call(s32[1]{0:T(128)} %bitcast.half.core, s32[8]{0:T(128)} %fusion.places, bf16[768,512]{1,0:T(8,128)(2,1)} %base.2.total, bf16[256,512]{1,0:T(8,128)(2,1)} %base.3.rest, bf16[8,128,512]{2,1,0:T(8,128)(2,1)} %copy-done, bf16[8,128,512]{2,1,0:T(8,128)(2,1)} %collective-permute-done.11.other, ...), custom_call_target="tpu_custom_call" | custom-call | tf_op jit(solution)/shard_map/join/pallas_call | solution.py:264
  102.5 8.2 %all-to-all-start.2 = ((bf16[8,128,512]{2,1,0:T(8,128)(2,1)}), bf16[8,128,512]{2,1,0:T(8,128)(2,1)S(1)}, u32[]{:S(2)}, u32[]{:S(2)}) async-start(bf16[8,128,512]{2,1,0:T(8,128)(2,1)} %join.1), calls=%async_computation.2 | async-start | bytes 2097152 | tf_op jit(solution)/shard_map/all_to_all | solution.py:405
  110.9 14.9 %all-to-all-done.2 = bf16[8,128,512]{2,1,0:T(8,128)(2,1)S(1)} async-done(((bf16[8,128,512]{2,1,0:T(8,128)(2,1)}), bf16[8,128,512]{2,1,0:T(8,128)(2,1)S(1)}, u32[]{:S(2)}, u32[]{:S(2)}) %all-to-all-start.2) | async-done | bytes 1048608 | tf_op jit(solution)/shard_map/all_to_all | solution.py:405
  126.1 19.5 %all_to_all.20.errors = bf16[8,128,512]{2,1,0:T(8,128)(2,1)} all-to-all(bf16[8,128,512]{2,1,0:T(8,128)(2,1)S(1)} %broadcast_in_dim.31), channel_id=1, replica_groups=mesh['dp'=8,'tp'=16] {'dp'}, dimensions={0} | all-to-all | bytes 2097152 | tf_op jit(solution)/shard_map/all_to_all | solution.py:57
  145.6 8.6 %grad.1 = f32[3,1024,512]{2,1,0:T(8,128)} custom-call(s32[1]{0:T(128)} %bitcast.half.core, s32[8]{0:T(128)} %fusion.places, bf16[8,128,512]{2,1,0:T(8,128)(2,1)} %all_to_all.20.errors, bf16[256,1024]{1,0:T(8,128)(2,1)} %pack.3.refs_0_, bf16[256,1024]{1,0:T(8,128)(2,1)} %copy-done.4, bf16[256,1024]{1,0:T(8,128)(2,1)} %copy-done.3, ...), custom_call_target="tpu_custom_call" | custom-call | tf_op jit(solution)/shard_map/grad/pallas_call | solution.py:335
  (52 shorter events, 10.3 us)
Async XLA Ops:
  2.3 15.1 %collective-permute-start.1 = (bf16[128,1024]{1,0:T(8,128)(2,1)}, bf16[128,1024]{1,0:T(8,128)(2,1)S(1)}, u32[]{:S(2)}, u32[]{:S(2)}) collective-permute-start(bf16[128,1024]{1,0:T(8,128)(2,1)} %pack.2), channel_id=1, source_target_pairs={{0,8},{1,9},{2,26},{3,27},{4,44},{5,45},{6,62},{7,63},{8,72},{9,73... | collective-permute-start | bytes 786440 | tf_op jit(solution)/shard_map/ppermute | solution.py:377
  5.5 12.0 %collective-permute-start = (bf16[128,1024]{1,0:T(8,128)(2,1)}, bf16[128,1024]{1,0:T(8,128)(2,1)S(1)}, u32[]{:S(2)}, u32[]{:S(2)}) collective-permute-start(bf16[128,1024]{1,0:T(8,128)(2,1)} %pack.2), channel_id=1, source_target_pairs={{0,0},{1,1},{2,18},{3,19},{4,36},{5,37},{6,54},{7,55},{8,64},{9,65... | collective-permute-start | bytes 786440 | tf_op jit(solution)/shard_map/ppermute | solution.py:377
  17.5 14.7 %collective-permute-start.2 = (bf16[8,128,512]{2,1,0:T(8,128)(2,1)}, bf16[8,128,512]{2,1,0:T(8,128)(2,1)}, u32[]{:S(2)}, u32[]{:S(2)}) collective-permute-start(bf16[8,128,512]{2,1,0:T(8,128)(2,1)} %project.3), channel_id=1, source_target_pairs={{0,1},{1,0},{2,3},{3,2},{4,5},{5,4},{6,7},{7,6},{8,9},{9,8},{10,11... | collective-permute-start | bytes 3145736 | tf_op jit(solution)/shard_map/ppermute | solution.py:383
  20.1 19.2 %collective-permute-start.4 = (bf16[256,1024]{1,0:T(8,128)(2,1)}, bf16[256,1024]{1,0:T(8,128)(2,1)S(1)}, u32[]{:S(2)}, u32[]{:S(2)}) collective-permute-start(bf16[256,1024]{1,0:T(8,128)(2,1)} %pack.3.refs_0_), channel_id=1, source_target_pairs={{0,2},{1,3},{2,4},{3,5},{4,6},{5,7},{6,0},{7,1},{8,10},{9,11},{10,... | collective-permute-start | bytes 1572872 | tf_op jit(solution)/shard_map/ppermute | solution.py:382
  23.9 16.3 %collective-permute-start.3 = (bf16[256,1024]{1,0:T(8,128)(2,1)}, bf16[256,1024]{1,0:T(8,128)(2,1)S(1)}, u32[]{:S(2)}, u32[]{:S(2)}) collective-permute-start(bf16[256,1024]{1,0:T(8,128)(2,1)} %pack.3.refs_0_), channel_id=1, source_target_pairs={{0,6},{1,7},{2,0},{3,1},{4,2},{5,3},{6,4},{7,5},{8,14},{9,15},{10,... | collective-permute-start | bytes 1572872 | tf_op jit(solution)/shard_map/ppermute | solution.py:382
  32.2 14.9 %copy-start.1 = (bf16[256,1024]{1,0:T(8,128)(2,1)S(1)}, bf16[256,1024]{1,0:T(8,128)(2,1)}, u32[]{:S(2)}) copy-start(bf16[256,1024]{1,0:T(8,128)(2,1)} %pack.3.refs_0_) | copy-start | bytes 1572868
  39.4 0.9 copy-start.2
  40.2 0.8 copy-start.3
  41.0 21.9 %all-to-all-start = ((bf16[8,128,512]{2,1,0:T(8,128)(2,1)}), bf16[8,128,512]{2,1,0:T(8,128)(2,1)S(1)}, u32[]{:S(2)}, u32[]{:S(2)}) async-start(bf16[8,128,512]{2,1,0:T(8,128)(2,1)} %add_convert_fusion), calls=%async_computation | async-start | bytes 2097152 | tf_op jit(solution)/shard_map/all_to_all | solution.py:387
  47.1 4.7 %collective-permute-start.5 = (bf16[256,1024]{1,0:T(8,128)(2,1)S(1)}, bf16[256,1024]{1,0:T(8,128)(2,1)S(1)}, u32[]{:S(2)}, u32[]{:S(2)}) collective-permute-start(bf16[256,1024]{1,0:T(8,128)(2,1)S(1)} %copy-done.1), channel_id=1, source_target_pairs={{0,1},{1,0},{2,3},{3,2},{4,5},{5,4},{6,7},{7,6},{8,9},{9,8},{10,11... | collective-permute-start | bytes 1572872 | tf_op jit(solution)/shard_map/ppermute | solution.py:392
  47.2 5.4 %collective-permute-start.6 = (bf16[256,1024]{1,0:T(8,128)(2,1)}, bf16[256,1024]{1,0:T(8,128)(2,1)S(1)}, u32[]{:S(2)}, u32[]{:S(2)}) collective-permute-start(bf16[256,1024]{1,0:T(8,128)(2,1)} %copy-done.3), channel_id=1, source_target_pairs={{0,1},{1,0},{2,3},{3,2},{4,5},{5,4},{6,7},{7,6},{8,9},{9,8},{10,11... | collective-permute-start | bytes 1572872 | tf_op jit(solution)/shard_map/ppermute | solution.py:392
  47.7 5.7 %collective-permute-start.7 = (bf16[256,1024]{1,0:T(8,128)(2,1)}, bf16[256,1024]{1,0:T(8,128)(2,1)}, u32[]{:S(2)}, u32[]{:S(2)}) collective-permute-start(bf16[256,1024]{1,0:T(8,128)(2,1)} %copy-done.2), channel_id=1, source_target_pairs={{0,1},{1,0},{2,3},{3,2},{4,5},{5,4},{6,7},{7,6},{8,9},{9,8},{10,11... | collective-permute-start | bytes 1572872 | tf_op jit(solution)/shard_map/ppermute | solution.py:392
  48.3 31.9 %collective-permute-start.9 = (bf16[256,1024]{1,0:T(8,128)(2,1)S(1)}, bf16[256,1024]{1,0:T(8,128)(2,1)}, u32[]{:S(2)}, u32[]{:S(2)}) collective-permute-start(bf16[256,1024]{1,0:T(8,128)(2,1)S(1)} %copy-done.1), channel_id=1, source_target_pairs={{0,4},{1,5},{2,6},{3,7},{4,0},{5,1},{6,2},{7,3},{8,12},{9,13},{10,... | collective-permute-start | bytes 1572872 | tf_op jit(solution)/shard_map/ppermute | solution.py:382
  52.6 0.8 copy-start.5
  53.4 9.7 %copy-start.10 = (bf16[128,512]{1,0:T(8,128)(2,1)S(1)}, bf16[128,512]{1,0:T(8,128)(2,1)}, u32[]{:S(2)}) copy-start(bf16[128,512]{1,0:T(8,128)(2,1)} %param.15) | copy-start | bytes 393220
  63.1 47.7 %copy-start.7 = (bf16[128,512]{1,0:T(8,128)(2,1)}, bf16[128,512]{1,0:T(8,128)(2,1)S(1)}, u32[]{:S(2)}) copy-start(bf16[128,512]{1,0:T(8,128)(2,1)S(1)} %add_convert_fusion.1) | copy-start | bytes 393220
  63.2 0.7 collective-permute-start.8
  64.9 29.8 %all-to-all-start.1 = ((bf16[8,128,512]{2,1,0:T(8,128)(2,1)}), bf16[8,128,512]{2,1,0:T(8,128)(2,1)S(1)}, u32[]{:S(2)}, u32[]{:S(2)}) async-start(bf16[8,128,512]{2,1,0:T(8,128)(2,1)} %broadcast_in_dim.28), calls=%async_computation.1 | async-start | bytes 2097152 | tf_op jit(solution)/shard_map/all_to_all | solution.py:57
  80.3 2.2 %collective-permute-start.10 = (bf16[256,1024]{1,0:T(8,128)(2,1)}, bf16[256,1024]{1,0:T(8,128)(2,1)S(1)}, u32[]{:S(2)}, u32[]{:S(2)}) collective-permute-start(bf16[256,1024]{1,0:T(8,128)(2,1)} %collective-permute-done.9.refs_0_.refs_4_), channel_id=1, source_target_pairs={{0,1},{1,0},{2,3},{3,2},{4,5},{5,4},{6,7},{7,6},{8,9},{9,8},{10,11... | collective-permute-start | bytes 1572872 | tf_op jit(solution)/shard_map/ppermute | solution.py:392
  82.5 0.8 copy-start.6
  86.6 24.1 %copy-start.11 = (s32[32]{0:T(128)S(1)}, s32[32]{0:T(128)}, u32[]{:S(2)}) copy-start(s32[32]{0:T(128)} %param.14) | copy-start | bytes 388
  94.7 2.8 %copy-start = (bf16[8,128,512]{2,1,0:T(8,128)(2,1)}, bf16[8,128,512]{2,1,0:T(8,128)(2,1)S(1)}, u32[]{:S(2)}) copy-start(bf16[8,128,512]{2,1,0:T(8,128)(2,1)S(1)} %all-to-all-done.1.own) | copy-start | bytes 3145732
  94.7 2.8 %collective-permute-start.11 = (bf16[8,128,512]{2,1,0:T(8,128)(2,1)S(1)}, bf16[8,128,512]{2,1,0:T(8,128)(2,1)}, u32[]{:S(2)}, u32[]{:S(2)}) collective-permute-start(bf16[8,128,512]{2,1,0:T(8,128)(2,1)S(1)} %all-to-all-done.1.own), channel_id=1, source_target_pairs={{0,1},{1,0},{2,3},{3,2},{4,5},{5,4},{6,7},{7,6},{8,9},{9,8},{10,11... | collective-permute-start | bytes 3145736 | tf_op jit(solution)/shard_map/ppermute | solution.py:403
  102.5 23.3 %all-to-all-start.2 = ((bf16[8,128,512]{2,1,0:T(8,128)(2,1)}), bf16[8,128,512]{2,1,0:T(8,128)(2,1)S(1)}, u32[]{:S(2)}, u32[]{:S(2)}) async-start(bf16[8,128,512]{2,1,0:T(8,128)(2,1)} %join.1), calls=%async_computation.2 | async-start | bytes 2097152 | tf_op jit(solution)/shard_map/all_to_all | solution.py:405
  (3 other events, 2.3 us)

commit v5 on v4

--- a/solution.py
+++ b/solution.py
@@ -67,7 +67,7 @@
     return copies
 
 
-def attend_kernel(lens, queries, keys, values, out, held, scores, weights, gathered, sems):
+def attend_kernel(lens, half, queries, keys, values, weight, out, made, held, scores, weights, gathered, strips, sems, strip_sems):
     rows, width = held.shape[1], keys.shape[2]
     heads = queries.shape[1] // width
     size = heads * STEPS
@@ -78,6 +78,14 @@
             for j, source in enumerate((keys, values))
         ],
         sems,
+    )
+    cut = made.shape[-1]
+    arriving = fetch(
+        [
+            (weight.at[:, pl.ds((2 * t + half[0]) * cut, cut)], strips.at[t])
+            for t in range(CHIPS)
+        ],
+        strip_sems,
     )
     shape = (size, keys.shape[1])
     position = lax.broadcasted_iota(jnp.int32, shape, 1)
@@ -106,28 +114,37 @@
     for h in range(heads):
         context = [gathered[r, h * STEPS : (h + 1) * STEPS, :] for r in range(rows)]
         out[:, h * width : (h + 1) * width] = jnp.concatenate(context, axis=0).astype(out.dtype)
-
-
-def attend(queries, keys, values, lens):
+    for t in range(CHIPS):
+        arriving[t].wait()
+        made[t] = dot(out[...], strips[t]).astype(made.dtype)
+
+
+def attend(queries, keys, values, lens, weight, half):
     rows, positions, width = keys.shape
     tokens, depth = queries.shape
     size = STEPS * depth // width
+    cut = weight.shape[1] // (2 * CHIPS)
     return pl.pallas_call(
         attend_kernel,
-        in_specs=[SCALARS, HERE, THERE, THERE],
-        out_specs=HERE,
-        out_shape=jax.ShapeDtypeStruct(queries.shape, queries.dtype),
+        in_specs=[SCALARS, SCALARS, HERE, THERE, THERE, THERE],
+        out_specs=[HERE, HERE],
+        out_shape=[
+            jax.ShapeDtypeStruct(queries.shape, queries.dtype),
+            jax.ShapeDtypeStruct((CHIPS, tokens, cut), jnp.bfloat16),
+        ],
         scratch_shapes=[
             pltpu.VMEM((2, rows, positions, width), jnp.bfloat16),
             pltpu.VMEM((rows * size, positions), jnp.float32),
             pltpu.VMEM((rows * size, positions), jnp.bfloat16),
             pltpu.VMEM((rows, size, width), jnp.float32),
+            pltpu.VMEM((CHIPS, depth, cut), jnp.bfloat16),
             pltpu.SemaphoreType.DMA((4,)),
+            pltpu.SemaphoreType.DMA((CHIPS,)),
         ],
         compiler_params=pltpu.CompilerParams(vmem_limit_bytes=VMEM),
         cost_estimate=FREE,
         name="attend",
-    )(lens, queries, keys, values)
+    )(lens, half, queries, keys, values, weight)
 
 
 def pack_kernel(cuts, *refs):
@@ -375,8 +392,9 @@
 
     both = pack([low_hidden, mid_hidden], 1)
     both = [lax.ppermute(both, BOTH, way) for way in (TO_READER, TO_ACROSS)]
-    context = attend(queries, keys_cache[:, 0], values_cache[:, 0], prefix_len)
-    taken = project(context, out_weight, 1 - me)
+    context, taken = attend(
+        queries, keys_cache[:, 0], values_cache[:, 0], prefix_len, out_weight, 1 - me
+    )
     taken, *both = lax.optimization_barrier((taken, *both))
     both = pack(both, 0)
     both = [both] + [lax.ppermute(both, "tp", from_y(far)) for far in (1, 2, 3)]

time: 155 us -> 153 us (0.987)
  Pallas kernels: 40.5 us -> 38.6 us
    pallas_call x2 -> x1, Pallas kernels: 9.74 us -> 4.86 us  [project(): pl.pallas_call(project_kernel, in_specs=[SCALARS, HERE, THERE], out_specs...]
    pallas_call x1, Pallas kernels: 5.48 us -> 8.47 us  [attend(): pl.pallas_call(attend_kernel, in_specs=[SCALARS, SCALARS, HERE, THERE, TH...]
    all_to_all x1, starting transfers between devices: 8.18 us -> 5.54 us  [local(): merged_parts = lax.all_to_all(total, 'dp', 0, 0, tiled=True)]
  transfers between devices with their start and end apart: 15 -> 15, of which waited for: 7 -> 7; matrix products, arithmetic and copies ran while one was open for 3% -> 3% of each run, Pallas kernels for 16% -> 15%
where the time goes in v5:
time: 153 us; the launch traced here: 152 us
  starting transfers between devices  45 us (29%)
  waiting for transfers between devices  39.1 us (26%)
  Pallas kernels  38.6 us (25%)
  blocking collectives  19.5 us (13%)
  local copies, waits for them, and re-layouts  5.26 us (3%)
  other arithmetic  3.92 us (3%)
    all_to_all x1, blocking collectives, spread(): lax.all_to_all(copies, axis, 0, 0, tiled=True, axis_index_groups=groups)  19.5 us
    all_to_all x1, starting transfers between devices, spread(): lax.all_to_all(copies, axis, 0, 0, tiled=True, axis_index_groups=groups)  15.3 us
    all_to_all x1, waiting for transfers between devices, local(): merged_parts = lax.all_to_all(total, 'dp', 0, 0, tiled=True)  14.9 us
    ppermute x3, starting transfers between devices, local(): both = [both] + [lax.ppermute(both, 'tp', from_y(far)) for far in (1, 2, 3)]  11.8 us
    all_to_all x1, waiting for transfers between devices, spread(): lax.all_to_all(copies, axis, 0, 0, tiled=True, axis_index_groups=groups)  8.9 us
    pallas_call x1, Pallas kernels, grad(): pl.pallas_call(grad_kernel, in_specs=[SCALARS] * 2 + [THERE] * (count + 3...  8.56 us
    pallas_call x1, Pallas kernels, attend(): pl.pallas_call(attend_kernel, in_specs=[SCALARS, SCALARS, HERE, THERE, TH...  8.47 us
    pallas_call x2, Pallas kernels, base(): pl.pallas_call(base_kernel, in_specs=[SCALARS] + [THERE] * (len(pieces) +...  8.22 us
  transfers between devices with their start and end apart: 15, of which 7 were waited for; matrix products, arithmetic and copies ran while one was open for 3% of the time, Pallas kernels for 15%

profile of v5, /device:TPU:0, one launch (start us, length us, event | category | flops | bytes accessed | tf_op | source)
XLA Modules:
  0.0 152.4 jit_solution(17088821634140150972)
XLA Ops:
  0.6 1.7 %pack.2 = bf16[128,1024]{1,0:T(8,128)(2,1)} custom-call(bf16[128,512]{1,0:T(8,128)(2,1)} %refs_0_.1, bf16[128,512]{1,0:T(8,128)(2,1)} %refs_1_.1), custom_call_target="tpu_custom_call" | custom-call | tf_op jit(solution)/shard_map/pack/pallas_call | solution.py:163
  2.3 3.2 %collective-permute-start.1 = (bf16[128,1024]{1,0:T(8,128)(2,1)}, bf16[128,1024]{1,0:T(8,128)(2,1)S(1)}, u32[]{:S(2)}, u32[]{:S(2)}) collective-permute-start(bf16[128,1024]{1,0:T(8,128)(2,1)} %pack.2), channel_id=1, source_target_pairs={{0,8},{1,9},{2,26},{3,27},{4,44},{5,45},{6,62},{7,63},{8,72},{9,73... | collective-permute-start | bytes 786440 | tf_op jit(solution)/shard_map/ppermute | solution.py:394
  5.5 1.6 %collective-permute-start = (bf16[128,1024]{1,0:T(8,128)(2,1)}, bf16[128,1024]{1,0:T(8,128)(2,1)S(1)}, u32[]{:S(2)}, u32[]{:S(2)}) collective-permute-start(bf16[128,1024]{1,0:T(8,128)(2,1)} %pack.2), channel_id=1, source_target_pairs={{0,0},{1,1},{2,18},{3,19},{4,36},{5,37},{6,54},{7,55},{8,64},{9,65... | collective-permute-start | bytes 786440 | tf_op jit(solution)/shard_map/ppermute | solution.py:394
  7.1 8.5 %attend.1 = (bf16[128,512]{1,0:T(8,128)(2,1)}, bf16[8,128,512]{2,1,0:T(8,128)(2,1)}) custom-call(s32[32]{0:T(128)} %lens.1, s32[1]{0:T(128)S(6)} %sub.26.half, bf16[128,512]{1,0:T(8,128)(2,1)} %queries.1, bf16[32,384,128]{2,1,0:T(8,128)(2,1)} %bitcast.10, bf16[32,384,128]{2,1,0:T(8,128)(2,1)} %bitcast.11, bf16[512,8192]{1,0:T(8,128)(2,1)} %weight.3), custom_call_target="tpu_custom_call" | custom-call | tf_op jit(solution)/shard_map/attend/pallas_call | solution.py:127
  16.4 1.9 %pack.3.refs_0_ = bf16[256,1024]{1,0:T(8,128)(2,1)} custom-call(bf16[128,1024]{1,0:T(8,128)(2,1)} %copy-done.9, bf16[128,1024]{1,0:T(8,128)(2,1)} %copy-done.8), custom_call_target="tpu_custom_call" | custom-call | tf_op jit(solution)/shard_map/pack/pallas_call | solution.py:163
  18.3 5.4 %collective-permute-start.4 = (bf16[256,1024]{1,0:T(8,128)(2,1)}, bf16[256,1024]{1,0:T(8,128)(2,1)S(1)}, u32[]{:S(2)}, u32[]{:S(2)}) collective-permute-start(bf16[256,1024]{1,0:T(8,128)(2,1)} %pack.3.refs_0_), channel_id=1, source_target_pairs={{0,2},{1,3},{2,4},{3,5},{4,6},{5,7},{6,0},{7,1},{8,10},{9,11},{10,... | collective-permute-start | bytes 1572872 | tf_op jit(solution)/shard_map/ppermute | solution.py:400
  23.7 3.0 %collective-permute-start.3 = (bf16[256,1024]{1,0:T(8,128)(2,1)}, bf16[256,1024]{1,0:T(8,128)(2,1)S(1)}, u32[]{:S(2)}, u32[]{:S(2)}) collective-permute-start(bf16[256,1024]{1,0:T(8,128)(2,1)} %pack.3.refs_0_), channel_id=1, source_target_pairs={{0,6},{1,7},{2,0},{3,1},{4,2},{5,3},{6,4},{7,5},{8,14},{9,15},{10,... | collective-permute-start | bytes 1572872 | tf_op jit(solution)/shard_map/ppermute | solution.py:400
  26.7 4.9 %project.1 = bf16[8,128,512]{2,1,0:T(8,128)(2,1)} custom-call(s32[1]{0:T(128)} %bitcast.half.core, bf16[128,512]{1,0:T(8,128)(2,1)} %get-tuple-element.15.context, bf16[512,8192]{1,0:T(8,128)(2,1)} %weight.3), custom_call_target="tpu_custom_call" | custom-call | tf_op jit(solution)/shard_map/project/pallas_call | solution.py:196
  31.6 2.9 %add_convert_fusion = bf16[8,128,512]{2,1,0:T(8,128)(2,1)} fusion(bf16[8,128,512]{2,1,0:T(8,128)(2,1)} %collective-permute-done.2, bf16[8,128,512]{2,1,0:T(8,128)(2,1)} %project.1), kind=kLoop, calls=%fused_computation.2 | loop fusion | flops 2097152 | bytes 3145728 | tf_op jit(solution)/shard_map/convert_element_type | solution.py:403
  34.5 4.3 %collective-permute-done.4.refs_4_.refs_6_ = bf16[256,1024]{1,0:T(8,128)(2,1)S(1)} collective-permute-done((bf16[256,1024]{1,0:T(8,128)(2,1)}, bf16[256,1024]{1,0:T(8,128)(2,1)S(1)}, u32[]{:S(2)}, u32[]{:S(2)}) %collective-permute-start.4) | collective-permute-done | bytes 524320 | tf_op jit(solution)/shard_map/ppermute | solution.py:400
  41.0 6.0 %all-to-all-start = ((bf16[8,128,512]{2,1,0:T(8,128)(2,1)}), bf16[8,128,512]{2,1,0:T(8,128)(2,1)S(1)}, u32[]{:S(2)}, u32[]{:S(2)}) async-start(bf16[8,128,512]{2,1,0:T(8,128)(2,1)} %add_convert_fusion), calls=%async_computation | async-start | bytes 2097152 | tf_op jit(solution)/shard_map/all_to_all | solution.py:405
  48.4 3.4 %collective-permute-start.9 = (bf16[256,1024]{1,0:T(8,128)(2,1)S(1)}, bf16[256,1024]{1,0:T(8,128)(2,1)}, u32[]{:S(2)}, u32[]{:S(2)}) collective-permute-start(bf16[256,1024]{1,0:T(8,128)(2,1)S(1)} %copy-done.1), channel_id=1, source_target_pairs={{0,4},{1,5},{2,6},{3,7},{4,0},{5,1},{6,2},{7,3},{8,12},{9,13},{10,... | collective-permute-start | bytes 1572872 | tf_op jit(solution)/shard_map/ppermute | solution.py:400
  53.4 5.0 %base.2.total = bf16[768,512]{1,0:T(8,128)(2,1)} custom-call(s32[1]{0:T(128)} %bitcast.half.core, bf16[256,1024]{1,0:T(8,128)(2,1)} %pack.3.refs_0_, bf16[256,1024]{1,0:T(8,128)(2,1)} %copy-done.4, bf16[256,1024]{1,0:T(8,128)(2,1)} %copy-done.3, bf16[256,1024]{1,0:T(8,128)(2,1)} %copy-done.5, bf16[256,1024]{1,0:T(8,128)(2,1)} %copy-done.2, ...), custom_call_target="tpu_custom_call" | custom-call | tf_op jit(solution)/shard_map/base/pallas_call | solution.py:237
  58.4 4.6 %all-to-all-done = bf16[8,128,512]{2,1,0:T(8,128)(2,1)S(1)} async-done(((bf16[8,128,512]{2,1,0:T(8,128)(2,1)}), bf16[8,128,512]{2,1,0:T(8,128)(2,1)S(1)}, u32[]{:S(2)}, u32[]{:S(2)}) %all-to-all-start) | async-done | bytes 1048608 | tf_op jit(solution)/shard_map/all_to_all | solution.py:405
  64.9 15.3 %all-to-all-start.1 = ((bf16[8,128,512]{2,1,0:T(8,128)(2,1)}), bf16[8,128,512]{2,1,0:T(8,128)(2,1)S(1)}, u32[]{:S(2)}, u32[]{:S(2)}) async-start(bf16[8,128,512]{2,1,0:T(8,128)(2,1)} %broadcast_in_dim.28), calls=%async_computation.1 | async-start | bytes 2097152 | tf_op jit(solution)/shard_map/all_to_all | solution.py:57
  80.3 2.1 %collective-permute-done.10.refs_1_.refs_5_ = bf16[256,1024]{1,0:T(8,128)(2,1)S(1)} collective-permute-done((bf16[256,1024]{1,0:T(8,128)(2,1)}, bf16[256,1024]{1,0:T(8,128)(2,1)S(1)}, u32[]{:S(2)}, u32[]{:S(2)}) %collective-permute-start.10) | collective-permute-done | bytes 524320 | tf_op jit(solution)/shard_map/ppermute | solution.py:410
  83.3 3.3 %base.3.rest = bf16[256,512]{1,0:T(8,128)(2,1)} custom-call(s32[1]{0:T(128)} %bitcast.half.core, bf16[256,1024]{1,0:T(8,128)(2,1)} %collective-permute-done.9.refs_0_.refs_4_, bf16[256,1024]{1,0:T(8,128)(2,1)} %copy-done.6, bf16[3,2,512,512]{3,2,1,0:T(8,128)(2,1)} %bitcast.7), custom_call_target="tpu_custom_call" | custom-call | tf_op jit(solution)/shard_map/base/pallas_call | solution.py:237
  86.5 8.9 %all-to-all-done.1.own = bf16[8,128,512]{2,1,0:T(8,128)(2,1)S(1)} async-done(((bf16[8,128,512]{2,1,0:T(8,128)(2,1)}), bf16[8,128,512]{2,1,0:T(8,128)(2,1)S(1)}, u32[]{:S(2)}, u32[]{:S(2)}) %all-to-all-start.1) | async-done | bytes 1048608 | tf_op jit(solution)/shard_map/all_to_all | solution.py:57
  95.4 2.8 %collective-permute-done.11.other = bf16[8,128,512]{2,1,0:T(8,128)(2,1)} collective-permute-done((bf16[8,128,512]{2,1,0:T(8,128)(2,1)S(1)}, bf16[8,128,512]{2,1,0:T(8,128)(2,1)}, u32[]{:S(2)}, u32[]{:S(2)}) %collective-permute-start.11) | collective-permute-done | bytes 1048608 | tf_op jit(solution)/shard_map/ppermute | solution.py:421
  98.2 5.0 %join.1 = bf16[8,128,512]{2,1,0:T(8,128)(2,1)} custom-call(s32[1]{0:T(128)} %bitcast.half.core, s32[8]{0:T(128)} %fusion.places, bf16[768,512]{1,0:T(8,128)(2,1)} %base.2.total, bf16[256,512]{1,0:T(8,128)(2,1)} %base.3.rest, bf16[8,128,512]{2,1,0:T(8,128)(2,1)} %copy-done, bf16[8,128,512]{2,1,0:T(8,128)(2,1)} %collective-permute-done.11.other, ...), custom_call_target="tpu_custom_call" | custom-call | tf_op jit(solution)/shard_map/join/pallas_call | solution.py:281
  103.2 5.5 %all-to-all-start.2 = ((bf16[8,128,512]{2,1,0:T(8,128)(2,1)}), bf16[8,128,512]{2,1,0:T(8,128)(2,1)S(1)}, u32[]{:S(2)}, u32[]{:S(2)}) async-start(bf16[8,128,512]{2,1,0:T(8,128)(2,1)} %join.1), calls=%async_computation.2 | async-start | bytes 2097152 | tf_op jit(solution)/shard_map/all_to_all | solution.py:423
  109.0 14.9 %all-to-all-done.2 = bf16[8,128,512]{2,1,0:T(8,128)(2,1)S(1)} async-done(((bf16[8,128,512]{2,1,0:T(8,128)(2,1)}), bf16[8,128,512]{2,1,0:T(8,128)(2,1)S(1)}, u32[]{:S(2)}, u32[]{:S(2)}) %all-to-all-start.2) | async-done | bytes 1048608 | tf_op jit(solution)/shard_map/all_to_all | solution.py:423
  124.2 19.5 %all_to_all.20.errors = bf16[8,128,512]{2,1,0:T(8,128)(2,1)} all-to-all(bf16[8,128,512]{2,1,0:T(8,128)(2,1)S(1)} %broadcast_in_dim.31), channel_id=1, replica_groups=mesh['dp'=8,'tp'=16] {'dp'}, dimensions={0} | all-to-all | bytes 2097152 | tf_op jit(solution)/shard_map/all_to_all | solution.py:57
  143.7 8.6 %grad.1 = f32[3,1024,512]{2,1,0:T(8,128)} custom-call(s32[1]{0:T(128)} %bitcast.half.core, s32[8]{0:T(128)} %fusion.places, bf16[8,128,512]{2,1,0:T(8,128)(2,1)} %all_to_all.20.errors, bf16[256,1024]{1,0:T(8,128)(2,1)} %pack.3.refs_0_, bf16[256,1024]{1,0:T(8,128)(2,1)} %copy-done.4, bf16[256,1024]{1,0:T(8,128)(2,1)} %copy-done.3, ...), custom_call_target="tpu_custom_call" | custom-call | tf_op jit(solution)/shard_map/grad/pallas_call | solution.py:352
  (51 shorter events, 9.4 us)
Async XLA Ops:
  2.3 13.2 %collective-permute-start.1 = (bf16[128,1024]{1,0:T(8,128)(2,1)}, bf16[128,1024]{1,0:T(8,128)(2,1)S(1)}, u32[]{:S(2)}, u32[]{:S(2)}) collective-permute-start(bf16[128,1024]{1,0:T(8,128)(2,1)} %pack.2), channel_id=1, source_target_pairs={{0,8},{1,9},{2,26},{3,27},{4,44},{5,45},{6,62},{7,63},{8,72},{9,73... | collective-permute-start | bytes 786440 | tf_op jit(solution)/shard_map/ppermute | solution.py:394
  5.5 10.1 %collective-permute-start = (bf16[128,1024]{1,0:T(8,128)(2,1)}, bf16[128,1024]{1,0:T(8,128)(2,1)S(1)}, u32[]{:S(2)}, u32[]{:S(2)}) collective-permute-start(bf16[128,1024]{1,0:T(8,128)(2,1)} %pack.2), channel_id=1, source_target_pairs={{0,0},{1,1},{2,18},{3,19},{4,36},{5,37},{6,54},{7,55},{8,64},{9,65... | collective-permute-start | bytes 786440 | tf_op jit(solution)/shard_map/ppermute | solution.py:394
  15.6 0.8 copy-start.9
  15.6 15.9 %collective-permute-start.2 = (bf16[8,128,512]{2,1,0:T(8,128)(2,1)}, bf16[8,128,512]{2,1,0:T(8,128)(2,1)}, u32[]{:S(2)}, u32[]{:S(2)}) collective-permute-start(bf16[8,128,512]{2,1,0:T(8,128)(2,1)} %get-tuple-element.17), channel_id=1, source_target_pairs={{0,1},{1,0},{2,3},{3,2},{4,5},{5,4},{6,7},{7,6},{8,9},{9,8},{10,11... | collective-permute-start | bytes 3145736 | tf_op jit(solution)/shard_map/ppermute | solution.py:401
  18.3 20.4 %collective-permute-start.4 = (bf16[256,1024]{1,0:T(8,128)(2,1)}, bf16[256,1024]{1,0:T(8,128)(2,1)S(1)}, u32[]{:S(2)}, u32[]{:S(2)}) collective-permute-start(bf16[256,1024]{1,0:T(8,128)(2,1)} %pack.3.refs_0_), channel_id=1, source_target_pairs={{0,2},{1,3},{2,4},{3,5},{4,6},{5,7},{6,0},{7,1},{8,10},{9,11},{10,... | collective-permute-start | bytes 1572872 | tf_op jit(solution)/shard_map/ppermute | solution.py:400
  23.7 16.6 %collective-permute-start.3 = (bf16[256,1024]{1,0:T(8,128)(2,1)}, bf16[256,1024]{1,0:T(8,128)(2,1)S(1)}, u32[]{:S(2)}, u32[]{:S(2)}) collective-permute-start(bf16[256,1024]{1,0:T(8,128)(2,1)} %pack.3.refs_0_), channel_id=1, source_target_pairs={{0,6},{1,7},{2,0},{3,1},{4,2},{5,3},{6,4},{7,5},{8,14},{9,15},{10,... | collective-permute-start | bytes 1572872 | tf_op jit(solution)/shard_map/ppermute | solution.py:400
  31.6 15.5 %copy-start.1 = (bf16[256,1024]{1,0:T(8,128)(2,1)S(1)}, bf16[256,1024]{1,0:T(8,128)(2,1)}, u32[]{:S(2)}) copy-start(bf16[256,1024]{1,0:T(8,128)(2,1)} %pack.3.refs_0_) | copy-start | bytes 1572868
  38.7 1.5 %copy-start.2 = (bf16[256,1024]{1,0:T(8,128)(2,1)}, bf16[256,1024]{1,0:T(8,128)(2,1)S(1)}, u32[]{:S(2)}) copy-start(bf16[256,1024]{1,0:T(8,128)(2,1)S(1)} %collective-permute-done.4.refs_4_.refs_6_) | copy-start | bytes 1572868
  40.2 0.8 copy-start.3
  41.0 21.9 %all-to-all-start = ((bf16[8,128,512]{2,1,0:T(8,128)(2,1)}), bf16[8,128,512]{2,1,0:T(8,128)(2,1)S(1)}, u32[]{:S(2)}, u32[]{:S(2)}) async-start(bf16[8,128,512]{2,1,0:T(8,128)(2,1)} %add_convert_fusion), calls=%async_computation | async-start | bytes 2097152 | tf_op jit(solution)/shard_map/all_to_all | solution.py:405
  47.1 4.7 %collective-permute-start.5 = (bf16[256,1024]{1,0:T(8,128)(2,1)S(1)}, bf16[256,1024]{1,0:T(8,128)(2,1)S(1)}, u32[]{:S(2)}, u32[]{:S(2)}) collective-permute-start(bf16[256,1024]{1,0:T(8,128)(2,1)S(1)} %copy-done.1), channel_id=1, source_target_pairs={{0,1},{1,0},{2,3},{3,2},{4,5},{5,4},{6,7},{7,6},{8,9},{9,8},{10,11... | collective-permute-start | bytes 1572872 | tf_op jit(solution)/shard_map/ppermute | solution.py:410
  47.2 5.4 %collective-permute-start.6 = (bf16[256,1024]{1,0:T(8,128)(2,1)}, bf16[256,1024]{1,0:T(8,128)(2,1)S(1)}, u32[]{:S(2)}, u32[]{:S(2)}) collective-permute-start(bf16[256,1024]{1,0:T(8,128)(2,1)} %copy-done.3), channel_id=1, source_target_pairs={{0,1},{1,0},{2,3},{3,2},{4,5},{5,4},{6,7},{7,6},{8,9},{9,8},{10,11... | collective-permute-start | bytes 1572872 | tf_op jit(solution)/shard_map/ppermute | solution.py:410
  47.7 5.7 %collective-permute-start.7 = (bf16[256,1024]{1,0:T(8,128)(2,1)}, bf16[256,1024]{1,0:T(8,128)(2,1)}, u32[]{:S(2)}, u32[]{:S(2)}) collective-permute-start(bf16[256,1024]{1,0:T(8,128)(2,1)} %copy-done.2), channel_id=1, source_target_pairs={{0,1},{1,0},{2,3},{3,2},{4,5},{5,4},{6,7},{7,6},{8,9},{9,8},{10,11... | collective-permute-start | bytes 1572872 | tf_op jit(solution)/shard_map/ppermute | solution.py:410
  48.4 31.9 %collective-permute-start.9 = (bf16[256,1024]{1,0:T(8,128)(2,1)S(1)}, bf16[256,1024]{1,0:T(8,128)(2,1)}, u32[]{:S(2)}, u32[]{:S(2)}) collective-permute-start(bf16[256,1024]{1,0:T(8,128)(2,1)S(1)} %copy-done.1), channel_id=1, source_target_pairs={{0,4},{1,5},{2,6},{3,7},{4,0},{5,1},{6,2},{7,3},{8,12},{9,13},{10,... | collective-permute-start | bytes 1572872 | tf_op jit(solution)/shard_map/ppermute | solution.py:400
  52.6 0.8 copy-start.5
  53.4 9.7 %copy-start.10 = (bf16[128,512]{1,0:T(8,128)(2,1)S(1)}, bf16[128,512]{1,0:T(8,128)(2,1)}, u32[]{:S(2)}) copy-start(bf16[128,512]{1,0:T(8,128)(2,1)} %param.15) | copy-start | bytes 393220
  63.2 45.8 %copy-start.7 = (bf16[128,512]{1,0:T(8,128)(2,1)}, bf16[128,512]{1,0:T(8,128)(2,1)S(1)}, u32[]{:S(2)}) copy-start(bf16[128,512]{1,0:T(8,128)(2,1)S(1)} %add_convert_fusion.1) | copy-start | bytes 393220
  63.2 0.7 collective-permute-start.8
  64.9 30.5 %all-to-all-start.1 = ((bf16[8,128,512]{2,1,0:T(8,128)(2,1)}), bf16[8,128,512]{2,1,0:T(8,128)(2,1)S(1)}, u32[]{:S(2)}, u32[]{:S(2)}) async-start(bf16[8,128,512]{2,1,0:T(8,128)(2,1)} %broadcast_in_dim.28), calls=%async_computation.1 | async-start | bytes 2097152 | tf_op jit(solution)/shard_map/all_to_all | solution.py:57
  80.3 2.2 %collective-permute-start.10 = (bf16[256,1024]{1,0:T(8,128)(2,1)}, bf16[256,1024]{1,0:T(8,128)(2,1)S(1)}, u32[]{:S(2)}, u32[]{:S(2)}) collective-permute-start(bf16[256,1024]{1,0:T(8,128)(2,1)} %collective-permute-done.9.refs_0_.refs_4_), channel_id=1, source_target_pairs={{0,1},{1,0},{2,3},{3,2},{4,5},{5,4},{6,7},{7,6},{8,9},{9,8},{10,11... | collective-permute-start | bytes 1572872 | tf_op jit(solution)/shard_map/ppermute | solution.py:410
  86.5 22.2 %copy-start.11 = (s32[32]{0:T(128)S(1)}, s32[32]{0:T(128)}, u32[]{:S(2)}) copy-start(s32[32]{0:T(128)} %param.14) | copy-start | bytes 388
  95.4 2.8 %copy-start = (bf16[8,128,512]{2,1,0:T(8,128)(2,1)}, bf16[8,128,512]{2,1,0:T(8,128)(2,1)S(1)}, u32[]{:S(2)}) copy-start(bf16[8,128,512]{2,1,0:T(8,128)(2,1)S(1)} %all-to-all-done.1.own) | copy-start | bytes 3145732
  95.4 2.8 %collective-permute-start.11 = (bf16[8,128,512]{2,1,0:T(8,128)(2,1)S(1)}, bf16[8,128,512]{2,1,0:T(8,128)(2,1)}, u32[]{:S(2)}, u32[]{:S(2)}) collective-permute-start(bf16[8,128,512]{2,1,0:T(8,128)(2,1)S(1)} %all-to-all-done.1.own), channel_id=1, source_target_pairs={{0,1},{1,0},{2,3},{3,2},{4,5},{5,4},{6,7},{7,6},{8,9},{9,8},{10,11... | collective-permute-start | bytes 3145736 | tf_op jit(solution)/shard_map/ppermute | solution.py:421
  103.2 20.6 %all-to-all-start.2 = ((bf16[8,128,512]{2,1,0:T(8,128)(2,1)}), bf16[8,128,512]{2,1,0:T(8,128)(2,1)S(1)}, u32[]{:S(2)}, u32[]{:S(2)}) async-start(bf16[8,128,512]{2,1,0:T(8,128)(2,1)} %join.1), calls=%async_computation.2 | async-start | bytes 2097152 | tf_op jit(solution)/shard_map/all_to_all | solution.py:423
  (3 other events, 2.3 us)

commit v6 on v5

--- a/solution.py
+++ b/solution.py
@@ -9,7 +9,7 @@
 
 STEPS = 4
 CHIPS = 8
-VMEM = 62 * 2**20
+VMEM = 61 * 2**20
 
 
 def dev(xl, z, xh, y, c):
@@ -258,20 +258,20 @@
     pairs += [
         (part.at[pl.ds(i * rows, rows)], held.at[places[b]]) for (part, i), b in zip(lies, order)
     ]
-    for p in range(0, blocks, 2):
-        pairs += [(part.at[p : p + 2], near.at[i, p : p + 2]) for i, part in enumerate((own, other))]
-    copies = fetch(pairs, sems)
+    for p in range(0, blocks, 4):
+        pairs += [(part.at[p : p + 4], near.at[i, p : p + 4]) for i, part in enumerate((own, other))]
+    copies = fetch(pairs, sems.at[pl.ds(0, len(pairs))])
     for copy in copies[: 1 + blocks]:
         copy.wait()
     sent = []
-    for p in range(0, blocks, 2):
-        copies[1 + blocks + p].wait()
-        copies[2 + blocks + p].wait()
-        joined = dot(near[0, p : p + 2].reshape(2 * rows, width), held_weight[core[0]])
-        joined += dot(near[1, p : p + 2].reshape(2 * rows, width), held_weight[1 - core[0]])
-        joined = joined.reshape(2, rows, width) + held[p : p + 2].astype(jnp.float32)
-        made[p : p + 2] = joined.astype(made.dtype)
-        sent += fetch([(made.at[p : p + 2], out.at[p : p + 2])], out_sems.at[pl.ds(p // 2, 1)])
+    for p in range(0, blocks, 4):
+        copies[1 + blocks + p // 2].wait()
+        copies[2 + blocks + p // 2].wait()
+        joined = dot(near[0, p : p + 4].reshape(4 * rows, width), held_weight[core[0]])
+        joined += dot(near[1, p : p + 4].reshape(4 * rows, width), held_weight[1 - core[0]])
+        joined = joined.reshape(4, rows, width) + held[p : p + 4].astype(jnp.float32)
+        made[p : p + 4] = joined.astype(made.dtype)
+        sent += fetch([(made.at[p : p + 4], out.at[p : p + 4])], out_sems.at[pl.ds(p // 4, 1)])
     for copy in sent:
         copy.wait()
 

time: 153 us -> 153 us (level)
  waiting for transfers between devices: 39.1 us -> 40.9 us
    all_to_all x1, waiting for transfers between devices: 4.62 us -> 6.18 us  [local(): lax.all_to_all(pair, 'tp', 0, 0, tiled=True, axis_index_groups=SAME_CORE)]
    unnamed x24 -> x22, local copies, waits for them, and re-layouts: 3.9 us -> 2.48 us
where the time goes in v6:
time: 153 us; the launch traced here: 152 us
  starting transfers between devices  45 us (29%)
  waiting for transfers between devices  40.9 us (27%)
  Pallas kernels  38.6 us (25%)
  blocking collectives  19.5 us (13%)
  local copies, waits for them, and re-layouts  3.84 us (3%)
  other arithmetic  3.59 us (2%)
    all_to_all x1, blocking collectives, spread(): lax.all_to_all(copies, axis, 0, 0, tiled=True, axis_index_groups=groups)  19.5 us
    all_to_all x1, starting transfers between devices, spread(): lax.all_to_all(copies, axis, 0, 0, tiled=True, axis_index_groups=groups)  15.3 us
    all_to_all x1, waiting for transfers between devices, local(): merged_parts = lax.all_to_all(total, 'dp', 0, 0, tiled=True)  14.9 us
    ppermute x3, starting transfers between devices, local(): both = [both] + [lax.ppermute(both, 'tp', from_y(far)) for far in (1, 2, 3)]  11.9 us
    all_to_all x1, waiting for transfers between devices, spread(): lax.all_to_all(copies, axis, 0, 0, tiled=True, axis_index_groups=groups)  9 us
    pallas_call x1, Pallas kernels, grad(): pl.pallas_call(grad_kernel, in_specs=[SCALARS] * 2 + [THERE] * (count + 3...  8.56 us
    pallas_call x1, Pallas kernels, attend(): pl.pallas_call(attend_kernel, in_specs=[SCALARS, SCALARS, HERE, THERE, TH...  8.46 us
    pallas_call x2, Pallas kernels, base(): pl.pallas_call(base_kernel, in_specs=[SCALARS] + [THERE] * (len(pieces) +...  8.22 us
  transfers between devices with their start and end apart: 15, of which 7 were waited for; matrix products, arithmetic and copies ran while one was open for 3% of the time, Pallas kernels for 15%

profile of v6, /device:TPU:0, one launch (start us, length us, event | category | flops | bytes accessed | tf_op | source)
XLA Modules:
  0.0 152.4 jit_solution(8301074058576504167)
XLA Ops:
  0.6 1.7 %pack.2 = bf16[128,1024]{1,0:T(8,128)(2,1)} custom-call(bf16[128,512]{1,0:T(8,128)(2,1)} %refs_0_.1, bf16[128,512]{1,0:T(8,128)(2,1)} %refs_1_.1), custom_call_target="tpu_custom_call" | custom-call | tf_op jit(solution)/shard_map/pack/pallas_call | solution.py:163
  2.3 3.2 %collective-permute-start.1 = (bf16[128,1024]{1,0:T(8,128)(2,1)}, bf16[128,1024]{1,0:T(8,128)(2,1)S(1)}, u32[]{:S(2)}, u32[]{:S(2)}) collective-permute-start(bf16[128,1024]{1,0:T(8,128)(2,1)} %pack.2), channel_id=1, source_target_pairs={{0,8},{1,9},{2,26},{3,27},{4,44},{5,45},{6,62},{7,63},{8,72},{9,73... | collective-permute-start | bytes 786440 | tf_op jit(solution)/shard_map/ppermute | solution.py:394
  5.5 1.6 %collective-permute-start = (bf16[128,1024]{1,0:T(8,128)(2,1)}, bf16[128,1024]{1,0:T(8,128)(2,1)S(1)}, u32[]{:S(2)}, u32[]{:S(2)}) collective-permute-start(bf16[128,1024]{1,0:T(8,128)(2,1)} %pack.2), channel_id=1, source_target_pairs={{0,0},{1,1},{2,18},{3,19},{4,36},{5,37},{6,54},{7,55},{8,64},{9,65... | collective-permute-start | bytes 786440 | tf_op jit(solution)/shard_map/ppermute | solution.py:394
  7.1 8.5 %attend.1 = (bf16[128,512]{1,0:T(8,128)(2,1)}, bf16[8,128,512]{2,1,0:T(8,128)(2,1)}) custom-call(s32[32]{0:T(128)} %lens.1, s32[1]{0:T(128)S(6)} %sub.26.half, bf16[128,512]{1,0:T(8,128)(2,1)} %queries.1, bf16[32,384,128]{2,1,0:T(8,128)(2,1)} %bitcast.11, bf16[32,384,128]{2,1,0:T(8,128)(2,1)} %bitcast.12, bf16[512,8192]{1,0:T(8,128)(2,1)} %weight.3), custom_call_target="tpu_custom_call" | custom-call | tf_op jit(solution)/shard_map/attend/pallas_call | solution.py:127
  16.4 1.8 %pack.3.refs_0_ = bf16[256,1024]{1,0:T(8,128)(2,1)} custom-call(bf16[128,1024]{1,0:T(8,128)(2,1)} %copy-done.8, bf16[128,1024]{1,0:T(8,128)(2,1)} %copy-done.7), custom_call_target="tpu_custom_call" | custom-call | tf_op jit(solution)/shard_map/pack/pallas_call | solution.py:163
  18.2 5.4 %collective-permute-start.4 = (bf16[256,1024]{1,0:T(8,128)(2,1)}, bf16[256,1024]{1,0:T(8,128)(2,1)S(1)}, u32[]{:S(2)}, u32[]{:S(2)}) collective-permute-start(bf16[256,1024]{1,0:T(8,128)(2,1)} %pack.3.refs_0_), channel_id=1, source_target_pairs={{0,2},{1,3},{2,4},{3,5},{4,6},{5,7},{6,0},{7,1},{8,10},{9,11},{10,... | collective-permute-start | bytes 1572872 | tf_op jit(solution)/shard_map/ppermute | solution.py:400
  23.7 3.0 %collective-permute-start.3 = (bf16[256,1024]{1,0:T(8,128)(2,1)}, bf16[256,1024]{1,0:T(8,128)(2,1)S(1)}, u32[]{:S(2)}, u32[]{:S(2)}) collective-permute-start(bf16[256,1024]{1,0:T(8,128)(2,1)} %pack.3.refs_0_), channel_id=1, source_target_pairs={{0,6},{1,7},{2,0},{3,1},{4,2},{5,3},{6,4},{7,5},{8,14},{9,15},{10,... | collective-permute-start | bytes 1572872 | tf_op jit(solution)/shard_map/ppermute | solution.py:400
  26.7 4.9 %project.1 = bf16[8,128,512]{2,1,0:T(8,128)(2,1)} custom-call(s32[1]{0:T(128)} %bitcast.half.core, bf16[128,512]{1,0:T(8,128)(2,1)} %get-tuple-element.15.context, bf16[512,8192]{1,0:T(8,128)(2,1)} %weight.3), custom_call_target="tpu_custom_call" | custom-call | tf_op jit(solution)/shard_map/project/pallas_call | solution.py:196
  31.6 2.6 %add_convert_fusion = bf16[8,128,512]{2,1,0:T(8,128)(2,1)} fusion(bf16[8,128,512]{2,1,0:T(8,128)(2,1)S(1)} %collective-permute-done.2, bf16[8,128,512]{2,1,0:T(8,128)(2,1)} %project.1), kind=kLoop, calls=%fused_computation.2 | loop fusion | flops 2097152 | bytes 3145728 | tf_op jit(solution)/shard_map/convert_element_type | solution.py:403
  34.2 4.5 %collective-permute-done.4.refs_4_.refs_6_ = bf16[256,1024]{1,0:T(8,128)(2,1)S(1)} collective-permute-done((bf16[256,1024]{1,0:T(8,128)(2,1)}, bf16[256,1024]{1,0:T(8,128)(2,1)S(1)}, u32[]{:S(2)}, u32[]{:S(2)}) %collective-permute-start.4) | collective-permute-done | bytes 524320 | tf_op jit(solution)/shard_map/ppermute | solution.py:400
  40.2 5.9 %all-to-all-start = ((bf16[8,128,512]{2,1,0:T(8,128)(2,1)}), bf16[8,128,512]{2,1,0:T(8,128)(2,1)S(1)}, u32[]{:S(2)}, u32[]{:S(2)}) async-start(bf16[8,128,512]{2,1,0:T(8,128)(2,1)} %add_convert_fusion), calls=%async_computation | async-start | bytes 2097152 | tf_op jit(solution)/shard_map/all_to_all | solution.py:405
  47.4 3.4 %collective-permute-start.9 = (bf16[256,1024]{1,0:T(8,128)(2,1)S(1)}, bf16[256,1024]{1,0:T(8,128)(2,1)}, u32[]{:S(2)}, u32[]{:S(2)}) collective-permute-start(bf16[256,1024]{1,0:T(8,128)(2,1)S(1)} %copy-done.1), channel_id=1, source_target_pairs={{0,4},{1,5},{2,6},{3,7},{4,0},{5,1},{6,2},{7,3},{8,12},{9,13},{10,... | collective-permute-start | bytes 1572872 | tf_op jit(solution)/shard_map/ppermute | solution.py:400
  50.9 4.9 %base.2.total = bf16[768,512]{1,0:T(8,128)(2,1)} custom-call(s32[1]{0:T(128)} %bitcast.half.core, bf16[256,1024]{1,0:T(8,128)(2,1)} %pack.3.refs_0_, bf16[256,1024]{1,0:T(8,128)(2,1)} %collective-permute-done.5.refs_1_, bf16[256,1024]{1,0:T(8,128)(2,1)} %copy-done.4, bf16[256,1024]{1,0:T(8,128)(2,1)} %collective-permute-done.6.refs_3_, ...), custom_call_target="tpu_custom_call" | custom-call | tf_op jit(solution)/shard_map/base/pallas_call | solution.py:237
  55.9 6.2 %all-to-all-done = bf16[8,128,512]{2,1,0:T(8,128)(2,1)S(1)} async-done(((bf16[8,128,512]{2,1,0:T(8,128)(2,1)}), bf16[8,128,512]{2,1,0:T(8,128)(2,1)S(1)}, u32[]{:S(2)}, u32[]{:S(2)}) %all-to-all-start) | async-done | bytes 1048608 | tf_op jit(solution)/shard_map/all_to_all | solution.py:405
  64.0 15.3 %all-to-all-start.1 = ((bf16[8,128,512]{2,1,0:T(8,128)(2,1)}), bf16[8,128,512]{2,1,0:T(8,128)(2,1)S(1)}, u32[]{:S(2)}, u32[]{:S(2)}) async-start(bf16[8,128,512]{2,1,0:T(8,128)(2,1)} %broadcast_in_dim.28), calls=%async_computation.1 | async-start | bytes 2097152 | tf_op jit(solution)/shard_map/all_to_all | solution.py:57
  79.4 2.1 %collective-permute-done.10.refs_1_.refs_5_ = bf16[256,1024]{1,0:T(8,128)(2,1)S(1)} collective-permute-done((bf16[256,1024]{1,0:T(8,128)(2,1)}, bf16[256,1024]{1,0:T(8,128)(2,1)S(1)}, u32[]{:S(2)}, u32[]{:S(2)}) %collective-permute-start.10) | collective-permute-done | bytes 524320 | tf_op jit(solution)/shard_map/ppermute | solution.py:410
  82.3 3.3 %base.3.rest = bf16[256,512]{1,0:T(8,128)(2,1)} custom-call(s32[1]{0:T(128)} %bitcast.half.core, bf16[256,1024]{1,0:T(8,128)(2,1)} %collective-permute-done.9.refs_0_.refs_4_, bf16[256,1024]{1,0:T(8,128)(2,1)} %copy-done.5, bf16[3,2,512,512]{3,2,1,0:T(8,128)(2,1)} %bitcast.7), custom_call_target="tpu_custom_call" | custom-call | tf_op jit(solution)/shard_map/base/pallas_call | solution.py:237
  85.6 9.0 %all-to-all-done.1.own = bf16[8,128,512]{2,1,0:T(8,128)(2,1)S(1)} async-done(((bf16[8,128,512]{2,1,0:T(8,128)(2,1)}), bf16[8,128,512]{2,1,0:T(8,128)(2,1)S(1)}, u32[]{:S(2)}, u32[]{:S(2)}) %all-to-all-start.1) | async-done | bytes 1048608 | tf_op jit(solution)/shard_map/all_to_all | solution.py:57
  94.6 2.7 %collective-permute-done.11.other = bf16[8,128,512]{2,1,0:T(8,128)(2,1)S(1)} collective-permute-done((bf16[8,128,512]{2,1,0:T(8,128)(2,1)S(1)}, bf16[8,128,512]{2,1,0:T(8,128)(2,1)S(1)}, u32[]{:S(2)}, u32[]{:S(2)}) %collective-permute-start.11) | collective-permute-done | bytes 1048608 | tf_op jit(solution)/shard_map/ppermute | solution.py:421
  98.3 4.9 %join.1 = bf16[8,128,512]{2,1,0:T(8,128)(2,1)} custom-call(s32[1]{0:T(128)} %bitcast.half.core, s32[8]{0:T(128)} %fusion.places, bf16[768,512]{1,0:T(8,128)(2,1)} %base.2.total, bf16[256,512]{1,0:T(8,128)(2,1)} %base.3.rest, bf16[8,128,512]{2,1,0:T(8,128)(2,1)} %copy-done, bf16[8,128,512]{2,1,0:T(8,128)(2,1)} %copy-done.2, bf16[3,2,512,512]{3,2,1,0:T(8,128)(2,1)} %bitcast.8), custom_call_target="tpu_custom_call" | custom-call | tf_op jit(solution)/shard_map/join/pallas_call | solution.py:281
  103.2 5.6 %all-to-all-start.2 = ((bf16[8,128,512]{2,1,0:T(8,128)(2,1)}), bf16[8,128,512]{2,1,0:T(8,128)(2,1)S(1)}, u32[]{:S(2)}, u32[]{:S(2)}) async-start(bf16[8,128,512]{2,1,0:T(8,128)(2,1)} %join.1), calls=%async_computation.2 | async-start | bytes 2097152 | tf_op jit(solution)/shard_map/all_to_all | solution.py:423
  109.0 14.9 %all-to-all-done.2 = bf16[8,128,512]{2,1,0:T(8,128)(2,1)S(1)} async-done(((bf16[8,128,512]{2,1,0:T(8,128)(2,1)}), bf16[8,128,512]{2,1,0:T(8,128)(2,1)S(1)}, u32[]{:S(2)}, u32[]{:S(2)}) %all-to-all-start.2) | async-done | bytes 1048608 | tf_op jit(solution)/shard_map/all_to_all | solution.py:423
  124.2 19.5 %all_to_all.20.errors = bf16[8,128,512]{2,1,0:T(8,128)(2,1)} all-to-all(bf16[8,128,512]{2,1,0:T(8,128)(2,1)S(1)} %broadcast_in_dim.31), channel_id=1, replica_groups=mesh['dp'=8,'tp'=16] {'dp'}, dimensions={0} | all-to-all | bytes 2097152 | tf_op jit(solution)/shard_map/all_to_all | solution.py:57
  143.7 8.6 %grad.1 = f32[3,1024,512]{2,1,0:T(8,128)} custom-call(s32[1]{0:T(128)} %bitcast.half.core, s32[8]{0:T(128)} %fusion.places, bf16[8,128,512]{2,1,0:T(8,128)(2,1)} %all_to_all.20.errors, bf16[256,1024]{1,0:T(8,128)(2,1)} %pack.3.refs_0_, bf16[256,1024]{1,0:T(8,128)(2,1)} %collective-permute-done.5.refs_1_, bf16[256,1024]{1,0:T(8,128)(2,1)} %copy-done.4, ...), custom_call_target="tpu_custom_call" | custom-call | tf_op jit(solution)/shard_map/grad/pallas_call | solution.py:352
  (49 shorter events, 7.9 us)
Async XLA Ops:
  2.3 13.2 %collective-permute-start.1 = (bf16[128,1024]{1,0:T(8,128)(2,1)}, bf16[128,1024]{1,0:T(8,128)(2,1)S(1)}, u32[]{:S(2)}, u32[]{:S(2)}) collective-permute-start(bf16[128,1024]{1,0:T(8,128)(2,1)} %pack.2), channel_id=1, source_target_pairs={{0,8},{1,9},{2,26},{3,27},{4,44},{5,45},{6,62},{7,63},{8,72},{9,73... | collective-permute-start | bytes 786440 | tf_op jit(solution)/shard_map/ppermute | solution.py:394
  5.5 10.1 %collective-permute-start = (bf16[128,1024]{1,0:T(8,128)(2,1)}, bf16[128,1024]{1,0:T(8,128)(2,1)S(1)}, u32[]{:S(2)}, u32[]{:S(2)}) collective-permute-start(bf16[128,1024]{1,0:T(8,128)(2,1)} %pack.2), channel_id=1, source_target_pairs={{0,0},{1,1},{2,18},{3,19},{4,36},{5,37},{6,54},{7,55},{8,64},{9,65... | collective-permute-start | bytes 786440 | tf_op jit(solution)/shard_map/ppermute | solution.py:394
  15.6 16.0 %collective-permute-start.2 = (bf16[8,128,512]{2,1,0:T(8,128)(2,1)}, bf16[8,128,512]{2,1,0:T(8,128)(2,1)S(1)}, u32[]{:S(2)}, u32[]{:S(2)}) collective-permute-start(bf16[8,128,512]{2,1,0:T(8,128)(2,1)} %get-tuple-element.17), channel_id=1, source_target_pairs={{0,1},{1,0},{2,3},{3,2},{4,5},{5,4},{6,7},{7,6},{8,9},{9,8},{10,11... | collective-permute-start | bytes 3145736 | tf_op jit(solution)/shard_map/ppermute | solution.py:401
  18.2 20.5 %collective-permute-start.4 = (bf16[256,1024]{1,0:T(8,128)(2,1)}, bf16[256,1024]{1,0:T(8,128)(2,1)S(1)}, u32[]{:S(2)}, u32[]{:S(2)}) collective-permute-start(bf16[256,1024]{1,0:T(8,128)(2,1)} %pack.3.refs_0_), channel_id=1, source_target_pairs={{0,2},{1,3},{2,4},{3,5},{4,6},{5,7},{6,0},{7,1},{8,10},{9,11},{10,... | collective-permute-start | bytes 1572872 | tf_op jit(solution)/shard_map/ppermute | solution.py:400
  23.7 16.6 %collective-permute-start.3 = (bf16[256,1024]{1,0:T(8,128)(2,1)}, bf16[256,1024]{1,0:T(8,128)(2,1)S(1)}, u32[]{:S(2)}, u32[]{:S(2)}) collective-permute-start(bf16[256,1024]{1,0:T(8,128)(2,1)} %pack.3.refs_0_), channel_id=1, source_target_pairs={{0,6},{1,7},{2,0},{3,1},{4,2},{5,3},{6,4},{7,5},{8,14},{9,15},{10,... | collective-permute-start | bytes 1572872 | tf_op jit(solution)/shard_map/ppermute | solution.py:400
  31.6 14.6 %copy-start.1 = (bf16[256,1024]{1,0:T(8,128)(2,1)S(1)}, bf16[256,1024]{1,0:T(8,128)(2,1)}, u32[]{:S(2)}) copy-start(bf16[256,1024]{1,0:T(8,128)(2,1)} %pack.3.refs_0_) | copy-start | bytes 1572868
  38.7 12.2 %copy-start.3 = (bf16[256,1024]{1,0:T(8,128)(2,1)}, bf16[256,1024]{1,0:T(8,128)(2,1)S(1)}, u32[]{:S(2)}) copy-start(bf16[256,1024]{1,0:T(8,128)(2,1)S(1)} %collective-permute-done.4.refs_4_.refs_6_) | copy-start | bytes 1572868
  40.2 10.7 %copy-start.4 = (bf16[256,1024]{1,0:T(8,128)(2,1)}, bf16[256,1024]{1,0:T(8,128)(2,1)S(1)}, u32[]{:S(2)}) copy-start(bf16[256,1024]{1,0:T(8,128)(2,1)S(1)} %collective-permute-done.3.refs_2_) | copy-start | bytes 1572868
  40.2 21.8 %all-to-all-start = ((bf16[8,128,512]{2,1,0:T(8,128)(2,1)}), bf16[8,128,512]{2,1,0:T(8,128)(2,1)S(1)}, u32[]{:S(2)}, u32[]{:S(2)}) async-start(bf16[8,128,512]{2,1,0:T(8,128)(2,1)} %add_convert_fusion), calls=%async_computation | async-start | bytes 2097152 | tf_op jit(solution)/shard_map/all_to_all | solution.py:405
  46.2 4.7 %collective-permute-start.5 = (bf16[256,1024]{1,0:T(8,128)(2,1)S(1)}, bf16[256,1024]{1,0:T(8,128)(2,1)}, u32[]{:S(2)}, u32[]{:S(2)}) collective-permute-start(bf16[256,1024]{1,0:T(8,128)(2,1)S(1)} %copy-done.1), channel_id=1, source_target_pairs={{0,1},{1,0},{2,3},{3,2},{4,5},{5,4},{6,7},{7,6},{8,9},{9,8},{10,11... | collective-permute-start | bytes 1572872 | tf_op jit(solution)/shard_map/ppermute | solution.py:410
  46.3 4.6 %collective-permute-start.6 = (bf16[256,1024]{1,0:T(8,128)(2,1)S(1)}, bf16[256,1024]{1,0:T(8,128)(2,1)}, u32[]{:S(2)}, u32[]{:S(2)}) collective-permute-start(bf16[256,1024]{1,0:T(8,128)(2,1)S(1)} %collective-permute-done.3.refs_2_), channel_id=1, source_target_pairs={{0,1},{1,0},{2,3},{3,2},{4,5},{5,4},{6,7},{7,6},{8,9},{9,8},{10,11... | collective-permute-start | bytes 1572872 | tf_op jit(solution)/shard_map/ppermute | solution.py:410
  46.8 4.1 %collective-permute-start.7 = (bf16[256,1024]{1,0:T(8,128)(2,1)S(1)}, bf16[256,1024]{1,0:T(8,128)(2,1)}, u32[]{:S(2)}, u32[]{:S(2)}) collective-permute-start(bf16[256,1024]{1,0:T(8,128)(2,1)S(1)} %collective-permute-done.4.refs_4_.refs_6_), channel_id=1, source_target_pairs={{0,1},{1,0},{2,3},{3,2},{4,5},{5,4},{6,7},{7,6},{8,9},{9,8},{10,11... | collective-permute-start | bytes 1572872 | tf_op jit(solution)/shard_map/ppermute | solution.py:410
  47.4 31.9 %collective-permute-start.9 = (bf16[256,1024]{1,0:T(8,128)(2,1)S(1)}, bf16[256,1024]{1,0:T(8,128)(2,1)}, u32[]{:S(2)}, u32[]{:S(2)}) collective-permute-start(bf16[256,1024]{1,0:T(8,128)(2,1)S(1)} %copy-done.1), channel_id=1, source_target_pairs={{0,4},{1,5},{2,6},{3,7},{4,0},{5,1},{6,2},{7,3},{8,12},{9,13},{10,... | collective-permute-start | bytes 1572872 | tf_op jit(solution)/shard_map/ppermute | solution.py:400
  50.9 11.3 %copy-start.9 = (bf16[128,512]{1,0:T(8,128)(2,1)S(1)}, bf16[128,512]{1,0:T(8,128)(2,1)}, u32[]{:S(2)}) copy-start(bf16[128,512]{1,0:T(8,128)(2,1)} %param.15) | copy-start | bytes 393220
  62.2 46.7 %copy-start.6 = (bf16[128,512]{1,0:T(8,128)(2,1)}, bf16[128,512]{1,0:T(8,128)(2,1)S(1)}, u32[]{:S(2)}) copy-start(bf16[128,512]{1,0:T(8,128)(2,1)S(1)} %add_convert_fusion.1) | copy-start | bytes 393220
  62.3 0.7 collective-permute-start.8
  64.0 30.6 %all-to-all-start.1 = ((bf16[8,128,512]{2,1,0:T(8,128)(2,1)}), bf16[8,128,512]{2,1,0:T(8,128)(2,1)S(1)}, u32[]{:S(2)}, u32[]{:S(2)}) async-start(bf16[8,128,512]{2,1,0:T(8,128)(2,1)} %broadcast_in_dim.28), calls=%async_computation.1 | async-start | bytes 2097152 | tf_op jit(solution)/shard_map/all_to_all | solution.py:57
  79.3 2.2 %collective-permute-start.10 = (bf16[256,1024]{1,0:T(8,128)(2,1)}, bf16[256,1024]{1,0:T(8,128)(2,1)S(1)}, u32[]{:S(2)}, u32[]{:S(2)}) collective-permute-start(bf16[256,1024]{1,0:T(8,128)(2,1)} %collective-permute-done.9.refs_0_.refs_4_), channel_id=1, source_target_pairs={{0,1},{1,0},{2,3},{3,2},{4,5},{5,4},{6,7},{7,6},{8,9},{9,8},{10,11... | collective-permute-start | bytes 1572872 | tf_op jit(solution)/shard_map/ppermute | solution.py:410
  81.5 0.8 copy-start.5
  85.6 23.1 %copy-start.10 = (s32[32]{0:T(128)S(1)}, s32[32]{0:T(128)}, u32[]{:S(2)}) copy-start(s32[32]{0:T(128)} %param.14) | copy-start | bytes 388
  94.6 2.7 %copy-start = (bf16[8,128,512]{2,1,0:T(8,128)(2,1)}, bf16[8,128,512]{2,1,0:T(8,128)(2,1)S(1)}, u32[]{:S(2)}) copy-start(bf16[8,128,512]{2,1,0:T(8,128)(2,1)S(1)} %all-to-all-done.1.own) | copy-start | bytes 3145732
  94.6 2.7 %collective-permute-start.11 = (bf16[8,128,512]{2,1,0:T(8,128)(2,1)S(1)}, bf16[8,128,512]{2,1,0:T(8,128)(2,1)S(1)}, u32[]{:S(2)}, u32[]{:S(2)}) collective-permute-start(bf16[8,128,512]{2,1,0:T(8,128)(2,1)S(1)} %all-to-all-done.1.own), channel_id=1, source_target_pairs={{0,1},{1,0},{2,3},{3,2},{4,5},{5,4},{6,7},{7,6},{8,9},{9,8},{10,11... | collective-permute-start | bytes 3145736 | tf_op jit(solution)/shard_map/ppermute | solution.py:421
  97.3 1.0 copy-start.2
  103.2 20.7 %all-to-all-start.2 = ((bf16[8,128,512]{2,1,0:T(8,128)(2,1)}), bf16[8,128,512]{2,1,0:T(8,128)(2,1)S(1)}, u32[]{:S(2)}, u32[]{:S(2)}) async-start(bf16[8,128,512]{2,1,0:T(8,128)(2,1)} %join.1), calls=%async_computation.2 | async-start | bytes 2097152 | tf_op jit(solution)/shard_map/all_to_all | solution.py:423
  (2 other events, 1.5 us)
